TPU v7x, 256 devices: a whole 4x4x8 slice. The times are simulated.
256 devices in a mesh: dp: 64 (over z, y, core), group: 4 (over x).
Axes of the slice: x: 4, y: 4, z: 8, core: 2. Of those that a mesh axis runs over, the one named last changes fastest.
Arguments:
- tokens: bfloat16 [262144, 512], P(('dp', 'group'))
- stamps: int32 [262144], P(('dp', 'group')), may hold values from 0 to 523776, as said below
- lengths: int32 [64, 4, 4], P('dp', 'group'), may hold values from 1 to 768, as said below
- in_weight: bfloat16 [512, 2048], P(None, ('dp', 'group')), may hold values from -0.25 to 0.25
- out_weight: bfloat16 [512, 512], P(None, 'dp'), may hold values from -0.25 to 0.25
- pos_table: float32 [12], replicated, may hold values from -1.5 to 1.5
- time_table: float32 [20], replicated, may hold values from -1.5 to 1.5
Outputs:
- updated: bfloat16 [262144, 512], P(('dp', 'group'))
Inputs may be any that keep to these rules, and one draw needn't show every extreme that they name: Each device's 4 lengths sum to 1024. The longest history of a device grows with its dp index, from about 1024 / 4 rows at index 0; every device at the last dp index holds one of 768 rows. `stamps`: within each device's 1024 rows the times never fall, the first row's time is 0 and the last row's time is 523776.
All inputs are finite; a program needn't handle non-finite values.
Results may differ from a plain program's by a relative error of at most 0.0055.
Values may be sent and summed in bfloat16 or wider, within the bound.
No kernel may reach another device: no remote copies, remote signals or barrier semaphores. Data moves between devices by JAX's collectives and lax.ppermute only.
A program may use at most 64 MiB of HBM per device.

v0:
```python
import jax
import jax.numpy as jnp
from jax import lax
from jax.sharding import PartitionSpec as P

D = 512
HEADS = 4
HEAD_DIM = 128
QBLOCK = 512
POS_BUCKETS = 12
TIME_BUCKETS = 20


def normalize(values):
    center = values - jnp.mean(values, axis=-1, keepdims=True)
    spread = jnp.mean(center * center, axis=-1, keepdims=True)
    return center * lax.rsqrt(spread + 1e-05)


def bucket_ids(gap, count):
    total = jnp.zeros(gap.shape, jnp.int32)
    for power in range(1, count):
        total = total + (gap + 1 >= 2**power).astype(jnp.int32)
    return total


def table_bias(ids, table, count):
    result = jnp.zeros(ids.shape, jnp.float32)
    for entry in range(count):
        result = result + jnp.where(ids == entry, table[entry], 0.0)
    return result


def row_layout(lengths, count):
    ends = jnp.cumsum(lengths)
    starts = ends - lengths
    row_ids = jnp.arange(count, dtype=jnp.int32)
    segment = jnp.sum((row_ids[:, None] >= ends[None, :]).astype(jnp.int32), axis=1)
    slots = jnp.arange(lengths.shape[0], dtype=jnp.int32)
    first_row = jnp.sum(jnp.where(segment[:, None] == slots[None, :], starts[None, :], 0), axis=1)
    return (segment, first_row)


def attend_block(
    value_part,
    query_part,
    key_part,
    segment,
    first_row,
    stamp_rows,
    pos_table,
    time_table,
    block_index,
):
    width = QBLOCK
    scale = HEAD_DIM ** (-0.5)
    row_start = block_index * width
    query_rows = lax.dynamic_slice_in_dim(query_part, row_start, width, 0).reshape(
        width, HEADS, HEAD_DIM
    )
    query_seg = lax.dynamic_slice_in_dim(segment, row_start, width, 0)
    query_stamp = lax.dynamic_slice_in_dim(stamp_rows, row_start, width, 0)
    query_index = row_start + jnp.arange(width, dtype=jnp.int32)
    low_tile = lax.dynamic_index_in_dim(first_row, row_start, keepdims=False) // width

    def tile_step(tile_index, totals):
        col_start = tile_index * width
        key_rows = lax.dynamic_slice_in_dim(key_part, col_start, width, 0).reshape(
            width, HEADS, HEAD_DIM
        )
        value_rows = lax.dynamic_slice_in_dim(value_part, col_start, width, 0).reshape(
            width, HEADS, HEAD_DIM
        )
        key_seg = lax.dynamic_slice_in_dim(segment, col_start, width, 0)
        key_stamp = lax.dynamic_slice_in_dim(stamp_rows, col_start, width, 0)
        key_index = col_start + jnp.arange(width, dtype=jnp.int32)
        scores = (
            jnp.einsum("qhd,khd->hqk", query_rows, key_rows, preferred_element_type=jnp.float32)
            * scale
        )
        offset = query_index[:, None] - key_index[None, :]
        elapsed = query_stamp[:, None] - key_stamp[None, :]
        bias = table_bias(bucket_ids(offset, POS_BUCKETS), pos_table, POS_BUCKETS) + table_bias(
            bucket_ids(elapsed, TIME_BUCKETS), time_table, TIME_BUCKETS
        )
        live = (query_seg[:, None] == key_seg[None, :]) & (offset >= 0)
        weights = jnp.where(live[None], jax.nn.silu(scores + bias[None]), 0.0).astype(jnp.bfloat16)
        return totals + jnp.einsum(
            "hqk,khd->qhd", weights, value_rows, preferred_element_type=jnp.float32
        )

    totals = lax.fori_loop(
        low_tile, block_index + 1, tile_step, jnp.zeros((width, HEADS, HEAD_DIM), jnp.float32)
    )
    return totals.reshape(width, HEADS * HEAD_DIM).astype(jnp.bfloat16)


def attend_many(
    value_part, query_part, key_part, buffer_lengths, stamp_rows, pos_table, time_table, block_list
):
    segment, first_row = row_layout(buffer_lengths, stamp_rows.shape[0])

    def one_block(block_index):
        return attend_block(
            value_part,
            query_part,
            key_part,
            segment,
            first_row,
            stamp_rows,
            pos_table,
            time_table,
            block_index,
        )

    return lax.map(one_block, block_list)


def shards(tokens, stamps, lengths, in_weight, out_weight, pos_table, time_table):
    count = tokens.shape[0]
    blocks_total = count // QBLOCK
    own_lengths = lengths.reshape(-1)
    normed = normalize(tokens.astype(jnp.float32)).astype(jnp.bfloat16)
    mixed = jax.nn.silu(
        jnp.dot(
            normed,
            lax.all_gather(in_weight, ("dp", "group"), axis=1, tiled=True),
            preferred_element_type=jnp.float32,
        )
    ).astype(jnp.bfloat16)
    block_list = jnp.arange(blocks_total, dtype=jnp.int32)
    attended = attend_many(
        mixed[:, D : 2 * D],
        mixed[:, 2 * D : 3 * D],
        mixed[:, 3 * D :],
        own_lengths,
        stamps,
        pos_table,
        time_table,
        block_list,
    ).reshape(count, D)
    gated = (normalize(attended.astype(jnp.float32)) * mixed[:, :D].astype(jnp.float32)).astype(
        jnp.bfloat16
    )
    projected = jnp.dot(
        gated,
        lax.all_gather(out_weight, "dp", axis=1, tiled=True),
        preferred_element_type=jnp.float32,
    )
    return (tokens.astype(jnp.float32) + projected).astype(jnp.bfloat16)


def solution(mesh):
    return jax.shard_map(
        shards,
        mesh=mesh,
        in_specs=(
            P(("dp", "group"), None),
            P(("dp", "group")),
            P("dp", "group", None),
            P(None, ("dp", "group")),
            P(None, "dp"),
            P(),
            P(),
        ),
        out_specs=P(("dp", "group"), None),
        check_vma=False,
    )
```

profile of v0, /device:TPU:1, one launch (start us, length us, event | category | flops | bytes accessed | tf_op | source)
XLA Modules:
  0.0 266.5 jit_solution(15335521536688918232)
XLA Ops:
  6.5 0.7 all-gather.2.cloned.1.call-update
  7.3 0.8 reduce-window.7
  8.1 0.1 convert_reduce_fusion.2
  8.2 0.7 bitcast_subtract_fusion.1
  8.8 0.1 select_reduce_fusion
  8.9 59.4 %all_gather.7 = bf16[512,512]{0,1:T(8,128)(2,1)} all-gather(bf16[512,8]{0,1:T(8,128)(2,1)} %param.15), channel_id=1, replica_groups=mesh['dp'=64,'group'=4] {'dp'}, dimensions={1}, use_global_device_ids=true | all-gather | bytes 532480 | tf_op jit(solution)/shard_map/all_gather | solution.py:147
  68.4 1.4 convert_reduce_fusion
  69.8 0.5 fusion.41
  70.4 49.0 %all-gather.2.cloned.1.call-done = bf16[512,2048]{0,1:T(8,128)(2,1)} async-done(((bf16[512,8]{0,1:T(8,128)(2,1)}), bf16[512,2048]{0,1:T(8,128)(2,1)}) %all-gather.2.cloned.1.call-update) | async-done | bytes 2097168 | tf_op jit(solution)/shard_map/all_gather | solution.py:127
  119.3 5.3 %multiply_convert_fusion = bf16[1024,2048]{1,0:T(8,128)(2,1)S(1)} fusion(bf16[512,2048]{0,1:T(8,128)(2,1)} %all-gather.2.cloned.1.call-done, bf16[1024,512]{1,0:T(8,128)(2,1)S(1)} %copy-done.6, f32[1024]{0:T(1024)S(1)} %add_rsqrt_fusion, f32[1024]{0:T(1024)S(1)} %broadcast_multiply_fusion.1), kind=kOutput, calls=%fused_computation.52 | convolution fusion | flops 2160066560 | bytes 7348224 | tf_op jit(solution)/shard_map/dot_general | solution.py:125
  124.7 1.4 fusion.53
  126.1 0.9 copy-done.5
  127.0 1.5 copy.22
  128.5 1.3 copy.23
  129.8 122.6 %while.33 = (s32[]{:T(128)}, bf16[2,512,512]{1,2,0:T(8,128)(2,1)}, s32[2]{0:T(128)S(1)}, s32[1024]{0:T(1024)S(1)}, bf16[1024,512]{1,0:T(8,128)(2,1)S(1)}, /*inde...) while((s32[]{:T(128)}, bf16[2,512,512]{1,2,0:T(8,128)(2,1)}, ...), condition=%wide.region_8.9_spmd, body=%wide.region_5.8_spmd.sunk | while | flops 595854336 | bytes 23631620 | solution.py:116
  130.0 0.7 dynamic_slice.60
  131.4 0.6 dynamic_slice.61
  134.6 0.1 dynamic_slice.62
  134.8 0.2 copy.32
  135.0 1.0 copy.33
  136.6 1.1 broadcast.895
  137.8 34.2 %while.34 = (s32[]{:T(128)}, f32[512,4,128]{0,2,1:T(8,128)}, s32[]{:T(128)}, bf16[1024,512]{0,1:T(8,128)(2,1)S(1)}, s32[512]{0:T(512)S(1)}, /*index=5*/s32[1024]...) while((s32[]{:T(128)}, f32[512,4,128]{0,2,1:T(8,128)}, ...), condition=%wide.region_7.7_spmd.clone, body=%wide.region_6.6_spmd.clone.sunk | while | flops 595592192 | bytes 8417887 | solution.py:92
  137.8 0.7 fusion.70
  138.5 0.1 dynamic_slice.65
  138.6 0.7 fusion.71
  139.3 0.6 slice.246
  139.9 26.2 %add_add_fusion.2 = f32[512,512]{0,1:T(8,128)S(1)} fusion(f32[]{:T(128)} %bitcast.134, f32[]{:T(128)} %bitcast.135, f32[]{:T(128)} %bitcast.136, f32[]{:T(128)} %bitcast.137, f32[]{:T(128)} %bitcast.138, f32[]{:T(128)} %bitcast.139, f32[]{:T(128)} %bitcast.140, f32[]{:T(128)} %bitcast.141, f32[]{:T(128)} %bitcast.142, f32[]{:T(128)} %bitcast.143, ...), kind=kLoop, calls=%fused_computation.19.clone.1 | loop fusion | flops 49020928 | bytes 1056896 | tf_op jit(solution)/shard_map/while/body/eval_jaxpr/while/body/add | solution.py:83
  166.1 0.1 dynamic_slice.66
  166.2 0.3 fusion.72
  166.5 1.1 constant_dynamic-slice_fusion.6
  167.7 4.3 %fusion.73 = f32[512,4,128]{0,2,1:T(8,128)} fusion(f32[512,4,128]{0,2,1:T(8,128)} %get-tuple-element.652, bf16[512,4,128]{0,2,1:T(8,128)(2,1)S(1)} %bitcast.167, bf16[512,4,128]{0,2,1:T(8,128)(2,1)S(1)} %bitcast.166, bf16[512,4,128]{2,0,1:T(8,128)(2,1)} %get-tuple-element.675, f32[512,512]{0,1:T(8,128)S(1)} %add_add_fusion.2, ...), kind=kOutput, calls=%fused_computation.18.clone.1 | convolution fusion | flops 545521664 | bytes 4980736 | tf_op jit(solution)/shard_map/while/body/eval_jaxpr/while/body/hqk,khd->qhd/dot_general | solution.py:88
  172.0 1.4 convert_element_type.455
  173.3 0.8 constant_dynamic-update-slice_fusion.2
  174.2 0.7 dynamic_slice.60
  175.5 0.6 dynamic_slice.61
  178.7 0.1 dynamic_slice.62
  178.9 0.2 copy.32
  179.1 1.0 copy.33
  180.8 1.1 broadcast.895
  181.9 68.4 %while.34 = (s32[]{:T(128)}, f32[512,4,128]{0,2,1:T(8,128)}, s32[]{:T(128)}, bf16[1024,512]{0,1:T(8,128)(2,1)S(1)}, s32[512]{0:T(512)S(1)}, /*index=5*/s32[1024]...) while((s32[]{:T(128)}, f32[512,4,128]{0,2,1:T(8,128)}, ...), condition=%wide.region_7.7_spmd.clone, body=%wide.region_6.6_spmd.clone.sunk | while | flops 595592192 | bytes 8417887 | solution.py:92
  181.9 0.7 fusion.70
  182.6 0.1 dynamic_slice.65
  182.7 0.7 fusion.71
  183.4 0.6 slice.246
  184.0 26.2 %add_add_fusion.2 = f32[512,512]{0,1:T(8,128)S(1)} fusion(f32[]{:T(128)} %bitcast.134, f32[]{:T(128)} %bitcast.135, f32[]{:T(128)} %bitcast.136, f32[]{:T(128)} %bitcast.137, f32[]{:T(128)} %bitcast.138, f32[]{:T(128)} %bitcast.139, f32[]{:T(128)} %bitcast.140, f32[]{:T(128)} %bitcast.141, f32[]{:T(128)} %bitcast.142, f32[]{:T(128)} %bitcast.143, ...), kind=kLoop, calls=%fused_computation.19.clone.1 | loop fusion | flops 49020928 | bytes 1056896 | tf_op jit(solution)/shard_map/while/body/eval_jaxpr/while/body/add | solution.py:83
  210.2 0.1 dynamic_slice.66
  210.3 0.3 fusion.72
  210.6 1.1 constant_dynamic-slice_fusion.6
  211.8 4.3 %fusion.73 = f32[512,4,128]{0,2,1:T(8,128)} fusion(f32[512,4,128]{0,2,1:T(8,128)} %get-tuple-element.652, bf16[512,4,128]{0,2,1:T(8,128)(2,1)S(1)} %bitcast.167, bf16[512,4,128]{0,2,1:T(8,128)(2,1)S(1)} %bitcast.166, bf16[512,4,128]{2,0,1:T(8,128)(2,1)} %get-tuple-element.675, f32[512,512]{0,1:T(8,128)S(1)} %add_add_fusion.2, ...), kind=kOutput, calls=%fused_computation.18.clone.1 | convolution fusion | flops 545521664 | bytes 4980736 | tf_op jit(solution)/shard_map/while/body/eval_jaxpr/while/body/hqk,khd->qhd/dot_general | solution.py:88
  216.1 0.7 fusion.70
  216.9 0.7 fusion.71
  217.6 0.6 slice.246
  218.2 26.2 %add_add_fusion.2 = f32[512,512]{0,1:T(8,128)S(1)} fusion(f32[]{:T(128)} %bitcast.134, f32[]{:T(128)} %bitcast.135, f32[]{:T(128)} %bitcast.136, f32[]{:T(128)} %bitcast.137, f32[]{:T(128)} %bitcast.138, f32[]{:T(128)} %bitcast.139, f32[]{:T(128)} %bitcast.140, f32[]{:T(128)} %bitcast.141, f32[]{:T(128)} %bitcast.142, f32[]{:T(128)} %bitcast.143, ...), kind=kLoop, calls=%fused_computation.19.clone.1 | loop fusion | flops 49020928 | bytes 1056896 | tf_op jit(solution)/shard_map/while/body/eval_jaxpr/while/body/add | solution.py:83
  244.4 0.1 dynamic_slice.66
  244.5 0.3 fusion.72
  244.8 1.1 constant_dynamic-slice_fusion.6
  245.9 4.3 %fusion.73 = f32[512,4,128]{0,2,1:T(8,128)} fusion(f32[512,4,128]{0,2,1:T(8,128)} %get-tuple-element.652, bf16[512,4,128]{0,2,1:T(8,128)(2,1)S(1)} %bitcast.167, bf16[512,4,128]{0,2,1:T(8,128)(2,1)S(1)} %bitcast.166, bf16[512,4,128]{2,0,1:T(8,128)(2,1)} %get-tuple-element.675, f32[512,512]{0,1:T(8,128)S(1)} %add_add_fusion.2, ...), kind=kOutput, calls=%fused_computation.18.clone.1 | convolution fusion | flops 545521664 | bytes 4980736 | tf_op jit(solution)/shard_map/while/body/eval_jaxpr/while/body/hqk,khd->qhd/dot_general | solution.py:88
  250.2 1.4 convert_element_type.455
  251.6 0.8 constant_dynamic-update-slice_fusion.2
  252.5 1.5 convert_reduce_fusion.1
  254.0 1.5 copy.24
  255.5 0.3 multiply_reduce_fusion
  255.8 2.0 fusion.46
  257.9 1.7 fusion.43
  (40 shorter events, 0.4 us)
Async XLA Ops:
  6.5 63.3 %copy-start.6 = (bf16[1024,512]{1,0:T(8,128)(2,1)S(1)}, bf16[1024,512]{1,0:T(8,128)(2,1)}, u32[]{:S(2)}) copy-start(bf16[1024,512]{1,0:T(8,128)(2,1)} %param.11) | copy-start | bytes 3145732
  6.5 112.8 %all-gather.2.cloned.1.call-start = ((), (), s32[]{:S(2)}) async-start(), calls=%async_computation | async-start | bytes 2105344 | tf_op jit(solution)/shard_map/all_gather | solution.py:127
  124.6 2.3 copy-start.5
  127.0 2.9 %copy-start = (f32[20]{0:T(128)S(1)}, f32[20]{0:T(128)}, u32[]{:S(2)}) copy-start(f32[20]{0:T(128)} %param.17) | copy-start | bytes 244
  127.0 2.9 %copy-start.1 = (f32[12]{0:T(128)S(1)}, f32[12]{0:T(128)}, u32[]{:S(2)}) copy-start(f32[12]{0:T(128)} %param.16) | copy-start | bytes 148
  127.0 2.9 %copy-start.8 = (s32[1024]{0:T(1024)S(1)}, s32[1024]{0:T(1024)}, u32[]{:S(2)}) copy-start(s32[1024]{0:T(1024)} %param.12) | copy-start | bytes 12292
  130.0 7.7 %copy-start.2 = (bf16[1024,512]{1,0:T(8,128)(2,1)}, bf16[1024,512]{1,0:T(8,128)(2,1)S(1)}, u32[]{:S(2)}) copy-start(bf16[1024,512]{1,0:T(8,128)(2,1)S(1)} %get-tuple-element.737) | copy-start | bytes 3145732 | tf_op jit(solution)/shard_map/while
  172.0 2.2 copy-start.3
  174.2 7.7 %copy-start.2 = (bf16[1024,512]{1,0:T(8,128)(2,1)}, bf16[1024,512]{1,0:T(8,128)(2,1)S(1)}, u32[]{:S(2)}) copy-start(bf16[1024,512]{1,0:T(8,128)(2,1)S(1)} %get-tuple-element.737) | copy-start | bytes 3145732 | tf_op jit(solution)/shard_map/while
  250.2 2.2 copy-start.3
  252.5 3.0 %copy-start.4 = (bf16[2,512,512]{1,2,0:T(8,128)(2,1)S(1)}, bf16[2,512,512]{1,2,0:T(8,128)(2,1)}, u32[]{:S(2)}) copy-start(bf16[2,512,512]{1,2,0:T(8,128)(2,1)} %get-tuple-element.815) | copy-start | bytes 3145732
  255.8 2.1 copy-start.7
  255.8 2.1 copy-start.9
Sparse Core Ops, SparseCore 0:
  11.1 108.2 all-gather.1
where the time goes:
time: 268 us; the launch traced here: 266 us
  other arithmetic  89.7 us (33%)
  blocking collectives  59.4 us (22%)
  waiting for transfers between devices  49.7 us (19%)
  local copies, waits for them, and re-layouts  26.1 us (10%)
  matrix products  19.9 us (7%)
  between operations  13.6 us (5%)
  loops' own time  8 us (3%)
    add x3, other arithmetic, tile_step(): table_bias(bucket_ids(offset, POS_BUCKETS), pos_table, POS_BUCKETS)  78.5 us
    all_gather x1, blocking collectives, shards(): lax.all_gather(out_weight, 'dp', axis=1, tiled=True)  59.4 us
    all_gather x1, waiting for transfers between devices, shards(): lax.all_gather(in_weight, ('dp', 'group'), axis=1, tiled=True)  49 us
    dot_general x3, matrix products, tile_step(): jnp.einsum('hqk,khd->qhd', weights, value_rows, preferred_element_type=jn...  12.9 us
    another operation x1, loops' own time, attend_many(): return lax.map(one_block, block_list)  7.9 us
    slice x9, local copies, waits for them, and re-layouts, table_bias(): result = result + jnp.where(ids == entry, table[entry], 0.0)  6.15 us
  transfers between devices with their start and end apart: 1, of which 1 were waited for; matrix products, arithmetic and copies ran while one was open for 1% of the time, Pallas kernels for 0%

commit v1 on v0

v1 whole, which is shorter than its diff:
```python
import functools

import jax
import jax.numpy as jnp
from jax import lax
from jax.experimental import pallas as pl
from jax.experimental.pallas import tpu as pltpu
from jax.sharding import PartitionSpec as P

D = 512
HEADS = 4
HEAD_DIM = 128
ROWS = 1024
BLOCK = 256
TILE = 128
POS_BUCKETS = 12
TIME_BUCKETS = 20
NEVER = -1e30
TRANS_B = (((1,), (1,)), ((), ()))
PAIRS = [(i, j) for i in range(ROWS // BLOCK) for j in range(i + 1)]


def normalize(values):
    center = values - jnp.mean(values, axis=-1, keepdims=True)
    spread = jnp.mean(center * center, axis=-1, keepdims=True)
    return center * lax.rsqrt(spread + 1e-05)


def prepare_kernel(lengths, pos_table, time_table, tokens, stamps, normed, bias, pos_tiles):
    for i in range(ROWS // BLOCK):
        rows = slice(i * BLOCK, (i + 1) * BLOCK)
        normed[rows, :] = normalize(tokens[rows, :].astype(jnp.float32)).astype(jnp.bfloat16)

    apart = lax.broadcasted_iota(jnp.int32, (TILE, TILE), 0) - lax.broadcasted_iota(
        jnp.int32, (TILE, TILE), 1
    )
    for d in range(ROWS // TILE):
        offset = apart + d * TILE
        tile = jnp.full((TILE, TILE), pos_table[0] * 0.5, jnp.float32)
        for power in range(1, POS_BUCKETS):
            if 2**power - 1 <= (d + 1) * TILE - 1:
                tile = jnp.where(offset + 1 >= 2**power, pos_table[power] * 0.5, tile)
        pos_tiles[d] = jnp.where(offset >= 0, tile, NEVER)

    first = lengths[0]
    second = first + lengths[1]
    third = second + lengths[2]
    row_id = (
        lax.broadcasted_iota(jnp.int32, (8, TILE), 0) * TILE
        + lax.broadcasted_iota(jnp.int32, (8, TILE), 1)
    )
    segment = (
        (row_id >= first).astype(jnp.int32)
        + (row_id >= second).astype(jnp.int32)
        + (row_id >= third).astype(jnp.int32)
    )
    times = stamps[...] + segment * (1 << 20)

    lane = lax.broadcasted_iota(jnp.int32, (TILE, TILE), 1)
    lookup = jnp.full((TILE, TILE), NEVER, jnp.float32)
    for entry in range(TIME_BUCKETS):
        lookup = jnp.where(lane == 31 - entry, time_table[entry] * 0.5, lookup)

    for i in range(ROWS // TILE):
        own = jnp.transpose(jnp.broadcast_to(times[i : i + 1, :], (TILE, TILE)))
        own = own + 1
        for j in range(ROWS // TILE):
            qi, kj = i // 2, j // 2
            if kj > qi:
                continue
            at = PAIRS.index((qi, kj))
            rows, cols = pl.ds((i % 2) * TILE, TILE), pl.ds((j % 2) * TILE, TILE)
            if j > i:
                bias[at, rows, cols] = jnp.full((TILE, TILE), NEVER, jnp.float32)
                continue
            gap = own - times[j : j + 1, :]
            time_bias = jnp.take_along_axis(lookup, lax.clz(gap), axis=1)
            bias[at, rows, cols] = time_bias + pos_tiles[i - j]


def prepare(lengths, pos_table, time_table, tokens, stamps):
    smem = pl.BlockSpec(memory_space=pltpu.SMEM)
    vmem = pl.BlockSpec(memory_space=pltpu.VMEM)
    return pl.pallas_call(
        prepare_kernel,
        out_shape=(
            jax.ShapeDtypeStruct((ROWS, D), jnp.bfloat16),
            jax.ShapeDtypeStruct((len(PAIRS), BLOCK, BLOCK), jnp.float32),
        ),
        in_specs=[smem, smem, smem, vmem, vmem],
        out_specs=(vmem, vmem),
        scratch_shapes=[pltpu.VMEM((ROWS // TILE, TILE, TILE), jnp.float32)],
        compiler_params=pltpu.CompilerParams(vmem_limit_bytes=40 * 2**20),
        cost_estimate=pl.CostEstimate(flops=2 * 10**7, bytes_accessed=5 * 10**6, transcendentals=0),
    )(lengths, pos_table, time_table, tokens, stamps)


def half_silu(z):
    return z + z * jnp.tanh(z)


def main_kernel(
    lengths, tokens_hbm, normed_hbm, bias_hbm, *refs
):
    planes_hbm, updated_hbm = refs[:8], refs[8]
    (
        tokens, normed, bias, planes, in_weight, out_weight, mixed, totals, updated, sems, out_sems,
    ) = refs[9:]
    dp, own_x = lax.axis_index("dp"), lax.axis_index("group")
    own_m, own_y, own_core = dp // 16, lax.rem(dp // 2, 4), lax.rem(dp, 2)
    def fetch(k, source, target):
        copy = pltpu.make_async_copy(source, target, sems.at[k])
        copy.start()
        return copy

    copy_normed = fetch(0, normed_hbm, normed)
    copies_in = []
    for side in range(2):
        core = own_core if side == 0 else 1 - own_core
        place = jnp.where(core == 0, own_y, own_x)
        for k in range(4):
            copies_in.append(
                fetch(
                    3 + side * 4 + k,
                    planes_hbm[side * 4 + k],
                    planes.at[core * 4 + lax.rem(place + 4 - k, 4)],
                )
            )
    copy_bias = fetch(1, bias_hbm, bias)
    copy_tokens = fetch(2, tokens_hbm, tokens)

    starts = [jnp.int32(0)]
    for k in range(3):
        starts.append(starts[-1] + lengths[k])

    copy_normed.wait()
    for copy in copies_in:
        copy.wait()

    def arrange(at, carry):
        m, y = at // 4, lax.rem(at, 4)
        m_slot = lax.rem(own_m + 4 - m, 4)
        units = []
        for core in range(2):
            for x in range(4):
                if core == 0:
                    plane, slot = y, lax.rem(own_x + 4 - x, 4)
                else:
                    plane, slot = 4 + x, lax.rem(own_y + 4 - y, 4)
                start = pl.multiple_of((slot * 4 + m_slot) * 16, 16)
                units.append(planes[plane, pl.ds(start, 16), :].astype(jnp.float32))
        for odd in range(2):
            halves = [unit[odd * 8 : odd * 8 + 8] for unit in units]
            start = pl.multiple_of(m * 512 + odd * 256 + y * 64, 64)
            in_weight[pl.ds(start, 64), :] = jnp.concatenate(
                [half[:, :D] for half in halves]
            ).astype(jnp.bfloat16)
            sides = [jnp.concatenate([h[:, D:] for h in halves[c * 4 : c * 4 + 4]], axis=1) for c in range(2)]
            start = pl.multiple_of(m * 128 + odd * 64 + y * 16, 16)
            out_weight[pl.ds(start, 16), :] = jnp.concatenate(sides).astype(jnp.bfloat16)
        return carry

    lax.fori_loop(0, 16, arrange, 0)
    sends = []
    for i in range(ROWS // BLOCK):
        rows = pl.ds(i * BLOCK, BLOCK)
        for part in range(4):
            cols = pl.ds(part * D, D)
            product = lax.dot_general(
                normed[rows, :], in_weight[cols, :], TRANS_B, preferred_element_type=jnp.float32
            )
            mixed[rows, cols] = half_silu(product * 0.5).astype(jnp.bfloat16)
        if i == 0:
            copy_bias.wait()
        low = jnp.int32(0)
        for k in range(1, 4):
            low = jnp.where(starts[k] <= i * BLOCK, starts[k], low)

        def attend(j, first, i=i, rows=rows):
            keys = pl.ds(j * BLOCK, BLOCK)
            pair_bias = bias[PAIRS.index((i, j))]
            for head in range(HEADS):
                cols = [pl.ds(part * D + head * HEAD_DIM, HEAD_DIM) for part in range(4)]
                scores = lax.dot_general(
                    mixed[rows, cols[2]], mixed[keys, cols[3]], TRANS_B,
                    preferred_element_type=jnp.float32,
                )
                weights = half_silu(scores * (0.5 * HEAD_DIM**-0.5) + pair_bias).astype(jnp.bfloat16)
                product = jnp.dot(weights, mixed[keys, cols[1]], preferred_element_type=jnp.float32)
                own = pl.ds(head * HEAD_DIM, HEAD_DIM)
                totals[:, own] = product if first else totals[:, own] + product

        attend(i, True)
        for j in range(i):
            pl.when(low < (j + 1) * BLOCK)(functools.partial(attend, j, False))
        attended = totals[...].astype(jnp.bfloat16).astype(jnp.float32)
        gate = mixed[rows, pl.ds(0, D)].astype(jnp.float32)
        gated = (normalize(attended) * gate).astype(jnp.bfloat16)
        if i == 0:
            copy_tokens.wait()
        projected = lax.dot_general(
            gated, out_weight[...], TRANS_B, preferred_element_type=jnp.float32
        )
        updated[rows, :] = (tokens[rows, :].astype(jnp.float32) + projected).astype(jnp.bfloat16)
        copy = pltpu.make_async_copy(updated.at[rows, :], updated_hbm.at[rows, :], out_sems.at[i])
        copy.start()
        sends.append(copy)
    for copy in sends:
        copy.wait()


def main(lengths, tokens, normed, bias, planes):
    anywhere = pl.BlockSpec(memory_space=pl.ANY)
    return pl.pallas_call(
        main_kernel,
        out_shape=jax.ShapeDtypeStruct((ROWS, D), jnp.bfloat16),
        in_specs=[pl.BlockSpec(memory_space=pltpu.SMEM)] + [anywhere] * 11,
        out_specs=anywhere,
        scratch_shapes=[
            pltpu.VMEM((ROWS, D), jnp.bfloat16),
            pltpu.VMEM((ROWS, D), jnp.bfloat16),
            pltpu.VMEM((len(PAIRS), BLOCK, BLOCK), jnp.float32),
            pltpu.VMEM((8, 256, 640), jnp.bfloat16),
            pltpu.VMEM((4 * D, D), jnp.bfloat16),
            pltpu.VMEM((D, D), jnp.bfloat16),
            pltpu.VMEM((ROWS, 4 * D), jnp.bfloat16),
            pltpu.VMEM((BLOCK, D), jnp.float32),
            pltpu.VMEM((ROWS, D), jnp.bfloat16),
            pltpu.SemaphoreType.DMA((11,)),
            pltpu.SemaphoreType.DMA((ROWS // BLOCK,)),
        ],
        compiler_params=pltpu.CompilerParams(vmem_limit_bytes=50 * 2**20),
        cost_estimate=pl.CostEstimate(
            flops=5 * 10**9, bytes_accessed=9 * 10**6, transcendentals=4 * 10**6
        ),
    )(lengths, tokens, normed, bias, *planes)


def device_of(x, y, z, core):
    return ((z % 8 * 4 + y % 4) * 2 + core % 2) * 4 + x % 4


def moves(step):
    return [
        (device_of(x, y, z, core), device_of(*step(x, y, z, core)))
        for z in range(8)
        for y in range(4)
        for core in range(2)
        for x in range(4)
    ]


def send(array, step):
    return lax.ppermute(array, ("dp", "group"), moves(step))


def gather(in_weight, out_weight):
    group = lax.axis_index("group")
    z = lax.axis_index("dp") // 8
    own = lax.dynamic_slice_in_dim(out_weight.T, group * HEAD_DIM, HEAD_DIM, axis=1)
    piece = jnp.concatenate([in_weight.T, own], axis=1)
    other = send(piece, lambda x, y, z, core: (x, y, z ^ 1, core))
    even = z % 2 == 0
    unit = jnp.concatenate([jnp.where(even, piece, other), jnp.where(even, other, piece)])
    units = [unit] + [
        send(unit, lambda x, y, z, core, k=k: (x, y, z + 2 * k, core)) for k in (1, 2, 3)
    ]
    line = jnp.concatenate(units)
    lines = [line] + [
        send(line, lambda x, y, z, core, k=k: (x + k * (1 - core), y + k * core, z, core))
        for k in (1, 2, 3)
    ]
    plane = jnp.concatenate(lines)
    planes = [plane] + [
        send(plane, lambda x, y, z, core, k=k: (x + k * core, y + k * (1 - core), z, core))
        for k in (1, 2, 3)
    ]
    return planes + [send(plane, lambda x, y, z, core: (x, y, z, core + 1)) for plane in planes]


def shards(tokens, stamps, lengths, in_weight, out_weight, pos_table, time_table):
    own_lengths = lengths.reshape(-1)
    normed, bias = prepare(own_lengths, pos_table, time_table, tokens, stamps.reshape(8, TILE))
    return main(own_lengths, tokens, normed, bias, gather(in_weight, out_weight))


def solution(mesh):
    return jax.shard_map(
        shards,
        mesh=mesh,
        in_specs=(
            P(("dp", "group"), None),
            P(("dp", "group")),
            P("dp", "group", None),
            P(None, ("dp", "group")),
            P(None, "dp"),
            P(),
            P(),
        ),
        out_specs=P(("dp", "group"), None),
        check_vma=False,
    )
```

time: 268 us -> 70.5 us (0.26)
  other arithmetic: 89.7 us -> 2.11 us
  blocking collectives: 59.4 us -> 0 us
  waiting for transfers between devices: 49.7 us -> 8.15 us
  starting transfers between devices: 0.01 us -> 35.5 us
  matrix products: 19.9 us -> 0 us
  local copies, waits for them, and re-layouts: 26.1 us -> 9.03 us
  Pallas kernels: 0 us -> 15 us
  between operations: 13.6 us -> 0.24 us
  loops' own time: 8 us -> 0 us
    add x6 -> x0, other arithmetic: 78.6 us -> none  [the longest x3 78.5 us: tile_step(): table_bias(bucket_ids(offset, POS_BUCKETS), pos_table, POS_BUCKETS)]
    all_gather x1 -> x0, blocking collectives: 59.4 us -> none  [shards(): lax.all_gather(out_weight, 'dp', axis=1, tiled=True)]
    all_gather x1 -> x0, waiting for transfers between devices: 49 us -> none  [shards(): lax.all_gather(in_weight, ('dp', 'group'), axis=1, tiled=True)]
    ppermute x0 -> x14, starting transfers between devices: none -> 35.5 us  [send(): return lax.ppermute(array, ('dp', 'group'), moves(step))]
    dot_general x5 -> x0, matrix products: 19.9 us -> none  [the longest x3 12.9 us: tile_step(): jnp.einsum('hqk,khd->qhd', weights, value_rows, preferred_element_type=jn...]
    pallas_call x0 -> x2, Pallas kernels: none -> 15 us  [the longest x1 12 us: main(): pl.pallas_call(main_kernel, out_shape=jax.ShapeDtypeStruct((ROWS, D), jnp...]
    ppermute x0 -> x14, waiting for transfers between devices: none -> 8.15 us  [send(): return lax.ppermute(array, ('dp', 'group'), moves(step))]
    unnamed x18 -> x26, local copies, waits for them, and re-layouts: 0.9 us -> 9.01 us
  transfers between devices with their start and end apart: 1 -> 14, of which waited for: 1 -> 6; matrix products, arithmetic and copies ran while one was open for 1% -> 0% of each run, Pallas kernels for 0% -> 4%
where the time goes in v1:
time: 70.5 us; the launch traced here: 70.1 us
  starting transfers between devices  35.5 us (50%)
  Pallas kernels  15 us (21%)
  local copies, waits for them, and re-layouts  9.03 us (13%)
  waiting for transfers between devices  8.15 us (12%)
  other arithmetic  2.11 us (3%)
    ppermute x14, starting transfers between devices, send(): return lax.ppermute(array, ('dp', 'group'), moves(step))  35.5 us
    pallas_call x1, Pallas kernels, main(): pl.pallas_call(main_kernel, out_shape=jax.ShapeDtypeStruct((ROWS, D), jnp...  12 us
    unnamed x26, local copies, waits for them, and re-layouts  9.01 us
    ppermute x14, waiting for transfers between devices, send(): return lax.ppermute(array, ('dp', 'group'), moves(step))  8.15 us
    pallas_call x1, Pallas kernels, prepare(): pl.pallas_call(prepare_kernel, out_shape=(jax.ShapeDtypeStruct((ROWS, D),...  3.01 us
    unnamed x2, other arithmetic  1.41 us
  transfers between devices with their start and end apart: 14, of which 6 were waited for; matrix products, arithmetic and copies ran while one was open for 0% of the time, Pallas kernels for 4%

profile of v1, /device:TPU:1, one launch (start us, length us, event | category | flops | bytes accessed | tf_op | source)
XLA Modules:
  0.0 70.1 jit_solution(6897869428946316337)
XLA Ops:
  0.0 0.0 copy-start
  0.0 0.7 copy-done
  0.7 0.7 pad_maximum_fusion.1
  1.4 2.5 %collective-permute-start = (bf16[8,640]{1,0:T(8,128)(2,1)S(1)}, bf16[8,640]{1,0:T(8,128)(2,1)S(1)}, u32[]{:S(2)}, u32[]{:S(2)}) collective-permute-start(bf16[8,640]{1,0:T(8,128)(2,1)S(1)} %pad_maximum_fusion.1), channel_id=1, source_target_pairs={{0,32},{1,33},{2,34},{3,35},{4,36},{5,37},{6,38},{7,39},{8,40},{9,... | collective-permute-start | bytes 30728 | tf_op jit(solution)/shard_map/ppermute | solution.py:254
  3.9 1.1 %collective-permute-done = bf16[8,640]{1,0:T(8,128)(2,1)S(1)} collective-permute-done((bf16[8,640]{1,0:T(8,128)(2,1)S(1)}, bf16[8,640]{1,0:T(8,128)(2,1)S(1)}, u32[]{:S(2)}, u32[]{:S(2)}) %collective-permute-start) | collective-permute-done | bytes 10272 | tf_op jit(solution)/shard_map/ppermute | solution.py:254
  4.9 0.7 %constant_dynamic-update-slice_fusion.4 = (bf16[64,640]{1,0:T(8,128)(2,1)S(1)}, bf16[8,640]{1,0:T(8,128)(2,1)S(1)}) fusion(bf16[8,640]{1,0:T(8,128)(2,1)S(1)} %collective-permute-done, bf16[8,128]{1,0:T(8,128)(2,1)S(1)} %dynamic-slice_bitcast_fusion, bf16[8,512]{1,0:T(8,128)(2,1)} %bitcast.9, pred[]{:T(512)S(6)} %eq.5), kind=kLoop, calls=%fused_computation.4 | loop fusion | flops 25599 | bytes 40961
  5.6 0.7 %constant_dynamic-update-slice_fusion.3 = (bf16[64,640]{1,0:T(8,128)(2,1)S(1)}, bf16[8,640]{1,0:T(8,128)(2,1)S(1)}) fusion(bf16[64,640]{1,0:T(8,128)(2,1)S(1)} %get-tuple-element.11, bf16[8,640]{1,0:T(8,128)(2,1)S(1)} %collective-permute-done, bf16[8,128]{1,0:T(8,128)(2,1)S(1)} %dynamic-slice_bitcast_fusion, bf16[8,512]{1,0:T(8,128)(2,1)} %bitcast.10, pred[]{:T(512)S(6)} %eq.5), kind=kLoop, calls=%fused_computation.3 | loop fusion | flops 25600 | bytes 40961
  6.3 5.9 %collective-permute-start.3 = (bf16[16,640]{1,0:T(8,128)(2,1)S(1)}, bf16[16,640]{1,0:T(8,128)(2,1)S(1)}, u32[]{:S(2)}, u32[]{:S(2)}) collective-permute-start(bf16[16,640]{1,0:T(8,128)(2,1)S(1)} %pad_maximum_fusion), channel_id=1, source_target_pairs={{0,192},{1,193},{2,194},{3,195},{4,196},{5,197},{6,198},{7,199},{8... | collective-permute-start | bytes 61448 | tf_op jit(solution)/shard_map/ppermute | solution.py:254
  12.3 1.0 %collective-permute-start.2 = (bf16[16,640]{1,0:T(8,128)(2,1)S(1)}, bf16[16,640]{1,0:T(8,128)(2,1)S(1)}, u32[]{:S(2)}, u32[]{:S(2)}) collective-permute-start(bf16[16,640]{1,0:T(8,128)(2,1)S(1)} %pad_maximum_fusion), channel_id=1, source_target_pairs={{0,128},{1,129},{2,130},{3,131},{4,132},{5,133},{6,134},{7,135},{8... | collective-permute-start | bytes 61448 | tf_op jit(solution)/shard_map/ppermute | solution.py:254
  13.3 2.3 %collective-permute-start.1 = (bf16[16,640]{1,0:T(8,128)(2,1)S(1)}, bf16[16,640]{1,0:T(8,128)(2,1)S(1)}, u32[]{:S(2)}, u32[]{:S(2)}) collective-permute-start(bf16[16,640]{1,0:T(8,128)(2,1)S(1)} %pad_maximum_fusion), channel_id=1, source_target_pairs={{0,64},{1,65},{2,66},{3,67},{4,68},{5,69},{6,70},{7,71},{8,72},{9,... | collective-permute-start | bytes 61448 | tf_op jit(solution)/shard_map/ppermute | solution.py:254
  15.5 2.5 %collective-permute-done.1 = bf16[16,640]{1,0:T(8,128)(2,1)S(1)} collective-permute-done((bf16[16,640]{1,0:T(8,128)(2,1)S(1)}, bf16[16,640]{1,0:T(8,128)(2,1)S(1)}, u32[]{:S(2)}, u32[]{:S(2)}) %collective-permute-start.1) | collective-permute-done | bytes 20512 | tf_op jit(solution)/shard_map/ppermute | solution.py:254
  18.0 0.8 %collective-permute-done.2 = bf16[16,640]{1,0:T(8,128)(2,1)S(1)} collective-permute-done((bf16[16,640]{1,0:T(8,128)(2,1)S(1)}, bf16[16,640]{1,0:T(8,128)(2,1)S(1)}, u32[]{:S(2)}, u32[]{:S(2)}) %collective-permute-start.2) | collective-permute-done | bytes 20512 | tf_op jit(solution)/shard_map/ppermute | solution.py:254
  18.8 0.0 collective-permute-done.3
  18.8 1.4 %collective-permute-start.4 = (bf16[64,640]{1,0:T(8,128)(2,1)S(1)}, bf16[64,640]{1,0:T(8,128)(2,1)S(1)}, u32[]{:S(2)}, u32[]{:S(2)}) collective-permute-start(bf16[64,640]{1,0:T(8,128)(2,1)S(1)} %get-tuple-element.13), channel_id=1, source_target_pairs={{0,1},{1,2},{2,3},{3,0},{4,12},{5,13},{6,14},{7,15},{8,9},{9,10},{... | collective-permute-start | bytes 245768 | tf_op jit(solution)/shard_map/ppermute | solution.py:254
  20.2 1.5 %collective-permute-start.6 = (bf16[64,640]{1,0:T(8,128)(2,1)S(1)}, bf16[64,640]{1,0:T(8,128)(2,1)S(1)}, u32[]{:S(2)}, u32[]{:S(2)}) collective-permute-start(bf16[64,640]{1,0:T(8,128)(2,1)S(1)} %get-tuple-element.13), channel_id=1, source_target_pairs={{0,3},{1,0},{2,1},{3,2},{4,28},{5,29},{6,30},{7,31},{8,11},{9,8},{... | collective-permute-start | bytes 245768 | tf_op jit(solution)/shard_map/ppermute | solution.py:254
  21.7 1.6 %collective-permute-start.5 = (bf16[64,640]{1,0:T(8,128)(2,1)S(1)}, bf16[64,640]{1,0:T(8,128)(2,1)S(1)}, u32[]{:S(2)}, u32[]{:S(2)}) collective-permute-start(bf16[64,640]{1,0:T(8,128)(2,1)S(1)} %get-tuple-element.13), channel_id=1, source_target_pairs={{0,2},{1,3},{2,0},{3,1},{4,20},{5,21},{6,22},{7,23},{8,10},{9,11},... | collective-permute-start | bytes 245768 | tf_op jit(solution)/shard_map/ppermute | solution.py:254
  23.3 0.2 collective-permute-done.4
  23.5 3.0 %collective-permute-done.5 = bf16[64,640]{1,0:T(8,128)(2,1)S(1)} collective-permute-done((bf16[64,640]{1,0:T(8,128)(2,1)S(1)}, bf16[64,640]{1,0:T(8,128)(2,1)S(1)}, u32[]{:S(2)}, u32[]{:S(2)}) %collective-permute-start.5) | collective-permute-done | bytes 81952 | tf_op jit(solution)/shard_map/ppermute | solution.py:254
  26.5 0.0 collective-permute-done.6
  26.6 2.6 %collective-permute-start.9 = (bf16[256,640]{1,0:T(8,128)(2,1)S(1)}, bf16[256,640]{1,0:T(8,128)(2,1)S(1)}, u32[]{:S(2)}, u32[]{:S(2)}) collective-permute-start(bf16[256,640]{1,0:T(8,128)(2,1)S(1)} %constant_dynamic-update-slice_fusion.5.refs_0_), channel_id=1, source_target_pairs={{0,24},{1,25},{2,26},{3,27},{4,7},{5,4},{6,5},{7,6},{8,0},{9,1},{1... | collective-permute-start | bytes 983048 | tf_op jit(solution)/shard_map/ppermute | solution.py:254
  29.1 0.5 collective-permute-start.8
  29.7 0.6 collective-permute-start.7
  30.3 5.8 %collective-permute-start.10 = (bf16[256,640]{1,0:T(8,128)(2,1)S(1)}, bf16[256,640]{1,0:T(8,128)(2,1)S(1)}, u32[]{:S(2)}, u32[]{:S(2)}) collective-permute-start(bf16[256,640]{1,0:T(8,128)(2,1)S(1)} %constant_dynamic-update-slice_fusion.5.refs_0_), channel_id=1, source_target_pairs={{0,4},{1,5},{2,6},{3,7},{4,0},{5,1},{6,2},{7,3},{8,12},{9,13},{10,... | collective-permute-start | bytes 983048 | tf_op jit(solution)/shard_map/ppermute | solution.py:254
  36.1 0.6 collective-permute-done.9.refs_3_
  36.7 5.9 %collective-permute-start.13 = (bf16[256,640]{1,0:T(8,128)(2,1)S(1)}, bf16[256,640]{1,0:T(8,128)(2,1)S(1)}, u32[]{:S(2)}, u32[]{:S(2)}) collective-permute-start(bf16[256,640]{1,0:T(8,128)(2,1)S(1)} %collective-permute-done.9.refs_3_), channel_id=1, source_target_pairs={{0,4},{1,5},{2,6},{3,7},{4,0},{5,1},{6,2},{7,3},{8,12},{9,13},{10,... | collective-permute-start | bytes 983048 | tf_op jit(solution)/shard_map/ppermute | solution.py:254
  42.6 0.0 collective-permute-done.8.refs_2_
  42.6 0.6 collective-permute-start.12
  43.2 0.0 collective-permute-done.7.refs_1_
  43.2 3.4 %collective-permute-start.11 = (bf16[256,640]{1,0:T(8,128)(2,1)S(1)}, bf16[256,640]{1,0:T(8,128)(2,1)S(1)}, u32[]{:S(2)}, u32[]{:S(2)}) collective-permute-start(bf16[256,640]{1,0:T(8,128)(2,1)S(1)} %collective-permute-done.7.refs_1_), channel_id=1, source_target_pairs={{0,4},{1,5},{2,6},{3,7},{4,0},{5,1},{6,2},{7,3},{8,12},{9,13},{10,... | collective-permute-start | bytes 983048 | tf_op jit(solution)/shard_map/ppermute | solution.py:254
  46.6 0.0 copy-start.1
  46.6 1.2 %copy-done.1 = bf16[1024,512]{1,0:T(8,128)(2,1)S(1)} copy-done((bf16[1024,512]{1,0:T(8,128)(2,1)S(1)}, bf16[1024,512]{1,0:T(8,128)(2,1)}, u32[]{:S(2)}) %copy-start.1) | copy-done | bytes 1048600
  47.8 0.0 copy-start.3
  47.8 0.7 copy-done.3
  48.5 0.0 copy-start.4
  48.5 0.7 copy-done.4
  49.1 0.0 copy-start.5
  49.1 0.7 copy-done.5
  49.8 0.0 copy-start.6
  49.8 0.7 copy-done.6
  50.5 3.0 %shard_map.73 = (bf16[1024,512]{1,0:T(8,128)(2,1)S(1)}, f32[10,256,256]{2,1,0:T(8,128)S(1)}) custom-call(s32[4]{0:T(128)S(1)} %bitcast.6, f32[12]{0:T(128)S(1)} %copy-done.4, f32[20]{0:T(128)S(1)} %copy-done.5, bf16[1024,512]{1,0:T(8,128)(2,1)S(1)} %copy-done.1, s32[8,128]{1,0:T(8,128)S(1)} %bitcast.5), custom_call_target="tpu_custom_call" | custom-call | flops 20000000 | bytes 5000000 | tf_op jit(solution)/shard_map/pallas_call | solution.py:84
  53.5 0.0 copy-start.8
  53.5 1.5 %copy-done.8 = f32[10,256,256]{2,1,0:T(8,128)} copy-done((f32[10,256,256]{2,1,0:T(8,128)}, f32[10,256,256]{2,1,0:T(8,128)S(1)}, u32[]{:S(2)}) %copy-start.8) | copy-done | bytes 2621464
  55.0 0.0 copy-start.9
  55.0 1.0 %copy-done.9 = bf16[1024,512]{1,0:T(8,128)(2,1)} copy-done((bf16[1024,512]{1,0:T(8,128)(2,1)}, bf16[1024,512]{1,0:T(8,128)(2,1)S(1)}, u32[]{:S(2)}) %copy-start.9) | copy-done | bytes 1048600
  56.0 0.0 collective-permute-done.10.refs_4_
  56.0 0.0 collective-permute-done.13.refs_7_
  56.0 0.0 collective-permute-done.12.refs_6_
  56.0 0.0 collective-permute-done.11.refs_5_
  56.0 0.0 copy-start.2
  56.0 1.2 %copy-done.2 = bf16[1024,512]{1,0:T(8,128)(2,1)S(1)} copy-done((bf16[1024,512]{1,0:T(8,128)(2,1)S(1)}, bf16[1024,512]{1,0:T(8,128)(2,1)}, u32[]{:S(2)}) %copy-start.2) | copy-done | bytes 1048600
  57.2 0.0 copy-start.7
  57.2 0.7 copy-done.7
  57.9 12.0 %shard_map.74 = bf16[1024,512]{1,0:T(8,128)(2,1)} custom-call(s32[4]{0:T(128)S(1)} %bitcast.7, bf16[1024,512]{1,0:T(8,128)(2,1)S(1)} %copy-done.2, bf16[1024,512]{1,0:T(8,128)(2,1)} %copy-done.9, f32[10,256,256]{2,1,0:T(8,128)} %copy-done.8, bf16[256,640]{1,0:T(8,128)(2,1)S(1)} %constant_dynamic-update-slice_fusion.5.refs_0_, ...), custom_call_target="tpu_custom_call" | custom-call | flops 5000000000 | bytes 9000000 | tf_op jit(solution)/shard_map/pallas_call | solution.py:214
  (10 shorter events, 0.1 us)
Async XLA Ops:
  0.0 0.7 copy-start
  1.4 3.5 %collective-permute-start = (bf16[8,640]{1,0:T(8,128)(2,1)S(1)}, bf16[8,640]{1,0:T(8,128)(2,1)S(1)}, u32[]{:S(2)}, u32[]{:S(2)}) collective-permute-start(bf16[8,640]{1,0:T(8,128)(2,1)S(1)} %pad_maximum_fusion.1), channel_id=1, source_target_pairs={{0,32},{1,33},{2,34},{3,35},{4,36},{5,37},{6,38},{7,39},{8,40},{9,... | collective-permute-start | bytes 30728 | tf_op jit(solution)/shard_map/ppermute | solution.py:254
  6.3 12.5 %collective-permute-start.3 = (bf16[16,640]{1,0:T(8,128)(2,1)S(1)}, bf16[16,640]{1,0:T(8,128)(2,1)S(1)}, u32[]{:S(2)}, u32[]{:S(2)}) collective-permute-start(bf16[16,640]{1,0:T(8,128)(2,1)S(1)} %pad_maximum_fusion), channel_id=1, source_target_pairs={{0,192},{1,193},{2,194},{3,195},{4,196},{5,197},{6,198},{7,199},{8... | collective-permute-start | bytes 61448 | tf_op jit(solution)/shard_map/ppermute | solution.py:254
  12.3 6.5 %collective-permute-start.2 = (bf16[16,640]{1,0:T(8,128)(2,1)S(1)}, bf16[16,640]{1,0:T(8,128)(2,1)S(1)}, u32[]{:S(2)}, u32[]{:S(2)}) collective-permute-start(bf16[16,640]{1,0:T(8,128)(2,1)S(1)} %pad_maximum_fusion), channel_id=1, source_target_pairs={{0,128},{1,129},{2,130},{3,131},{4,132},{5,133},{6,134},{7,135},{8... | collective-permute-start | bytes 61448 | tf_op jit(solution)/shard_map/ppermute | solution.py:254
  13.3 4.7 %collective-permute-start.1 = (bf16[16,640]{1,0:T(8,128)(2,1)S(1)}, bf16[16,640]{1,0:T(8,128)(2,1)S(1)}, u32[]{:S(2)}, u32[]{:S(2)}) collective-permute-start(bf16[16,640]{1,0:T(8,128)(2,1)S(1)} %pad_maximum_fusion), channel_id=1, source_target_pairs={{0,64},{1,65},{2,66},{3,67},{4,68},{5,69},{6,70},{7,71},{8,72},{9,... | collective-permute-start | bytes 61448 | tf_op jit(solution)/shard_map/ppermute | solution.py:254
  18.8 4.6 %collective-permute-start.4 = (bf16[64,640]{1,0:T(8,128)(2,1)S(1)}, bf16[64,640]{1,0:T(8,128)(2,1)S(1)}, u32[]{:S(2)}, u32[]{:S(2)}) collective-permute-start(bf16[64,640]{1,0:T(8,128)(2,1)S(1)} %get-tuple-element.13), channel_id=1, source_target_pairs={{0,1},{1,2},{2,3},{3,0},{4,12},{5,13},{6,14},{7,15},{8,9},{9,10},{... | collective-permute-start | bytes 245768 | tf_op jit(solution)/shard_map/ppermute | solution.py:254
  20.2 6.3 %collective-permute-start.6 = (bf16[64,640]{1,0:T(8,128)(2,1)S(1)}, bf16[64,640]{1,0:T(8,128)(2,1)S(1)}, u32[]{:S(2)}, u32[]{:S(2)}) collective-permute-start(bf16[64,640]{1,0:T(8,128)(2,1)S(1)} %get-tuple-element.13), channel_id=1, source_target_pairs={{0,3},{1,0},{2,1},{3,2},{4,28},{5,29},{6,30},{7,31},{8,11},{9,8},{... | collective-permute-start | bytes 245768 | tf_op jit(solution)/shard_map/ppermute | solution.py:254
  21.7 4.8 %collective-permute-start.5 = (bf16[64,640]{1,0:T(8,128)(2,1)S(1)}, bf16[64,640]{1,0:T(8,128)(2,1)S(1)}, u32[]{:S(2)}, u32[]{:S(2)}) collective-permute-start(bf16[64,640]{1,0:T(8,128)(2,1)S(1)} %get-tuple-element.13), channel_id=1, source_target_pairs={{0,2},{1,3},{2,0},{3,1},{4,20},{5,21},{6,22},{7,23},{8,10},{9,11},... | collective-permute-start | bytes 245768 | tf_op jit(solution)/shard_map/ppermute | solution.py:254
  26.6 10.1 %collective-permute-start.9 = (bf16[256,640]{1,0:T(8,128)(2,1)S(1)}, bf16[256,640]{1,0:T(8,128)(2,1)S(1)}, u32[]{:S(2)}, u32[]{:S(2)}) collective-permute-start(bf16[256,640]{1,0:T(8,128)(2,1)S(1)} %constant_dynamic-update-slice_fusion.5.refs_0_), channel_id=1, source_target_pairs={{0,24},{1,25},{2,26},{3,27},{4,7},{5,4},{6,5},{7,6},{8,0},{9,1},{1... | collective-permute-start | bytes 983048 | tf_op jit(solution)/shard_map/ppermute | solution.py:254
  29.1 13.5 %collective-permute-start.8 = (bf16[256,640]{1,0:T(8,128)(2,1)S(1)}, bf16[256,640]{1,0:T(8,128)(2,1)S(1)}, u32[]{:S(2)}, u32[]{:S(2)}) collective-permute-start(bf16[256,640]{1,0:T(8,128)(2,1)S(1)} %constant_dynamic-update-slice_fusion.5.refs_0_), channel_id=1, source_target_pairs={{0,16},{1,17},{2,18},{3,19},{4,6},{5,7},{6,4},{7,5},{8,24},{9,25},... | collective-permute-start | bytes 983048 | tf_op jit(solution)/shard_map/ppermute | solution.py:254
  29.7 13.5 %collective-permute-start.7 = (bf16[256,640]{1,0:T(8,128)(2,1)S(1)}, bf16[256,640]{1,0:T(8,128)(2,1)S(1)}, u32[]{:S(2)}, u32[]{:S(2)}) collective-permute-start(bf16[256,640]{1,0:T(8,128)(2,1)S(1)} %constant_dynamic-update-slice_fusion.5.refs_0_), channel_id=1, source_target_pairs={{0,8},{1,9},{2,10},{3,11},{4,5},{5,6},{6,7},{7,4},{8,16},{9,17},{1... | collective-permute-start | bytes 983048 | tf_op jit(solution)/shard_map/ppermute | solution.py:254
  30.3 25.7 %collective-permute-start.10 = (bf16[256,640]{1,0:T(8,128)(2,1)S(1)}, bf16[256,640]{1,0:T(8,128)(2,1)S(1)}, u32[]{:S(2)}, u32[]{:S(2)}) collective-permute-start(bf16[256,640]{1,0:T(8,128)(2,1)S(1)} %constant_dynamic-update-slice_fusion.5.refs_0_), channel_id=1, source_target_pairs={{0,4},{1,5},{2,6},{3,7},{4,0},{5,1},{6,2},{7,3},{8,12},{9,13},{10,... | collective-permute-start | bytes 983048 | tf_op jit(solution)/shard_map/ppermute | solution.py:254
  36.7 19.3 %collective-permute-start.13 = (bf16[256,640]{1,0:T(8,128)(2,1)S(1)}, bf16[256,640]{1,0:T(8,128)(2,1)S(1)}, u32[]{:S(2)}, u32[]{:S(2)}) collective-permute-start(bf16[256,640]{1,0:T(8,128)(2,1)S(1)} %collective-permute-done.9.refs_3_), channel_id=1, source_target_pairs={{0,4},{1,5},{2,6},{3,7},{4,0},{5,1},{6,2},{7,3},{8,12},{9,13},{10,... | collective-permute-start | bytes 983048 | tf_op jit(solution)/shard_map/ppermute | solution.py:254
  42.6 13.4 %collective-permute-start.12 = (bf16[256,640]{1,0:T(8,128)(2,1)S(1)}, bf16[256,640]{1,0:T(8,128)(2,1)S(1)}, u32[]{:S(2)}, u32[]{:S(2)}) collective-permute-start(bf16[256,640]{1,0:T(8,128)(2,1)S(1)} %collective-permute-done.8.refs_2_), channel_id=1, source_target_pairs={{0,4},{1,5},{2,6},{3,7},{4,0},{5,1},{6,2},{7,3},{8,12},{9,13},{10,... | collective-permute-start | bytes 983048 | tf_op jit(solution)/shard_map/ppermute | solution.py:254
  43.2 12.8 %collective-permute-start.11 = (bf16[256,640]{1,0:T(8,128)(2,1)S(1)}, bf16[256,640]{1,0:T(8,128)(2,1)S(1)}, u32[]{:S(2)}, u32[]{:S(2)}) collective-permute-start(bf16[256,640]{1,0:T(8,128)(2,1)S(1)} %collective-permute-done.7.refs_1_), channel_id=1, source_target_pairs={{0,4},{1,5},{2,6},{3,7},{4,0},{5,1},{6,2},{7,3},{8,12},{9,13},{10,... | collective-permute-start | bytes 983048 | tf_op jit(solution)/shard_map/ppermute | solution.py:254
  46.6 1.2 %copy-start.1 = (bf16[1024,512]{1,0:T(8,128)(2,1)S(1)}, bf16[1024,512]{1,0:T(8,128)(2,1)}, u32[]{:S(2)}) copy-start(bf16[1024,512]{1,0:T(8,128)(2,1)} %tokens_hbm.1) | copy-start | bytes 3145732
  47.8 0.7 copy-start.3
  48.5 0.7 copy-start.4
  49.1 0.7 copy-start.5
  49.8 0.7 copy-start.6
  53.5 1.5 %copy-start.8 = (f32[10,256,256]{2,1,0:T(8,128)}, f32[10,256,256]{2,1,0:T(8,128)S(1)}, u32[]{:S(2)}) copy-start(f32[10,256,256]{2,1,0:T(8,128)S(1)} %get-tuple-element.8.bias_hbm) | copy-start | bytes 7864324
  55.0 1.0 %copy-start.9 = (bf16[1024,512]{1,0:T(8,128)(2,1)}, bf16[1024,512]{1,0:T(8,128)(2,1)S(1)}, u32[]{:S(2)}) copy-start(bf16[1024,512]{1,0:T(8,128)(2,1)S(1)} %get-tuple-element.7.normed_hbm) | copy-start | bytes 3145732
  56.0 1.2 %copy-start.2 = (bf16[1024,512]{1,0:T(8,128)(2,1)S(1)}, bf16[1024,512]{1,0:T(8,128)(2,1)}, u32[]{:S(2)}) copy-start(bf16[1024,512]{1,0:T(8,128)(2,1)} %tokens_hbm.1) | copy-start | bytes 3145732
  57.2 0.7 copy-start.7

commit v2 on v1

--- a/solution.py
+++ b/solution.py
@@ -1,5 +1,3 @@
-import functools
-
 import jax
 import jax.numpy as jnp
 from jax import lax
@@ -16,6 +14,8 @@
 POS_BUCKETS = 12
 TIME_BUCKETS = 20
 NEVER = -1e30
+VMEM_PREPARE = 16
+VMEM_MAIN = 32
 TRANS_B = (((1,), (1,)), ((), ()))
 PAIRS = [(i, j) for i in range(ROWS // BLOCK) for j in range(i + 1)]
 
@@ -26,7 +26,26 @@
     return center * lax.rsqrt(spread + 1e-05)
 
 
-def prepare_kernel(lengths, pos_table, time_table, tokens, stamps, normed, bias, pos_tiles):
+def prepare_kernel(
+    lengths_hbm, pos_hbm, time_hbm, tokens_hbm, stamps_hbm, tokens, normed, bias,
+    lengths, pos_table, time_table, stamps, pos_tiles, sems,
+):
+    copies = [
+        pltpu.make_async_copy(source, target, sems.at[k])
+        for k, (source, target) in enumerate(
+            [
+                (lengths_hbm, lengths),
+                (pos_hbm, pos_table),
+                (time_hbm, time_table),
+                (stamps_hbm, stamps),
+                (tokens_hbm, tokens),
+            ]
+        )
+    ]
+    for copy in copies:
+        copy.start()
+    for copy in copies:
+        copy.wait()
     for i in range(ROWS // BLOCK):
         rows = slice(i * BLOCK, (i + 1) * BLOCK)
         normed[rows, :] = normalize(tokens[rows, :].astype(jnp.float32)).astype(jnp.bfloat16)
@@ -79,18 +98,26 @@
 
 
 def prepare(lengths, pos_table, time_table, tokens, stamps):
-    smem = pl.BlockSpec(memory_space=pltpu.SMEM)
+    anywhere = pl.BlockSpec(memory_space=pl.ANY)
     vmem = pl.BlockSpec(memory_space=pltpu.VMEM)
     return pl.pallas_call(
         prepare_kernel,
         out_shape=(
             jax.ShapeDtypeStruct((ROWS, D), jnp.bfloat16),
+            jax.ShapeDtypeStruct((ROWS, D), jnp.bfloat16),
             jax.ShapeDtypeStruct((len(PAIRS), BLOCK, BLOCK), jnp.float32),
         ),
-        in_specs=[smem, smem, smem, vmem, vmem],
-        out_specs=(vmem, vmem),
-        scratch_shapes=[pltpu.VMEM((ROWS // TILE, TILE, TILE), jnp.float32)],
-        compiler_params=pltpu.CompilerParams(vmem_limit_bytes=40 * 2**20),
+        in_specs=[anywhere] * 5,
+        out_specs=(vmem,) * 3,
+        scratch_shapes=[
+            pltpu.SMEM((4,), jnp.int32),
+            pltpu.SMEM((POS_BUCKETS,), jnp.float32),
+            pltpu.SMEM((TIME_BUCKETS,), jnp.float32),
+            pltpu.VMEM((ROWS // TILE, TILE), jnp.int32),
+            pltpu.VMEM((ROWS // TILE, TILE, TILE), jnp.float32),
+            pltpu.SemaphoreType.DMA((5,)),
+        ],
+        compiler_params=pltpu.CompilerParams(vmem_limit_bytes=VMEM_PREPARE * 2**20),
         cost_estimate=pl.CostEstimate(flops=2 * 10**7, bytes_accessed=5 * 10**6, transcendentals=0),
     )(lengths, pos_table, time_table, tokens, stamps)
 
@@ -100,20 +127,18 @@
 
 
 def main_kernel(
-    lengths, tokens_hbm, normed_hbm, bias_hbm, *refs
+    tokens, normed, bias, *refs
 ):
     planes_hbm, updated_hbm = refs[:8], refs[8]
-    (
-        tokens, normed, bias, planes, in_weight, out_weight, mixed, totals, updated, sems, out_sems,
-    ) = refs[9:]
+    planes, in_weight, out_weight, mixed, totals, updated, sems, out_sems = refs[9:]
     dp, own_x = lax.axis_index("dp"), lax.axis_index("group")
-    own_m, own_y, own_core = dp // 16, lax.rem(dp // 2, 4), lax.rem(dp, 2)
+    own_m, own_odd = dp // 16, lax.rem(dp // 8, 2)
+    own_y, own_core = lax.rem(dp // 2, 4), lax.rem(dp, 2)
     def fetch(k, source, target):
         copy = pltpu.make_async_copy(source, target, sems.at[k])
         copy.start()
         return copy
 
-    copy_normed = fetch(0, normed_hbm, normed)
     copies_in = []
     for side in range(2):
         core = own_core if side == 0 else 1 - own_core
@@ -121,19 +146,12 @@
         for k in range(4):
             copies_in.append(
                 fetch(
-                    3 + side * 4 + k,
+                    side * 4 + k,
                     planes_hbm[side * 4 + k],
                     planes.at[core * 4 + lax.rem(place + 4 - k, 4)],
                 )
             )
-    copy_bias = fetch(1, bias_hbm, bias)
-    copy_tokens = fetch(2, tokens_hbm, tokens)
-
-    starts = [jnp.int32(0)]
-    for k in range(3):
-        starts.append(starts[-1] + lengths[k])
-
-    copy_normed.wait()
+
     for copy in copies_in:
         copy.wait()
 
@@ -149,13 +167,17 @@
                     plane, slot = 4 + x, lax.rem(own_y + 4 - y, 4)
                 start = pl.multiple_of((slot * 4 + m_slot) * 16, 16)
                 units.append(planes[plane, pl.ds(start, 16), :].astype(jnp.float32))
-        for odd in range(2):
-            halves = [unit[odd * 8 : odd * 8 + 8] for unit in units]
+        for half in range(2):
+            odd = own_odd if half == 0 else 1 - own_odd
+            halves = [unit[half * 8 : half * 8 + 8] for unit in units]
             start = pl.multiple_of(m * 512 + odd * 256 + y * 64, 64)
             in_weight[pl.ds(start, 64), :] = jnp.concatenate(
-                [half[:, :D] for half in halves]
+                [piece[:, :D] for piece in halves]
             ).astype(jnp.bfloat16)
-            sides = [jnp.concatenate([h[:, D:] for h in halves[c * 4 : c * 4 + 4]], axis=1) for c in range(2)]
+            sides = [
+                jnp.concatenate([piece[:, D:] for piece in halves[c * 4 : c * 4 + 4]], axis=1)
+                for c in range(2)
+            ]
             start = pl.multiple_of(m * 128 + odd * 64 + y * 16, 16)
             out_weight[pl.ds(start, 16), :] = jnp.concatenate(sides).astype(jnp.bfloat16)
         return carry
@@ -170,11 +192,6 @@
                 normed[rows, :], in_weight[cols, :], TRANS_B, preferred_element_type=jnp.float32
             )
             mixed[rows, cols] = half_silu(product * 0.5).astype(jnp.bfloat16)
-        if i == 0:
-            copy_bias.wait()
-        low = jnp.int32(0)
-        for k in range(1, 4):
-            low = jnp.where(starts[k] <= i * BLOCK, starts[k], low)
 
         def attend(j, first, i=i, rows=rows):
             keys = pl.ds(j * BLOCK, BLOCK)
@@ -192,12 +209,10 @@
 
         attend(i, True)
         for j in range(i):
-            pl.when(low < (j + 1) * BLOCK)(functools.partial(attend, j, False))
+            attend(j, False)
         attended = totals[...].astype(jnp.bfloat16).astype(jnp.float32)
         gate = mixed[rows, pl.ds(0, D)].astype(jnp.float32)
         gated = (normalize(attended) * gate).astype(jnp.bfloat16)
-        if i == 0:
-            copy_tokens.wait()
         projected = lax.dot_general(
             gated, out_weight[...], TRANS_B, preferred_element_type=jnp.float32
         )
@@ -209,31 +224,29 @@
         copy.wait()
 
 
-def main(lengths, tokens, normed, bias, planes):
+def main(tokens, normed, bias, planes):
     anywhere = pl.BlockSpec(memory_space=pl.ANY)
+    vmem = pl.BlockSpec(memory_space=pltpu.VMEM)
     return pl.pallas_call(
         main_kernel,
         out_shape=jax.ShapeDtypeStruct((ROWS, D), jnp.bfloat16),
-        in_specs=[pl.BlockSpec(memory_space=pltpu.SMEM)] + [anywhere] * 11,
+        in_specs=[vmem] * 3 + [anywhere] * 8,
         out_specs=anywhere,
         scratch_shapes=[
-            pltpu.VMEM((ROWS, D), jnp.bfloat16),
-            pltpu.VMEM((ROWS, D), jnp.bfloat16),
-            pltpu.VMEM((len(PAIRS), BLOCK, BLOCK), jnp.float32),
             pltpu.VMEM((8, 256, 640), jnp.bfloat16),
             pltpu.VMEM((4 * D, D), jnp.bfloat16),
             pltpu.VMEM((D, D), jnp.bfloat16),
             pltpu.VMEM((ROWS, 4 * D), jnp.bfloat16),
             pltpu.VMEM((BLOCK, D), jnp.float32),
             pltpu.VMEM((ROWS, D), jnp.bfloat16),
-            pltpu.SemaphoreType.DMA((11,)),
+            pltpu.SemaphoreType.DMA((8,)),
             pltpu.SemaphoreType.DMA((ROWS // BLOCK,)),
         ],
-        compiler_params=pltpu.CompilerParams(vmem_limit_bytes=50 * 2**20),
+        compiler_params=pltpu.CompilerParams(vmem_limit_bytes=VMEM_MAIN * 2**20),
         cost_estimate=pl.CostEstimate(
             flops=5 * 10**9, bytes_accessed=9 * 10**6, transcendentals=4 * 10**6
         ),
-    )(lengths, tokens, normed, bias, *planes)
+    )(tokens, normed, bias, *planes)
 
 
 def device_of(x, y, z, core):
@@ -256,12 +269,10 @@
 
 def gather(in_weight, out_weight):
     group = lax.axis_index("group")
-    z = lax.axis_index("dp") // 8
     own = lax.dynamic_slice_in_dim(out_weight.T, group * HEAD_DIM, HEAD_DIM, axis=1)
     piece = jnp.concatenate([in_weight.T, own], axis=1)
     other = send(piece, lambda x, y, z, core: (x, y, z ^ 1, core))
-    even = z % 2 == 0
-    unit = jnp.concatenate([jnp.where(even, piece, other), jnp.where(even, other, piece)])
+    unit = jnp.concatenate([piece, other])
     units = [unit] + [
         send(unit, lambda x, y, z, core, k=k: (x, y, z + 2 * k, core)) for k in (1, 2, 3)
     ]
@@ -271,17 +282,23 @@
         for k in (1, 2, 3)
     ]
     plane = jnp.concatenate(lines)
-    planes = [plane] + [
+    return [plane] + [
         send(plane, lambda x, y, z, core, k=k: (x + k * core, y + k * (1 - core), z, core))
         for k in (1, 2, 3)
     ]
-    return planes + [send(plane, lambda x, y, z, core: (x, y, z, core + 1)) for plane in planes]
+
+
+def swap(planes):
+    return [send(plane, lambda x, y, z, core: (x, y, z, core + 1)) for plane in planes]
 
 
 def shards(tokens, stamps, lengths, in_weight, out_weight, pos_table, time_table):
     own_lengths = lengths.reshape(-1)
-    normed, bias = prepare(own_lengths, pos_table, time_table, tokens, stamps.reshape(8, TILE))
-    return main(own_lengths, tokens, normed, bias, gather(in_weight, out_weight))
+    prepared = prepare(own_lengths, pos_table, time_table, tokens, stamps.reshape(8, TILE))
+    own, *others = gather(in_weight, out_weight)
+    others, prepared = lax.optimization_barrier((others, prepared))
+    planes = [own, *others]
+    return main(*prepared, planes + swap(planes))
 
 
 def solution(mesh):

time: 70.5 us -> 58.8 us (0.83)
  starting transfers between devices: 35.5 us -> 29.6 us
  local copies, waits for them, and re-layouts: 9.03 us -> 4.66 us
  Pallas kernels: 15 us -> 13.4 us
  waiting for transfers between devices: 8.15 us -> 9.24 us
  other arithmetic: 2.11 us -> 1.4 us
    ppermute x14, starting transfers between devices: 35.5 us -> 29.6 us  [send(): return lax.ppermute(array, ('dp', 'group'), moves(step))]
    unnamed x26 -> x17, local copies, waits for them, and re-layouts: 9.01 us -> 4.63 us
    pallas_call x1, Pallas kernels: 12 us -> 10.4 us  [main(): pl.pallas_call(main_kernel, out_shape=jax.ShapeDtypeStruct((ROWS, D), jnp...]
    ppermute x14, waiting for transfers between devices: 8.15 us -> 9.24 us  [send(): return lax.ppermute(array, ('dp', 'group'), moves(step))]
    unnamed x2 -> x1, other arithmetic: 1.41 us -> 0.7 us
  transfers between devices with their start and end apart: 14 -> 14, of which waited for: 6 -> 8; matrix products, arithmetic and copies ran while one was open for 0% -> 0% of each run, Pallas kernels for 4% -> 5%
where the time goes in v2:
time: 58.8 us; the launch traced here: 58.5 us
  starting transfers between devices  29.6 us (50%)
  Pallas kernels  13.4 us (23%)
  waiting for transfers between devices  9.24 us (16%)
  local copies, waits for them, and re-layouts  4.66 us (8%)
  other arithmetic  1.4 us (2%)
    ppermute x14, starting transfers between devices, send(): return lax.ppermute(array, ('dp', 'group'), moves(step))  29.6 us
    pallas_call x1, Pallas kernels, main(): pl.pallas_call(main_kernel, out_shape=jax.ShapeDtypeStruct((ROWS, D), jnp...  10.4 us
    ppermute x14, waiting for transfers between devices, send(): return lax.ppermute(array, ('dp', 'group'), moves(step))  9.24 us
    unnamed x17, local copies, waits for them, and re-layouts  4.63 us
    pallas_call x1, Pallas kernels, prepare(): pl.pallas_call(prepare_kernel, out_shape=(jax.ShapeDtypeStruct((ROWS, D),...  3.06 us
  transfers between devices with their start and end apart: 14, of which 8 were waited for; matrix products, arithmetic and copies ran while one was open for 0% of the time, Pallas kernels for 5%

profile of v2, /device:TPU:1, one launch (start us, length us, event | category | flops | bytes accessed | tf_op | source)
XLA Modules:
  0.0 58.5 jit_solution(12144812358003236998)
XLA Ops:
  0.0 0.0 copy-start
  0.0 0.7 %copy-done = bf16[512,8]{0,1:T(8,128)(2,1)S(1)} copy-done((bf16[512,8]{0,1:T(8,128)(2,1)S(1)}, bf16[512,8]{0,1:T(8,128)(2,1)}, u32[]{:S(2)}) %copy-start) | copy-done | bytes 8216
  0.7 0.7 %constant_dynamic-update-slice_fusion.4 = (bf16[64,640]{1,0:T(8,128)(2,1)S(1)}, bf16[256,640]{1,0:T(8,128)(2,1)S(1)}, bf16[8,640]{1,0:T(8,128)(2,1)S(1)}) fusion(bf16[8,128]{1,0:T(8,128)(2,1)S(1)} %dynamic-slice_bitcast_fusion, bf16[8,512]{1,0:T(8,128)(2,1)} %bitcast.7), kind=kLoop, calls=%fused_computation.4 | loop fusion | flops 20478 | bytes 40960
  1.4 2.5 %collective-permute-start = (bf16[8,640]{1,0:T(8,128)(2,1)S(1)}, bf16[8,640]{1,0:T(8,128)(2,1)S(1)}, u32[]{:S(2)}, u32[]{:S(2)}) collective-permute-start(bf16[8,640]{1,0:T(8,128)(2,1)S(1)} %get-tuple-element.33), channel_id=1, source_target_pairs={{0,32},{1,33},{2,34},{3,35},{4,36},{5,37},{6,38},{7,39},{8,40},{9,... | collective-permute-start | bytes 30728 | tf_op jit(solution)/shard_map/ppermute | solution.py:267
  3.9 1.1 %collective-permute-done = bf16[8,640]{1,0:T(8,128)(2,1)S(1)} collective-permute-done((bf16[8,640]{1,0:T(8,128)(2,1)S(1)}, bf16[8,640]{1,0:T(8,128)(2,1)S(1)}, u32[]{:S(2)}, u32[]{:S(2)}) %collective-permute-start) | collective-permute-done | bytes 10272 | tf_op jit(solution)/shard_map/ppermute | solution.py:267
  4.9 0.7 %pad_maximum_fusion = bf16[16,640]{1,0:T(8,128)(2,1)S(1)} fusion(bf16[8,640]{1,0:T(8,128)(2,1)S(1)} %collective-permute-done, bf16[8,128]{1,0:T(8,128)(2,1)S(1)} %dynamic-slice_bitcast_fusion, bf16[8,512]{1,0:T(8,128)(2,1)} %bitcast.8), kind=kLoop, calls=%fused_computation.13 | loop fusion | flops 61440 | bytes 40960 | tf_op jit(solution)/shard_map/concatenate | solution.py:275
  5.6 5.8 %collective-permute-start.3 = (bf16[16,640]{1,0:T(8,128)(2,1)S(1)}, bf16[16,640]{1,0:T(8,128)(2,1)S(1)}, u32[]{:S(2)}, u32[]{:S(2)}) collective-permute-start(bf16[16,640]{1,0:T(8,128)(2,1)S(1)} %pad_maximum_fusion), channel_id=1, source_target_pairs={{0,192},{1,193},{2,194},{3,195},{4,196},{5,197},{6,198},{7,199},{8... | collective-permute-start | bytes 61448 | tf_op jit(solution)/shard_map/ppermute | solution.py:267
  11.5 0.9 %collective-permute-start.2 = (bf16[16,640]{1,0:T(8,128)(2,1)S(1)}, bf16[16,640]{1,0:T(8,128)(2,1)S(1)}, u32[]{:S(2)}, u32[]{:S(2)}) collective-permute-start(bf16[16,640]{1,0:T(8,128)(2,1)S(1)} %pad_maximum_fusion), channel_id=1, source_target_pairs={{0,128},{1,129},{2,130},{3,131},{4,132},{5,133},{6,134},{7,135},{8... | collective-permute-start | bytes 61448 | tf_op jit(solution)/shard_map/ppermute | solution.py:267
  12.4 2.4 %collective-permute-start.1 = (bf16[16,640]{1,0:T(8,128)(2,1)S(1)}, bf16[16,640]{1,0:T(8,128)(2,1)S(1)}, u32[]{:S(2)}, u32[]{:S(2)}) collective-permute-start(bf16[16,640]{1,0:T(8,128)(2,1)S(1)} %pad_maximum_fusion), channel_id=1, source_target_pairs={{0,64},{1,65},{2,66},{3,67},{4,68},{5,69},{6,70},{7,71},{8,72},{9,... | collective-permute-start | bytes 61448 | tf_op jit(solution)/shard_map/ppermute | solution.py:267
  14.7 2.4 %collective-permute-done.1 = bf16[16,640]{1,0:T(8,128)(2,1)S(1)} collective-permute-done((bf16[16,640]{1,0:T(8,128)(2,1)S(1)}, bf16[16,640]{1,0:T(8,128)(2,1)S(1)}, u32[]{:S(2)}, u32[]{:S(2)}) %collective-permute-start.1) | collective-permute-done | bytes 20512 | tf_op jit(solution)/shard_map/ppermute | solution.py:267
  17.2 0.8 %collective-permute-done.2 = bf16[16,640]{1,0:T(8,128)(2,1)S(1)} collective-permute-done((bf16[16,640]{1,0:T(8,128)(2,1)S(1)}, bf16[16,640]{1,0:T(8,128)(2,1)S(1)}, u32[]{:S(2)}, u32[]{:S(2)}) %collective-permute-start.2) | collective-permute-done | bytes 20512 | tf_op jit(solution)/shard_map/ppermute | solution.py:267
  18.0 0.0 collective-permute-done.3
  18.0 1.4 %collective-permute-start.4 = (bf16[64,640]{1,0:T(8,128)(2,1)S(1)}, bf16[64,640]{1,0:T(8,128)(2,1)S(1)}, u32[]{:S(2)}, u32[]{:S(2)}) collective-permute-start(bf16[64,640]{1,0:T(8,128)(2,1)S(1)} %get-tuple-element.23), channel_id=1, source_target_pairs={{0,1},{1,2},{2,3},{3,0},{4,12},{5,13},{6,14},{7,15},{8,9},{9,10},{... | collective-permute-start | bytes 245768 | tf_op jit(solution)/shard_map/ppermute | solution.py:267
  19.4 1.5 %collective-permute-start.6 = (bf16[64,640]{1,0:T(8,128)(2,1)S(1)}, bf16[64,640]{1,0:T(8,128)(2,1)S(1)}, u32[]{:S(2)}, u32[]{:S(2)}) collective-permute-start(bf16[64,640]{1,0:T(8,128)(2,1)S(1)} %get-tuple-element.23), channel_id=1, source_target_pairs={{0,3},{1,0},{2,1},{3,2},{4,28},{5,29},{6,30},{7,31},{8,11},{9,8},{... | collective-permute-start | bytes 245768 | tf_op jit(solution)/shard_map/ppermute | solution.py:267
  20.9 1.6 %collective-permute-start.5 = (bf16[64,640]{1,0:T(8,128)(2,1)S(1)}, bf16[64,640]{1,0:T(8,128)(2,1)S(1)}, u32[]{:S(2)}, u32[]{:S(2)}) collective-permute-start(bf16[64,640]{1,0:T(8,128)(2,1)S(1)} %get-tuple-element.23), channel_id=1, source_target_pairs={{0,2},{1,3},{2,0},{3,1},{4,20},{5,21},{6,22},{7,23},{8,10},{9,11},... | collective-permute-start | bytes 245768 | tf_op jit(solution)/shard_map/ppermute | solution.py:267
  22.5 0.2 collective-permute-done.4
  22.7 3.0 %collective-permute-done.5 = bf16[64,640]{1,0:T(8,128)(2,1)S(1)} collective-permute-done((bf16[64,640]{1,0:T(8,128)(2,1)S(1)}, bf16[64,640]{1,0:T(8,128)(2,1)S(1)}, u32[]{:S(2)}, u32[]{:S(2)}) %collective-permute-start.5) | collective-permute-done | bytes 81952 | tf_op jit(solution)/shard_map/ppermute | solution.py:267
  25.8 0.0 collective-permute-done.6
  25.8 2.6 %collective-permute-start.9 = (bf16[256,640]{1,0:T(8,128)(2,1)S(1)}, bf16[256,640]{1,0:T(8,128)(2,1)S(1)}, u32[]{:S(2)}, u32[]{:S(2)}) collective-permute-start(bf16[256,640]{1,0:T(8,128)(2,1)S(1)} %constant_dynamic-update-slice_fusion.5.refs_0_), channel_id=1, source_target_pairs={{0,24},{1,25},{2,26},{3,27},{4,7},{5,4},{6,5},{7,6},{8,0},{9,1},{1... | collective-permute-start | bytes 983048 | tf_op jit(solution)/shard_map/ppermute | solution.py:267
  28.3 0.5 collective-permute-start.8
  28.9 0.6 %collective-permute-start.7 = (bf16[256,640]{1,0:T(8,128)(2,1)S(1)}, bf16[256,640]{1,0:T(8,128)(2,1)S(1)}, u32[]{:S(2)}, u32[]{:S(2)}) collective-permute-start(bf16[256,640]{1,0:T(8,128)(2,1)S(1)} %constant_dynamic-update-slice_fusion.5.refs_0_), channel_id=1, source_target_pairs={{0,8},{1,9},{2,10},{3,11},{4,5},{5,6},{6,7},{7,4},{8,16},{9,17},{1... | collective-permute-start | bytes 983048 | tf_op jit(solution)/shard_map/ppermute | solution.py:267
  29.5 0.0 copy-start.1
  29.5 1.2 %copy-done.1 = bf16[1024,512]{1,0:T(8,128)(2,1)S(1)} copy-done((bf16[1024,512]{1,0:T(8,128)(2,1)S(1)}, bf16[1024,512]{1,0:T(8,128)(2,1)}, u32[]{:S(2)}) %copy-start.1) | copy-done | bytes 1048600
  30.7 0.0 copy-start.2
  30.7 0.7 %copy-done.2 = s32[1024]{0:T(1024)S(1)} copy-done((s32[1024]{0:T(1024)S(1)}, s32[1024]{0:T(1024)}, u32[]{:S(2)}) %copy-start.2) | copy-done | bytes 4120
  31.4 0.0 copy-start.3
  31.4 0.7 %copy-done.3 = s32[1,1,4]{2,1,0:T(1,128)S(1)} copy-done((s32[1,1,4]{2,1,0:T(1,128)S(1)}, s32[1,1,4]{2,1,0:T(1,128)}, u32[]{:S(2)}) %copy-start.3) | copy-done | bytes 40
  32.0 0.0 copy-start.4
  32.0 0.7 %copy-done.4 = f32[12]{0:T(128)S(1)} copy-done((f32[12]{0:T(128)S(1)}, f32[12]{0:T(128)}, u32[]{:S(2)}) %copy-start.4) | copy-done | bytes 72
  32.7 0.0 copy-start.5
  32.7 0.7 %copy-done.5 = f32[20]{0:T(128)S(1)} copy-done((f32[20]{0:T(128)S(1)}, f32[20]{0:T(128)}, u32[]{:S(2)}) %copy-start.5) | copy-done | bytes 104
  33.4 3.1 %shard_map.73 = (bf16[1024,512]{1,0:T(8,128)(2,1)S(1)}, bf16[1024,512]{1,0:T(8,128)(2,1)S(1)}, f32[10,256,256]{2,1,0:T(8,128)S(1)}) custom-call(s32[4]{0:T(128)S(1)} %bitcast.6, f32[12]{0:T(128)S(1)} %copy-done.4, f32[20]{0:T(128)S(1)} %copy-done.5, bf16[1024,512]{1,0:T(8,128)(2,1)S(1)} %copy-done.1, s32[8,128]{1,0:T(8,128)S(1)} %bitcast.5), custom_call_target="tpu_custom_call" | custom-call | flops 20000000 | bytes 5000000 | tf_op jit(solution)/shard_map/pallas_call | solution.py:103
  36.4 5.9 %collective-permute-start.10 = (bf16[256,640]{1,0:T(8,128)(2,1)S(1)}, bf16[256,640]{1,0:T(8,128)(2,1)S(1)}, u32[]{:S(2)}, u32[]{:S(2)}) collective-permute-start(bf16[256,640]{1,0:T(8,128)(2,1)S(1)} %constant_dynamic-update-slice_fusion.5.refs_0_), channel_id=1, source_target_pairs={{0,4},{1,5},{2,6},{3,7},{4,0},{5,1},{6,2},{7,3},{8,12},{9,13},{10,... | collective-permute-start | bytes 983048 | tf_op jit(solution)/shard_map/ppermute | solution.py:267
  42.3 0.0 collective-permute-done.9.refs_3_
  42.3 0.0 collective-permute-done.8.refs_2_
  42.3 0.0 collective-permute-done.7.refs_1_
  42.3 3.4 %collective-permute-start.11 = (bf16[256,640]{1,0:T(8,128)(2,1)S(1)}, bf16[256,640]{1,0:T(8,128)(2,1)S(1)}, u32[]{:S(2)}, u32[]{:S(2)}) collective-permute-start(bf16[256,640]{1,0:T(8,128)(2,1)S(1)} %collective-permute-done.7.refs_1_), channel_id=1, source_target_pairs={{0,4},{1,5},{2,6},{3,7},{4,0},{5,1},{6,2},{7,3},{8,12},{9,13},{10,... | collective-permute-start | bytes 983048 | tf_op jit(solution)/shard_map/ppermute | solution.py:267
  45.8 0.0 collective-permute-start.12
  45.8 0.5 collective-permute-start.13
  46.3 0.0 collective-permute-done.10.refs_4_
  46.3 0.7 %collective-permute-done.11.refs_5_ = bf16[256,640]{1,0:T(8,128)(2,1)S(1)} collective-permute-done((bf16[256,640]{1,0:T(8,128)(2,1)S(1)}, bf16[256,640]{1,0:T(8,128)(2,1)S(1)}, u32[]{:S(2)}, u32[]{:S(2)}) %collective-permute-start.11) | collective-permute-done | bytes 327712 | tf_op jit(solution)/shard_map/ppermute | solution.py:267
  47.0 0.5 collective-permute-done.12.refs_6_
  47.5 0.5 collective-permute-done.13.refs_7_
  48.0 10.4 %shard_map.74 = bf16[1024,512]{1,0:T(8,128)(2,1)} custom-call(bf16[1024,512]{1,0:T(8,128)(2,1)S(1)} %get-tuple-element.17.tokens, bf16[1024,512]{1,0:T(8,128)(2,1)S(1)} %get-tuple-element.18.normed, f32[10,256,256]{2,1,0:T(8,128)S(1)} %get-tuple-element.19.bias, bf16[256,640]{1,0:T(8,128)(2,1)S(1)} %constant_dynamic-update-slice_fusion.5.refs_0_, ...), custom_call_target="tpu_custom_call" | custom-call | flops 5000000000 | bytes 9000000 | tf_op jit(solution)/shard_map/pallas_call | solution.py:230
  (8 shorter events, 0.1 us)
Async XLA Ops:
  0.0 0.7 %copy-start = (bf16[512,8]{0,1:T(8,128)(2,1)S(1)}, bf16[512,8]{0,1:T(8,128)(2,1)}, u32[]{:S(2)}) copy-start(bf16[512,8]{0,1:T(8,128)(2,1)} %param.11) | copy-start | bytes 24580
  1.4 3.5 %collective-permute-start = (bf16[8,640]{1,0:T(8,128)(2,1)S(1)}, bf16[8,640]{1,0:T(8,128)(2,1)S(1)}, u32[]{:S(2)}, u32[]{:S(2)}) collective-permute-start(bf16[8,640]{1,0:T(8,128)(2,1)S(1)} %get-tuple-element.33), channel_id=1, source_target_pairs={{0,32},{1,33},{2,34},{3,35},{4,36},{5,37},{6,38},{7,39},{8,40},{9,... | collective-permute-start | bytes 30728 | tf_op jit(solution)/shard_map/ppermute | solution.py:267
  5.6 12.4 %collective-permute-start.3 = (bf16[16,640]{1,0:T(8,128)(2,1)S(1)}, bf16[16,640]{1,0:T(8,128)(2,1)S(1)}, u32[]{:S(2)}, u32[]{:S(2)}) collective-permute-start(bf16[16,640]{1,0:T(8,128)(2,1)S(1)} %pad_maximum_fusion), channel_id=1, source_target_pairs={{0,192},{1,193},{2,194},{3,195},{4,196},{5,197},{6,198},{7,199},{8... | collective-permute-start | bytes 61448 | tf_op jit(solution)/shard_map/ppermute | solution.py:267
  11.5 6.5 %collective-permute-start.2 = (bf16[16,640]{1,0:T(8,128)(2,1)S(1)}, bf16[16,640]{1,0:T(8,128)(2,1)S(1)}, u32[]{:S(2)}, u32[]{:S(2)}) collective-permute-start(bf16[16,640]{1,0:T(8,128)(2,1)S(1)} %pad_maximum_fusion), channel_id=1, source_target_pairs={{0,128},{1,129},{2,130},{3,131},{4,132},{5,133},{6,134},{7,135},{8... | collective-permute-start | bytes 61448 | tf_op jit(solution)/shard_map/ppermute | solution.py:267
  12.4 4.8 %collective-permute-start.1 = (bf16[16,640]{1,0:T(8,128)(2,1)S(1)}, bf16[16,640]{1,0:T(8,128)(2,1)S(1)}, u32[]{:S(2)}, u32[]{:S(2)}) collective-permute-start(bf16[16,640]{1,0:T(8,128)(2,1)S(1)} %pad_maximum_fusion), channel_id=1, source_target_pairs={{0,64},{1,65},{2,66},{3,67},{4,68},{5,69},{6,70},{7,71},{8,72},{9,... | collective-permute-start | bytes 61448 | tf_op jit(solution)/shard_map/ppermute | solution.py:267
  18.0 4.6 %collective-permute-start.4 = (bf16[64,640]{1,0:T(8,128)(2,1)S(1)}, bf16[64,640]{1,0:T(8,128)(2,1)S(1)}, u32[]{:S(2)}, u32[]{:S(2)}) collective-permute-start(bf16[64,640]{1,0:T(8,128)(2,1)S(1)} %get-tuple-element.23), channel_id=1, source_target_pairs={{0,1},{1,2},{2,3},{3,0},{4,12},{5,13},{6,14},{7,15},{8,9},{9,10},{... | collective-permute-start | bytes 245768 | tf_op jit(solution)/shard_map/ppermute | solution.py:267
  19.4 6.3 %collective-permute-start.6 = (bf16[64,640]{1,0:T(8,128)(2,1)S(1)}, bf16[64,640]{1,0:T(8,128)(2,1)S(1)}, u32[]{:S(2)}, u32[]{:S(2)}) collective-permute-start(bf16[64,640]{1,0:T(8,128)(2,1)S(1)} %get-tuple-element.23), channel_id=1, source_target_pairs={{0,3},{1,0},{2,1},{3,2},{4,28},{5,29},{6,30},{7,31},{8,11},{9,8},{... | collective-permute-start | bytes 245768 | tf_op jit(solution)/shard_map/ppermute | solution.py:267
  20.9 4.8 %collective-permute-start.5 = (bf16[64,640]{1,0:T(8,128)(2,1)S(1)}, bf16[64,640]{1,0:T(8,128)(2,1)S(1)}, u32[]{:S(2)}, u32[]{:S(2)}) collective-permute-start(bf16[64,640]{1,0:T(8,128)(2,1)S(1)} %get-tuple-element.23), channel_id=1, source_target_pairs={{0,2},{1,3},{2,0},{3,1},{4,20},{5,21},{6,22},{7,23},{8,10},{9,11},... | collective-permute-start | bytes 245768 | tf_op jit(solution)/shard_map/ppermute | solution.py:267
  25.8 16.5 %collective-permute-start.9 = (bf16[256,640]{1,0:T(8,128)(2,1)S(1)}, bf16[256,640]{1,0:T(8,128)(2,1)S(1)}, u32[]{:S(2)}, u32[]{:S(2)}) collective-permute-start(bf16[256,640]{1,0:T(8,128)(2,1)S(1)} %constant_dynamic-update-slice_fusion.5.refs_0_), channel_id=1, source_target_pairs={{0,24},{1,25},{2,26},{3,27},{4,7},{5,4},{6,5},{7,6},{8,0},{9,1},{1... | collective-permute-start | bytes 983048 | tf_op jit(solution)/shard_map/ppermute | solution.py:267
  28.3 14.0 %collective-permute-start.8 = (bf16[256,640]{1,0:T(8,128)(2,1)S(1)}, bf16[256,640]{1,0:T(8,128)(2,1)S(1)}, u32[]{:S(2)}, u32[]{:S(2)}) collective-permute-start(bf16[256,640]{1,0:T(8,128)(2,1)S(1)} %constant_dynamic-update-slice_fusion.5.refs_0_), channel_id=1, source_target_pairs={{0,16},{1,17},{2,18},{3,19},{4,6},{5,7},{6,4},{7,5},{8,24},{9,25},... | collective-permute-start | bytes 983048 | tf_op jit(solution)/shard_map/ppermute | solution.py:267
  28.9 13.5 %collective-permute-start.7 = (bf16[256,640]{1,0:T(8,128)(2,1)S(1)}, bf16[256,640]{1,0:T(8,128)(2,1)S(1)}, u32[]{:S(2)}, u32[]{:S(2)}) collective-permute-start(bf16[256,640]{1,0:T(8,128)(2,1)S(1)} %constant_dynamic-update-slice_fusion.5.refs_0_), channel_id=1, source_target_pairs={{0,8},{1,9},{2,10},{3,11},{4,5},{5,6},{6,7},{7,4},{8,16},{9,17},{1... | collective-permute-start | bytes 983048 | tf_op jit(solution)/shard_map/ppermute | solution.py:267
  29.5 1.2 %copy-start.1 = (bf16[1024,512]{1,0:T(8,128)(2,1)S(1)}, bf16[1024,512]{1,0:T(8,128)(2,1)}, u32[]{:S(2)}) copy-start(bf16[1024,512]{1,0:T(8,128)(2,1)} %tokens_hbm.1) | copy-start | bytes 3145732
  30.7 0.7 %copy-start.2 = (s32[1024]{0:T(1024)S(1)}, s32[1024]{0:T(1024)}, u32[]{:S(2)}) copy-start(s32[1024]{0:T(1024)} %param.8) | copy-start | bytes 12292
  31.4 0.7 %copy-start.3 = (s32[1,1,4]{2,1,0:T(1,128)S(1)}, s32[1,1,4]{2,1,0:T(1,128)}, u32[]{:S(2)}) copy-start(s32[1,1,4]{2,1,0:T(1,128)} %param.9) | copy-start | bytes 52
  32.0 0.7 %copy-start.4 = (f32[12]{0:T(128)S(1)}, f32[12]{0:T(128)}, u32[]{:S(2)}) copy-start(f32[12]{0:T(128)} %pos_hbm.1) | copy-start | bytes 148
  32.7 0.7 %copy-start.5 = (f32[20]{0:T(128)S(1)}, f32[20]{0:T(128)}, u32[]{:S(2)}) copy-start(f32[20]{0:T(128)} %time_hbm.1) | copy-start | bytes 244
  36.4 9.9 %collective-permute-start.10 = (bf16[256,640]{1,0:T(8,128)(2,1)S(1)}, bf16[256,640]{1,0:T(8,128)(2,1)S(1)}, u32[]{:S(2)}, u32[]{:S(2)}) collective-permute-start(bf16[256,640]{1,0:T(8,128)(2,1)S(1)} %constant_dynamic-update-slice_fusion.5.refs_0_), channel_id=1, source_target_pairs={{0,4},{1,5},{2,6},{3,7},{4,0},{5,1},{6,2},{7,3},{8,12},{9,13},{10,... | collective-permute-start | bytes 983048 | tf_op jit(solution)/shard_map/ppermute | solution.py:267
  42.3 4.7 %collective-permute-start.11 = (bf16[256,640]{1,0:T(8,128)(2,1)S(1)}, bf16[256,640]{1,0:T(8,128)(2,1)S(1)}, u32[]{:S(2)}, u32[]{:S(2)}) collective-permute-start(bf16[256,640]{1,0:T(8,128)(2,1)S(1)} %collective-permute-done.7.refs_1_), channel_id=1, source_target_pairs={{0,4},{1,5},{2,6},{3,7},{4,0},{5,1},{6,2},{7,3},{8,12},{9,13},{10,... | collective-permute-start | bytes 983048 | tf_op jit(solution)/shard_map/ppermute | solution.py:267
  45.8 1.7 %collective-permute-start.12 = (bf16[256,640]{1,0:T(8,128)(2,1)S(1)}, bf16[256,640]{1,0:T(8,128)(2,1)S(1)}, u32[]{:S(2)}, u32[]{:S(2)}) collective-permute-start(bf16[256,640]{1,0:T(8,128)(2,1)S(1)} %collective-permute-done.8.refs_2_), channel_id=1, source_target_pairs={{0,4},{1,5},{2,6},{3,7},{4,0},{5,1},{6,2},{7,3},{8,12},{9,13},{10,... | collective-permute-start | bytes 983048 | tf_op jit(solution)/shard_map/ppermute | solution.py:267
  45.8 2.2 %collective-permute-start.13 = (bf16[256,640]{1,0:T(8,128)(2,1)S(1)}, bf16[256,640]{1,0:T(8,128)(2,1)S(1)}, u32[]{:S(2)}, u32[]{:S(2)}) collective-permute-start(bf16[256,640]{1,0:T(8,128)(2,1)S(1)} %collective-permute-done.9.refs_3_), channel_id=1, source_target_pairs={{0,4},{1,5},{2,6},{3,7},{4,0},{5,1},{6,2},{7,3},{8,12},{9,13},{10,... | collective-permute-start | bytes 983048 | tf_op jit(solution)/shard_map/ppermute | solution.py:267

commit v3 on v2

--- a/solution.py
+++ b/solution.py
@@ -98,7 +98,7 @@
 
 
 def prepare(lengths, pos_table, time_table, tokens, stamps):
-    anywhere = pl.BlockSpec(memory_space=pl.ANY)
+    hbm = pl.BlockSpec(memory_space=pltpu.HBM)
     vmem = pl.BlockSpec(memory_space=pltpu.VMEM)
     return pl.pallas_call(
         prepare_kernel,
@@ -107,7 +107,7 @@
             jax.ShapeDtypeStruct((ROWS, D), jnp.bfloat16),
             jax.ShapeDtypeStruct((len(PAIRS), BLOCK, BLOCK), jnp.float32),
         ),
-        in_specs=[anywhere] * 5,
+        in_specs=[hbm] * 5,
         out_specs=(vmem,) * 3,
         scratch_shapes=[
             pltpu.SMEM((4,), jnp.int32),
@@ -119,7 +119,12 @@
         ],
         compiler_params=pltpu.CompilerParams(vmem_limit_bytes=VMEM_PREPARE * 2**20),
         cost_estimate=pl.CostEstimate(flops=2 * 10**7, bytes_accessed=5 * 10**6, transcendentals=0),
-    )(lengths, pos_table, time_table, tokens, stamps)
+    )(
+        *[
+            pltpu.with_memory_space_constraint(array, pltpu.HBM)
+            for array in (lengths, pos_table, time_table, tokens, stamps)
+        ]
+    )
 
 
 def half_silu(z):
@@ -132,7 +137,8 @@
     planes_hbm, updated_hbm = refs[:8], refs[8]
     planes, in_weight, out_weight, mixed, totals, updated, sems, out_sems = refs[9:]
     dp, own_x = lax.axis_index("dp"), lax.axis_index("group")
-    own_m, own_odd = dp // 16, lax.rem(dp // 8, 2)
+    own_z = dp // 8
+    own_odd = lax.rem(own_z, 2)
     own_y, own_core = lax.rem(dp // 2, 4), lax.rem(dp, 2)
     def fetch(k, source, target):
         copy = pltpu.make_async_copy(source, target, sems.at[k])
@@ -155,62 +161,42 @@
     for copy in copies_in:
         copy.wait()
 
-    def arrange(at, carry):
-        m, y = at // 4, lax.rem(at, 4)
-        m_slot = lax.rem(own_m + 4 - m, 4)
-        units = []
-        for core in range(2):
-            for x in range(4):
-                if core == 0:
-                    plane, slot = y, lax.rem(own_x + 4 - x, 4)
-                else:
-                    plane, slot = 4 + x, lax.rem(own_y + 4 - y, 4)
-                start = pl.multiple_of((slot * 4 + m_slot) * 16, 16)
-                units.append(planes[plane, pl.ds(start, 16), :].astype(jnp.float32))
-        for half in range(2):
-            odd = own_odd if half == 0 else 1 - own_odd
-            halves = [unit[half * 8 : half * 8 + 8] for unit in units]
-            start = pl.multiple_of(m * 512 + odd * 256 + y * 64, 64)
+    def arrange(y, carry):
+        for slot in range(8):
+            z = lax.rem(own_z - own_odd + 8 - slot // 2 * 2, 8) + jnp.where(slot % 2 == 0, own_odd, 1 - own_odd)
+            pieces = []
+            for core in range(2):
+                for x in range(4):
+                    if core == 0:
+                        plane, line = y, lax.rem(own_x + 4 - x, 4)
+                    else:
+                        plane, line = 4 + x, lax.rem(own_y + 4 - y, 4)
+                    pieces.append(planes[plane, line * 8 + slot].astype(jnp.float32))
+            start = pl.multiple_of(z * 256 + y * 64, 64)
             in_weight[pl.ds(start, 64), :] = jnp.concatenate(
-                [piece[:, :D] for piece in halves]
+                [piece[:, :D] for piece in pieces]
             ).astype(jnp.bfloat16)
-            sides = [
-                jnp.concatenate([piece[:, D:] for piece in halves[c * 4 : c * 4 + 4]], axis=1)
-                for c in range(2)
-            ]
-            start = pl.multiple_of(m * 128 + odd * 64 + y * 16, 16)
-            out_weight[pl.ds(start, 16), :] = jnp.concatenate(sides).astype(jnp.bfloat16)
+            start = pl.multiple_of(z * 64 + y * 16, 16)
+            out_weight[pl.ds(start, 16), :] = jnp.concatenate(
+                [
+                    jnp.concatenate([piece[:, D:] for piece in pieces[c * 4 : c * 4 + 4]], axis=1)
+                    for c in range(2)
+                ]
+            ).astype(jnp.bfloat16)
         return carry
 
-    lax.fori_loop(0, 16, arrange, 0)
-    sends = []
-    for i in range(ROWS // BLOCK):
-        rows = pl.ds(i * BLOCK, BLOCK)
+    lax.fori_loop(0, 4, arrange, 0)
+    for i in range(ROWS // 256):
+        rows = pl.ds(i * 256, 256)
         for part in range(4):
-            cols = pl.ds(part * D, D)
+            cols = pl.ds(part * 512, 512)
             product = lax.dot_general(
                 normed[rows, :], in_weight[cols, :], TRANS_B, preferred_element_type=jnp.float32
             )
             mixed[rows, cols] = half_silu(product * 0.5).astype(jnp.bfloat16)
-
-        def attend(j, first, i=i, rows=rows):
-            keys = pl.ds(j * BLOCK, BLOCK)
-            pair_bias = bias[PAIRS.index((i, j))]
-            for head in range(HEADS):
-                cols = [pl.ds(part * D + head * HEAD_DIM, HEAD_DIM) for part in range(4)]
-                scores = lax.dot_general(
-                    mixed[rows, cols[2]], mixed[keys, cols[3]], TRANS_B,
-                    preferred_element_type=jnp.float32,
-                )
-                weights = half_silu(scores * (0.5 * HEAD_DIM**-0.5) + pair_bias).astype(jnp.bfloat16)
-                product = jnp.dot(weights, mixed[keys, cols[1]], preferred_element_type=jnp.float32)
-                own = pl.ds(head * HEAD_DIM, HEAD_DIM)
-                totals[:, own] = product if first else totals[:, own] + product
-
-        attend(i, True)
-        for j in range(i):
-            attend(j, False)
-        attended = totals[...].astype(jnp.bfloat16).astype(jnp.float32)
+    def finish(i):
+        rows = pl.ds(i * BLOCK, BLOCK)
+        attended = totals[rows, :].astype(jnp.bfloat16).astype(jnp.float32)
         gate = mixed[rows, pl.ds(0, D)].astype(jnp.float32)
         gated = (normalize(attended) * gate).astype(jnp.bfloat16)
         projected = lax.dot_general(
@@ -220,6 +206,24 @@
         copy = pltpu.make_async_copy(updated.at[rows, :], updated_hbm.at[rows, :], out_sems.at[i])
         copy.start()
         sends.append(copy)
+
+    sends = []
+    for j in range(ROWS // BLOCK):
+        rows = pl.ds(j * BLOCK, ROWS - j * BLOCK)
+        keys = pl.ds(j * BLOCK, BLOCK)
+        pair_bias = jnp.concatenate([bias[PAIRS.index((i, j))] for i in range(j, ROWS // BLOCK)])
+        for head in range(HEADS):
+            cols = [pl.ds(part * D + head * HEAD_DIM, HEAD_DIM) for part in range(4)]
+            scores = lax.dot_general(
+                mixed[rows, cols[2]], mixed[keys, cols[3]], TRANS_B,
+                preferred_element_type=jnp.float32,
+            )
+            weights = half_silu(scores * (0.5 * HEAD_DIM**-0.5) + pair_bias).astype(jnp.bfloat16)
+            product = jnp.dot(weights, mixed[keys, cols[1]], preferred_element_type=jnp.float32)
+            own = pl.ds(head * HEAD_DIM, HEAD_DIM)
+            totals[rows, own] = product if j == 0 else totals[rows, own] + product
+    for i in range(ROWS // BLOCK):
+        finish(i)
     for copy in sends:
         copy.wait()
 
@@ -233,11 +237,11 @@
         in_specs=[vmem] * 3 + [anywhere] * 8,
         out_specs=anywhere,
         scratch_shapes=[
-            pltpu.VMEM((8, 256, 640), jnp.bfloat16),
+            pltpu.VMEM((8, 32, 8, D + HEAD_DIM), jnp.bfloat16),
             pltpu.VMEM((4 * D, D), jnp.bfloat16),
             pltpu.VMEM((D, D), jnp.bfloat16),
             pltpu.VMEM((ROWS, 4 * D), jnp.bfloat16),
-            pltpu.VMEM((BLOCK, D), jnp.float32),
+            pltpu.VMEM((ROWS, D), jnp.float32),
             pltpu.VMEM((ROWS, D), jnp.bfloat16),
             pltpu.SemaphoreType.DMA((8,)),
             pltpu.SemaphoreType.DMA((ROWS // BLOCK,)),
@@ -270,7 +274,7 @@
 def gather(in_weight, out_weight):
     group = lax.axis_index("group")
     own = lax.dynamic_slice_in_dim(out_weight.T, group * HEAD_DIM, HEAD_DIM, axis=1)
-    piece = jnp.concatenate([in_weight.T, own], axis=1)
+    piece = jnp.concatenate([in_weight.T, own], axis=1)[None]
     other = send(piece, lambda x, y, z, core: (x, y, z ^ 1, core))
     unit = jnp.concatenate([piece, other])
     units = [unit] + [
@@ -294,11 +298,13 @@
 
 def shards(tokens, stamps, lengths, in_weight, out_weight, pos_table, time_table):
     own_lengths = lengths.reshape(-1)
+    planes = gather(in_weight, out_weight)
+    swapped = swap(planes[:1])
+    swapped, stamps = lax.optimization_barrier((swapped, stamps))
     prepared = prepare(own_lengths, pos_table, time_table, tokens, stamps.reshape(8, TILE))
-    own, *others = gather(in_weight, out_weight)
-    others, prepared = lax.optimization_barrier((others, prepared))
-    planes = [own, *others]
-    return main(*prepared, planes + swap(planes))
+    planes[1], prepared = lax.optimization_barrier((planes[1], prepared))
+    swapped += swap(planes[1:2])
+    return main(*prepared, planes + swapped + swap(planes[2:]))
 
 
 def solution(mesh):

time: 58.8 us -> 53.4 us (0.908)
  local copies, waits for them, and re-layouts: 4.66 us -> 0.78 us
  waiting for transfers between devices: 9.24 us -> 12.8 us
  starting transfers between devices: 29.6 us -> 26.2 us
  Pallas kernels: 13.4 us -> 11.8 us
    unnamed x17 -> x7, local copies, waits for them, and re-layouts: 4.63 us -> 0.75 us
    ppermute x14, waiting for transfers between devices: 9.24 us -> 12.8 us  [send(): return lax.ppermute(array, ('dp', 'group'), moves(step))]
    ppermute x14, starting transfers between devices: 29.6 us -> 26.2 us  [send(): return lax.ppermute(array, ('dp', 'group'), moves(step))]
    pallas_call x1, Pallas kernels: 10.4 us -> 8.04 us  [main(): pl.pallas_call(main_kernel, out_shape=jax.ShapeDtypeStruct((ROWS, D), jnp...]
    broadcast_in_dim x0 -> x1, other arithmetic: none -> 0.7 us  [gather(): piece = jnp.concatenate([in_weight.T, own], axis=1)[None]]
    concatenate x1, other arithmetic: 0.7 us -> 0.01 us  [gather(): unit = jnp.concatenate([piece, other])]
    pallas_call x1, Pallas kernels: 3.06 us -> 3.75 us  [prepare(): pl.pallas_call(prepare_kernel, out_shape=(jax.ShapeDtypeStruct((ROWS, D),...]
  transfers between devices with their start and end apart: 14 -> 14, of which waited for: 8 -> 8; matrix products, arithmetic and copies ran while one was open for 0% -> 1% of each run, Pallas kernels for 5% -> 7%
where the time goes in v3:
time: 53.4 us; the launch traced here: 53.1 us
  starting transfers between devices  26.2 us (49%)
  waiting for transfers between devices  12.8 us (24%)
  Pallas kernels  11.8 us (22%)
  other arithmetic  1.4 us (3%)
  local copies, waits for them, and re-layouts  0.78 us (1%)
    ppermute x14, starting transfers between devices, send(): return lax.ppermute(array, ('dp', 'group'), moves(step))  26.2 us
    ppermute x14, waiting for transfers between devices, send(): return lax.ppermute(array, ('dp', 'group'), moves(step))  12.8 us
    pallas_call x1, Pallas kernels, main(): pl.pallas_call(main_kernel, out_shape=jax.ShapeDtypeStruct((ROWS, D), jnp...  8.04 us
    pallas_call x1, Pallas kernels, prepare(): pl.pallas_call(prepare_kernel, out_shape=(jax.ShapeDtypeStruct((ROWS, D),...  3.75 us
  transfers between devices with their start and end apart: 14, of which 8 were waited for; matrix products, arithmetic and copies ran while one was open for 1% of the time, Pallas kernels for 7%

profile of v3, /device:TPU:1, one launch (start us, length us, event | category | flops | bytes accessed | tf_op | source)
XLA Modules:
  0.0 53.1 jit_solution(16024265216892899426)
XLA Ops:
  0.0 0.0 copy-start
  0.0 0.7 %copy-done = bf16[512,8]{0,1:T(8,128)(2,1)S(1)} copy-done((bf16[512,8]{0,1:T(8,128)(2,1)S(1)}, bf16[512,8]{0,1:T(8,128)(2,1)}, u32[]{:S(2)}) %copy-start) | copy-done | bytes 8216
  0.7 0.7 %maximum_bitcast_fusion = bf16[1,8,640]{2,1,0:T(8,128)(2,1)S(1)} fusion(bf16[8,128]{1,0:T(8,128)(2,1)S(1)} %dynamic-slice_bitcast_fusion, bf16[8,512]{1,0:T(8,128)(2,1)} %bitcast.11), kind=kLoop, calls=%fused_computation.14 | loop fusion | flops 20480 | bytes 20480 | tf_op jit(solution)/shard_map/broadcast_in_dim | solution.py:277
  1.4 2.5 %collective-permute-start = (bf16[1,8,640]{2,1,0:T(8,128)(2,1)S(1)}, bf16[1,8,640]{2,1,0:T(8,128)(2,1)S(1)}, u32[]{:S(2)}, u32[]{:S(2)}) collective-permute-start(bf16[1,8,640]{2,1,0:T(8,128)(2,1)S(1)} %maximum_bitcast_fusion), channel_id=1, source_target_pairs={{0,32},{1,33},{2,34},{3,35},{4,36},{5,37},{6,38},{7,39},{8,40},{9,... | collective-permute-start | bytes 30728 | tf_op jit(solution)/shard_map/ppermute | solution.py:271
  3.9 0.7 %constant_dynamic-update-slice_fusion.4 = (bf16[8,8,640]{2,1,0:T(8,128)(2,1)S(1)}, bf16[32,8,640]{2,1,0:T(8,128)(2,1)S(1)}) fusion(bf16[8,128]{1,0:T(8,128)(2,1)S(1)} %dynamic-slice_bitcast_fusion, bf16[8,512]{1,0:T(8,128)(2,1)} %bitcast.12), kind=kLoop, calls=%fused_computation.4 | loop fusion | flops 20478 | bytes 30720
  4.6 0.4 collective-permute-done
  4.9 5.9 %collective-permute-start.3 = (bf16[2,8,640]{2,1,0:T(8,128)(2,1)S(1)}, bf16[2,8,640]{2,1,0:T(8,128)(2,1)S(1)}, u32[]{:S(2)}, u32[]{:S(2)}) collective-permute-start(bf16[2,8,640]{2,1,0:T(8,128)(2,1)S(1)} %pad_maximum_fusion), channel_id=1, source_target_pairs={{0,192},{1,193},{2,194},{3,195},{4,196},{5,197},{6,198},{7,199},{8... | collective-permute-start | bytes 61448 | tf_op jit(solution)/shard_map/ppermute | solution.py:271
  10.9 1.0 %collective-permute-start.2 = (bf16[2,8,640]{2,1,0:T(8,128)(2,1)S(1)}, bf16[2,8,640]{2,1,0:T(8,128)(2,1)S(1)}, u32[]{:S(2)}, u32[]{:S(2)}) collective-permute-start(bf16[2,8,640]{2,1,0:T(8,128)(2,1)S(1)} %pad_maximum_fusion), channel_id=1, source_target_pairs={{0,128},{1,129},{2,130},{3,131},{4,132},{5,133},{6,134},{7,135},{8... | collective-permute-start | bytes 61448 | tf_op jit(solution)/shard_map/ppermute | solution.py:271
  11.8 2.3 %collective-permute-start.1 = (bf16[2,8,640]{2,1,0:T(8,128)(2,1)S(1)}, bf16[2,8,640]{2,1,0:T(8,128)(2,1)S(1)}, u32[]{:S(2)}, u32[]{:S(2)}) collective-permute-start(bf16[2,8,640]{2,1,0:T(8,128)(2,1)S(1)} %pad_maximum_fusion), channel_id=1, source_target_pairs={{0,64},{1,65},{2,66},{3,67},{4,68},{5,69},{6,70},{7,71},{8,72},{9,... | collective-permute-start | bytes 61448 | tf_op jit(solution)/shard_map/ppermute | solution.py:271
  14.1 2.5 %collective-permute-done.1 = bf16[2,8,640]{2,1,0:T(8,128)(2,1)S(1)} collective-permute-done((bf16[2,8,640]{2,1,0:T(8,128)(2,1)S(1)}, bf16[2,8,640]{2,1,0:T(8,128)(2,1)S(1)}, u32[]{:S(2)}, u32[]{:S(2)}) %collective-permute-start.1) | collective-permute-done | bytes 20512 | tf_op jit(solution)/shard_map/ppermute | solution.py:271
  16.6 0.8 %collective-permute-done.2 = bf16[2,8,640]{2,1,0:T(8,128)(2,1)S(1)} collective-permute-done((bf16[2,8,640]{2,1,0:T(8,128)(2,1)S(1)}, bf16[2,8,640]{2,1,0:T(8,128)(2,1)S(1)}, u32[]{:S(2)}, u32[]{:S(2)}) %collective-permute-start.2) | collective-permute-done | bytes 20512 | tf_op jit(solution)/shard_map/ppermute | solution.py:271
  17.4 0.0 collective-permute-done.3
  17.4 1.4 %collective-permute-start.4 = (bf16[8,8,640]{2,1,0:T(8,128)(2,1)S(1)}, bf16[8,8,640]{2,1,0:T(8,128)(2,1)S(1)}, u32[]{:S(2)}, u32[]{:S(2)}) collective-permute-start(bf16[8,8,640]{2,1,0:T(8,128)(2,1)S(1)} %get-tuple-element.23), channel_id=1, source_target_pairs={{0,1},{1,2},{2,3},{3,0},{4,12},{5,13},{6,14},{7,15},{8,9},{9,10},{... | collective-permute-start | bytes 245768 | tf_op jit(solution)/shard_map/ppermute | solution.py:271
  18.8 1.5 %collective-permute-start.6 = (bf16[8,8,640]{2,1,0:T(8,128)(2,1)S(1)}, bf16[8,8,640]{2,1,0:T(8,128)(2,1)S(1)}, u32[]{:S(2)}, u32[]{:S(2)}) collective-permute-start(bf16[8,8,640]{2,1,0:T(8,128)(2,1)S(1)} %get-tuple-element.23), channel_id=1, source_target_pairs={{0,3},{1,0},{2,1},{3,2},{4,28},{5,29},{6,30},{7,31},{8,11},{9,8},{... | collective-permute-start | bytes 245768 | tf_op jit(solution)/shard_map/ppermute | solution.py:271
  20.3 1.6 %collective-permute-start.5 = (bf16[8,8,640]{2,1,0:T(8,128)(2,1)S(1)}, bf16[8,8,640]{2,1,0:T(8,128)(2,1)S(1)}, u32[]{:S(2)}, u32[]{:S(2)}) collective-permute-start(bf16[8,8,640]{2,1,0:T(8,128)(2,1)S(1)} %get-tuple-element.23), channel_id=1, source_target_pairs={{0,2},{1,3},{2,0},{3,1},{4,20},{5,21},{6,22},{7,23},{8,10},{9,11},... | collective-permute-start | bytes 245768 | tf_op jit(solution)/shard_map/ppermute | solution.py:271
  21.9 0.2 collective-permute-done.4
  22.1 3.0 %collective-permute-done.5 = bf16[8,8,640]{2,1,0:T(8,128)(2,1)S(1)} collective-permute-done((bf16[8,8,640]{2,1,0:T(8,128)(2,1)S(1)}, bf16[8,8,640]{2,1,0:T(8,128)(2,1)S(1)}, u32[]{:S(2)}, u32[]{:S(2)}) %collective-permute-start.5) | collective-permute-done | bytes 81952 | tf_op jit(solution)/shard_map/ppermute | solution.py:271
  25.1 0.0 collective-permute-done.6
  25.2 4.9 %collective-permute-start.8 = (bf16[32,8,640]{2,1,0:T(8,128)(2,1)S(1)}, bf16[32,8,640]{2,1,0:T(8,128)(2,1)S(1)}, u32[]{:S(2)}, u32[]{:S(2)}) collective-permute-start(bf16[32,8,640]{2,1,0:T(8,128)(2,1)S(1)} %constant_dynamic-update-slice_fusion.5.refs_0_), channel_id=1, source_target_pairs={{0,4},{1,5},{2,6},{3,7},{4,0},{5,1},{6,2},{7,3},{8,12},{9,13},{10,... | collective-permute-start | bytes 983048 | tf_op jit(solution)/shard_map/ppermute | solution.py:271
  30.1 0.0 collective-permute-start.7
  30.1 2.7 %collective-permute-start.10 = (bf16[32,8,640]{2,1,0:T(8,128)(2,1)S(1)}, bf16[32,8,640]{2,1,0:T(8,128)(2,1)S(1)}, u32[]{:S(2)}, u32[]{:S(2)}) collective-permute-start(bf16[32,8,640]{2,1,0:T(8,128)(2,1)S(1)} %constant_dynamic-update-slice_fusion.5.refs_0_), channel_id=1, source_target_pairs={{0,24},{1,25},{2,26},{3,27},{4,7},{5,4},{6,5},{7,6},{8,0},{9,1},{1... | collective-permute-start | bytes 983048 | tf_op jit(solution)/shard_map/ppermute | solution.py:271
  32.7 0.3 collective-permute-start.9
  33.1 0.0 collective-permute-done.8.refs_4_
  33.1 3.7 %shard_map.73 = (bf16[1024,512]{1,0:T(8,128)(2,1)S(1)}, bf16[1024,512]{1,0:T(8,128)(2,1)S(1)}, f32[10,256,256]{2,1,0:T(8,128)S(1)}) custom-call(s32[4]{0:T(128)} %bitcast.14, f32[12]{0:T(128)} %pos_hbm.1, f32[20]{0:T(128)} %time_hbm.1, bf16[1024,512]{1,0:T(8,128)(2,1)} %tokens_hbm.1, s32[8,128]{1,0:T(8,128)} %bitcast.13), custom_call_target="tpu_custom_call" | custom-call | flops 20000000 | bytes 5000000 | tf_op jit(solution)/shard_map/pallas_call | solution.py:103
  36.8 4.2 %collective-permute-done.7.refs_1_ = bf16[32,8,640]{2,1,0:T(8,128)(2,1)S(1)} collective-permute-done((bf16[32,8,640]{2,1,0:T(8,128)(2,1)S(1)}, bf16[32,8,640]{2,1,0:T(8,128)(2,1)S(1)}, u32[]{:S(2)}, u32[]{:S(2)}) %collective-permute-start.7) | collective-permute-done | bytes 327712 | tf_op jit(solution)/shard_map/ppermute | solution.py:271
  41.0 0.0 collective-permute-done.10.refs_3_
  41.0 0.0 collective-permute-start.13
  41.0 0.0 collective-permute-done.9.refs_2_
  41.0 2.2 %collective-permute-start.12 = (bf16[32,8,640]{2,1,0:T(8,128)(2,1)S(1)}, bf16[32,8,640]{2,1,0:T(8,128)(2,1)S(1)}, u32[]{:S(2)}, u32[]{:S(2)}) collective-permute-start(bf16[32,8,640]{2,1,0:T(8,128)(2,1)S(1)} %collective-permute-done.9.refs_2_), channel_id=1, source_target_pairs={{0,4},{1,5},{2,6},{3,7},{4,0},{5,1},{6,2},{7,3},{8,12},{9,13},{10,... | collective-permute-start | bytes 983048 | tf_op jit(solution)/shard_map/ppermute | solution.py:271
  43.2 0.0 collective-permute-start.11
  43.2 0.0 collective-permute-done.13.refs_7_
  43.2 1.2 %collective-permute-done.12.refs_6_ = bf16[32,8,640]{2,1,0:T(8,128)(2,1)S(1)} collective-permute-done((bf16[32,8,640]{2,1,0:T(8,128)(2,1)S(1)}, bf16[32,8,640]{2,1,0:T(8,128)(2,1)S(1)}, u32[]{:S(2)}, u32[]{:S(2)}) %collective-permute-start.12) | collective-permute-done | bytes 327712 | tf_op jit(solution)/shard_map/ppermute | solution.py:271
  44.5 0.5 collective-permute-done.11.refs_5_
  44.9 8.0 %shard_map.74 = bf16[1024,512]{1,0:T(8,128)(2,1)} custom-call(bf16[1024,512]{1,0:T(8,128)(2,1)S(1)} %get-tuple-element.18.tokens, bf16[1024,512]{1,0:T(8,128)(2,1)S(1)} %get-tuple-element.19.normed, f32[10,256,256]{2,1,0:T(8,128)S(1)} %get-tuple-element.20.bias, bf16[32,8,640]{2,1,0:T(8,128)(2,1)S(1)} %constant_dynamic-update-slice_fusion.5.refs_0_, ...), custom_call_target="tpu_custom_call" | custom-call | flops 5000000000 | bytes 9000000 | tf_op jit(solution)/shard_map/pallas_call | solution.py:234
  (9 shorter events, 0.1 us)
Async XLA Ops:
  0.0 0.7 %copy-start = (bf16[512,8]{0,1:T(8,128)(2,1)S(1)}, bf16[512,8]{0,1:T(8,128)(2,1)}, u32[]{:S(2)}) copy-start(bf16[512,8]{0,1:T(8,128)(2,1)} %param.11) | copy-start | bytes 24580
  1.4 3.5 %collective-permute-start = (bf16[1,8,640]{2,1,0:T(8,128)(2,1)S(1)}, bf16[1,8,640]{2,1,0:T(8,128)(2,1)S(1)}, u32[]{:S(2)}, u32[]{:S(2)}) collective-permute-start(bf16[1,8,640]{2,1,0:T(8,128)(2,1)S(1)} %maximum_bitcast_fusion), channel_id=1, source_target_pairs={{0,32},{1,33},{2,34},{3,35},{4,36},{5,37},{6,38},{7,39},{8,40},{9,... | collective-permute-start | bytes 30728 | tf_op jit(solution)/shard_map/ppermute | solution.py:271
  4.9 12.5 %collective-permute-start.3 = (bf16[2,8,640]{2,1,0:T(8,128)(2,1)S(1)}, bf16[2,8,640]{2,1,0:T(8,128)(2,1)S(1)}, u32[]{:S(2)}, u32[]{:S(2)}) collective-permute-start(bf16[2,8,640]{2,1,0:T(8,128)(2,1)S(1)} %pad_maximum_fusion), channel_id=1, source_target_pairs={{0,192},{1,193},{2,194},{3,195},{4,196},{5,197},{6,198},{7,199},{8... | collective-permute-start | bytes 61448 | tf_op jit(solution)/shard_map/ppermute | solution.py:271
  10.9 6.5 %collective-permute-start.2 = (bf16[2,8,640]{2,1,0:T(8,128)(2,1)S(1)}, bf16[2,8,640]{2,1,0:T(8,128)(2,1)S(1)}, u32[]{:S(2)}, u32[]{:S(2)}) collective-permute-start(bf16[2,8,640]{2,1,0:T(8,128)(2,1)S(1)} %pad_maximum_fusion), channel_id=1, source_target_pairs={{0,128},{1,129},{2,130},{3,131},{4,132},{5,133},{6,134},{7,135},{8... | collective-permute-start | bytes 61448 | tf_op jit(solution)/shard_map/ppermute | solution.py:271
  11.8 4.7 %collective-permute-start.1 = (bf16[2,8,640]{2,1,0:T(8,128)(2,1)S(1)}, bf16[2,8,640]{2,1,0:T(8,128)(2,1)S(1)}, u32[]{:S(2)}, u32[]{:S(2)}) collective-permute-start(bf16[2,8,640]{2,1,0:T(8,128)(2,1)S(1)} %pad_maximum_fusion), channel_id=1, source_target_pairs={{0,64},{1,65},{2,66},{3,67},{4,68},{5,69},{6,70},{7,71},{8,72},{9,... | collective-permute-start | bytes 61448 | tf_op jit(solution)/shard_map/ppermute | solution.py:271
  17.4 4.6 %collective-permute-start.4 = (bf16[8,8,640]{2,1,0:T(8,128)(2,1)S(1)}, bf16[8,8,640]{2,1,0:T(8,128)(2,1)S(1)}, u32[]{:S(2)}, u32[]{:S(2)}) collective-permute-start(bf16[8,8,640]{2,1,0:T(8,128)(2,1)S(1)} %get-tuple-element.23), channel_id=1, source_target_pairs={{0,1},{1,2},{2,3},{3,0},{4,12},{5,13},{6,14},{7,15},{8,9},{9,10},{... | collective-permute-start | bytes 245768 | tf_op jit(solution)/shard_map/ppermute | solution.py:271
  18.8 6.3 %collective-permute-start.6 = (bf16[8,8,640]{2,1,0:T(8,128)(2,1)S(1)}, bf16[8,8,640]{2,1,0:T(8,128)(2,1)S(1)}, u32[]{:S(2)}, u32[]{:S(2)}) collective-permute-start(bf16[8,8,640]{2,1,0:T(8,128)(2,1)S(1)} %get-tuple-element.23), channel_id=1, source_target_pairs={{0,3},{1,0},{2,1},{3,2},{4,28},{5,29},{6,30},{7,31},{8,11},{9,8},{... | collective-permute-start | bytes 245768 | tf_op jit(solution)/shard_map/ppermute | solution.py:271
  20.3 4.8 %collective-permute-start.5 = (bf16[8,8,640]{2,1,0:T(8,128)(2,1)S(1)}, bf16[8,8,640]{2,1,0:T(8,128)(2,1)S(1)}, u32[]{:S(2)}, u32[]{:S(2)}) collective-permute-start(bf16[8,8,640]{2,1,0:T(8,128)(2,1)S(1)} %get-tuple-element.23), channel_id=1, source_target_pairs={{0,2},{1,3},{2,0},{3,1},{4,20},{5,21},{6,22},{7,23},{8,10},{9,11},... | collective-permute-start | bytes 245768 | tf_op jit(solution)/shard_map/ppermute | solution.py:271
  25.2 7.9 %collective-permute-start.8 = (bf16[32,8,640]{2,1,0:T(8,128)(2,1)S(1)}, bf16[32,8,640]{2,1,0:T(8,128)(2,1)S(1)}, u32[]{:S(2)}, u32[]{:S(2)}) collective-permute-start(bf16[32,8,640]{2,1,0:T(8,128)(2,1)S(1)} %constant_dynamic-update-slice_fusion.5.refs_0_), channel_id=1, source_target_pairs={{0,4},{1,5},{2,6},{3,7},{4,0},{5,1},{6,2},{7,3},{8,12},{9,13},{10,... | collective-permute-start | bytes 983048 | tf_op jit(solution)/shard_map/ppermute | solution.py:271
  30.1 10.9 %collective-permute-start.7 = (bf16[32,8,640]{2,1,0:T(8,128)(2,1)S(1)}, bf16[32,8,640]{2,1,0:T(8,128)(2,1)S(1)}, u32[]{:S(2)}, u32[]{:S(2)}) collective-permute-start(bf16[32,8,640]{2,1,0:T(8,128)(2,1)S(1)} %constant_dynamic-update-slice_fusion.5.refs_0_), channel_id=1, source_target_pairs={{0,8},{1,9},{2,10},{3,11},{4,5},{5,6},{6,7},{7,4},{8,16},{9,17},{1... | collective-permute-start | bytes 983048 | tf_op jit(solution)/shard_map/ppermute | solution.py:271
  30.1 10.9 %collective-permute-start.10 = (bf16[32,8,640]{2,1,0:T(8,128)(2,1)S(1)}, bf16[32,8,640]{2,1,0:T(8,128)(2,1)S(1)}, u32[]{:S(2)}, u32[]{:S(2)}) collective-permute-start(bf16[32,8,640]{2,1,0:T(8,128)(2,1)S(1)} %constant_dynamic-update-slice_fusion.5.refs_0_), channel_id=1, source_target_pairs={{0,24},{1,25},{2,26},{3,27},{4,7},{5,4},{6,5},{7,6},{8,0},{9,1},{1... | collective-permute-start | bytes 983048 | tf_op jit(solution)/shard_map/ppermute | solution.py:271
  32.7 8.3 %collective-permute-start.9 = (bf16[32,8,640]{2,1,0:T(8,128)(2,1)S(1)}, bf16[32,8,640]{2,1,0:T(8,128)(2,1)S(1)}, u32[]{:S(2)}, u32[]{:S(2)}) collective-permute-start(bf16[32,8,640]{2,1,0:T(8,128)(2,1)S(1)} %constant_dynamic-update-slice_fusion.5.refs_0_), channel_id=1, source_target_pairs={{0,16},{1,17},{2,18},{3,19},{4,6},{5,7},{6,4},{7,5},{8,24},{9,25},... | collective-permute-start | bytes 983048 | tf_op jit(solution)/shard_map/ppermute | solution.py:271
  41.0 2.2 %collective-permute-start.13 = (bf16[32,8,640]{2,1,0:T(8,128)(2,1)S(1)}, bf16[32,8,640]{2,1,0:T(8,128)(2,1)S(1)}, u32[]{:S(2)}, u32[]{:S(2)}) collective-permute-start(bf16[32,8,640]{2,1,0:T(8,128)(2,1)S(1)} %collective-permute-done.10.refs_3_), channel_id=1, source_target_pairs={{0,4},{1,5},{2,6},{3,7},{4,0},{5,1},{6,2},{7,3},{8,12},{9,13},{10,... | collective-permute-start | bytes 983048 | tf_op jit(solution)/shard_map/ppermute | solution.py:271
  41.0 3.4 %collective-permute-start.12 = (bf16[32,8,640]{2,1,0:T(8,128)(2,1)S(1)}, bf16[32,8,640]{2,1,0:T(8,128)(2,1)S(1)}, u32[]{:S(2)}, u32[]{:S(2)}) collective-permute-start(bf16[32,8,640]{2,1,0:T(8,128)(2,1)S(1)} %collective-permute-done.9.refs_2_), channel_id=1, source_target_pairs={{0,4},{1,5},{2,6},{3,7},{4,0},{5,1},{6,2},{7,3},{8,12},{9,13},{10,... | collective-permute-start | bytes 983048 | tf_op jit(solution)/shard_map/ppermute | solution.py:271
  43.2 1.7 %collective-permute-start.11 = (bf16[32,8,640]{2,1,0:T(8,128)(2,1)S(1)}, bf16[32,8,640]{2,1,0:T(8,128)(2,1)S(1)}, u32[]{:S(2)}, u32[]{:S(2)}) collective-permute-start(bf16[32,8,640]{2,1,0:T(8,128)(2,1)S(1)} %collective-permute-done.7.refs_1_), channel_id=1, source_target_pairs={{0,4},{1,5},{2,6},{3,7},{4,0},{5,1},{6,2},{7,3},{8,12},{9,13},{10,... | collective-permute-start | bytes 983048 | tf_op jit(solution)/shard_map/ppermute | solution.py:271

commit v4 on v3

--- a/solution.py
+++ b/solution.py
@@ -14,6 +14,7 @@
 POS_BUCKETS = 12
 TIME_BUCKETS = 20
 NEVER = -1e30
+STEPS = (0, -1, 1, 2, -2, -3, 3, 4)
 VMEM_PREPARE = 16
 VMEM_MAIN = 32
 TRANS_B = (((1,), (1,)), ((), ()))
@@ -131,6 +132,12 @@
     return z + z * jnp.tanh(z)
 
 
+def line_slot(apart):
+    apart = lax.rem(apart, 4)
+    slot = jnp.where(apart == 1, 1, jnp.where(apart == 2, 3, 2))
+    return jnp.where(apart == 0, 0, slot)
+
+
 def main_kernel(
     tokens, normed, bias, *refs
 ):
@@ -163,14 +170,14 @@
 
     def arrange(y, carry):
         for slot in range(8):
-            z = lax.rem(own_z - own_odd + 8 - slot // 2 * 2, 8) + jnp.where(slot % 2 == 0, own_odd, 1 - own_odd)
+            z = lax.rem(own_z + 8 + jnp.where(own_odd == 1, STEPS[slot], -STEPS[slot]), 8)
             pieces = []
             for core in range(2):
                 for x in range(4):
                     if core == 0:
-                        plane, line = y, lax.rem(own_x + 4 - x, 4)
+                        plane, line = y, line_slot(own_x + 4 - x)
                     else:
-                        plane, line = 4 + x, lax.rem(own_y + 4 - y, 4)
+                        plane, line = 4 + x, line_slot(own_y + 4 - y)
                     pieces.append(planes[plane, line * 8 + slot].astype(jnp.float32))
             start = pl.multiple_of(z * 256 + y * 64, 64)
             in_weight[pl.ds(start, 64), :] = jnp.concatenate(
@@ -277,13 +284,16 @@
     piece = jnp.concatenate([in_weight.T, own], axis=1)[None]
     other = send(piece, lambda x, y, z, core: (x, y, z ^ 1, core))
     unit = jnp.concatenate([piece, other])
-    units = [unit] + [
-        send(unit, lambda x, y, z, core, k=k: (x, y, z + 2 * k, core)) for k in (1, 2, 3)
+    units = [
+        unit,
+        send(unit, lambda x, y, z, core: (x, y, z + 2 * (z % 2) - 1, core)),
+        send(unit, lambda x, y, z, core: (x, y, z + 4 * (z % 2) - 2, core)),
+        send(unit, lambda x, y, z, core: (x, y, z + 6 * (z % 2) - 3, core)),
     ]
     line = jnp.concatenate(units)
     lines = [line] + [
         send(line, lambda x, y, z, core, k=k: (x + k * (1 - core), y + k * core, z, core))
-        for k in (1, 2, 3)
+        for k in (1, 3, 2)
     ]
     plane = jnp.concatenate(lines)
     return [plane] + [

time: 53.4 us -> 51.5 us (0.964)
  waiting for transfers between devices: 12.8 us -> 10.2 us
    ppermute x14, waiting for transfers between devices: 12.8 us -> 10.2 us  [send(): return lax.ppermute(array, ('dp', 'group'), moves(step))]
where the time goes in v4:
time: 51.5 us; the launch traced here: 51.2 us
  starting transfers between devices  26.7 us (52%)
  Pallas kernels  11.9 us (23%)
  waiting for transfers between devices  10.2 us (20%)
  other arithmetic  1.4 us (3%)
  local copies, waits for them, and re-layouts  0.78 us (2%)
    ppermute x14, starting transfers between devices, send(): return lax.ppermute(array, ('dp', 'group'), moves(step))  26.7 us
    ppermute x14, waiting for transfers between devices, send(): return lax.ppermute(array, ('dp', 'group'), moves(step))  10.2 us
    pallas_call x1, Pallas kernels, main(): pl.pallas_call(main_kernel, out_shape=jax.ShapeDtypeStruct((ROWS, D), jnp...  8.19 us
    pallas_call x1, Pallas kernels, prepare(): pl.pallas_call(prepare_kernel, out_shape=(jax.ShapeDtypeStruct((ROWS, D),...  3.75 us
  transfers between devices with their start and end apart: 14, of which 8 were waited for; matrix products, arithmetic and copies ran while one was open for 1% of the time, Pallas kernels for 7%

profile of v4, /device:TPU:1, one launch (start us, length us, event | category | flops | bytes accessed | tf_op | source)
XLA Modules:
  0.0 51.2 jit_solution(9190207040019301947)
XLA Ops:
  0.0 0.0 copy-start
  0.0 0.7 %copy-done = bf16[512,8]{0,1:T(8,128)(2,1)S(1)} copy-done((bf16[512,8]{0,1:T(8,128)(2,1)S(1)}, bf16[512,8]{0,1:T(8,128)(2,1)}, u32[]{:S(2)}) %copy-start) | copy-done | bytes 8216
  0.7 0.7 %maximum_bitcast_fusion = bf16[1,8,640]{2,1,0:T(8,128)(2,1)S(1)} fusion(bf16[8,128]{1,0:T(8,128)(2,1)S(1)} %dynamic-slice_bitcast_fusion, bf16[8,512]{1,0:T(8,128)(2,1)} %bitcast.11), kind=kLoop, calls=%fused_computation.14 | loop fusion | flops 20480 | bytes 20480 | tf_op jit(solution)/shard_map/broadcast_in_dim | solution.py:284
  1.4 2.5 %collective-permute-start = (bf16[1,8,640]{2,1,0:T(8,128)(2,1)S(1)}, bf16[1,8,640]{2,1,0:T(8,128)(2,1)S(1)}, u32[]{:S(2)}, u32[]{:S(2)}) collective-permute-start(bf16[1,8,640]{2,1,0:T(8,128)(2,1)S(1)} %maximum_bitcast_fusion), channel_id=1, source_target_pairs={{0,32},{1,33},{2,34},{3,35},{4,36},{5,37},{6,38},{7,39},{8,40},{9,... | collective-permute-start | bytes 30728 | tf_op jit(solution)/shard_map/ppermute | solution.py:278
  3.9 0.7 %constant_dynamic-update-slice_fusion.4 = (bf16[8,8,640]{2,1,0:T(8,128)(2,1)S(1)}, bf16[32,8,640]{2,1,0:T(8,128)(2,1)S(1)}) fusion(bf16[8,128]{1,0:T(8,128)(2,1)S(1)} %dynamic-slice_bitcast_fusion, bf16[8,512]{1,0:T(8,128)(2,1)} %bitcast.12), kind=kLoop, calls=%fused_computation.4 | loop fusion | flops 20478 | bytes 30720
  4.6 0.4 collective-permute-done
  4.9 6.4 %collective-permute-start.3 = (bf16[2,8,640]{2,1,0:T(8,128)(2,1)S(1)}, bf16[2,8,640]{2,1,0:T(8,128)(2,1)S(1)}, u32[]{:S(2)}, u32[]{:S(2)}) collective-permute-start(bf16[2,8,640]{2,1,0:T(8,128)(2,1)S(1)} %pad_maximum_fusion), channel_id=1, source_target_pairs={{0,160},{1,161},{2,162},{3,163},{4,164},{5,165},{6,166},{7,167},{8... | collective-permute-start | bytes 61448 | tf_op jit(solution)/shard_map/ppermute | solution.py:278
  11.3 0.3 collective-permute-start.2
  11.6 2.8 %collective-permute-start.1 = (bf16[2,8,640]{2,1,0:T(8,128)(2,1)S(1)}, bf16[2,8,640]{2,1,0:T(8,128)(2,1)S(1)}, u32[]{:S(2)}, u32[]{:S(2)}) collective-permute-start(bf16[2,8,640]{2,1,0:T(8,128)(2,1)S(1)} %pad_maximum_fusion), channel_id=1, source_target_pairs={{0,224},{1,225},{2,226},{3,227},{4,228},{5,229},{6,230},{7,231},{8... | collective-permute-start | bytes 61448 | tf_op jit(solution)/shard_map/ppermute | solution.py:278
  14.4 1.4 %collective-permute-done.1 = bf16[2,8,640]{2,1,0:T(8,128)(2,1)S(1)} collective-permute-done((bf16[2,8,640]{2,1,0:T(8,128)(2,1)S(1)}, bf16[2,8,640]{2,1,0:T(8,128)(2,1)S(1)}, u32[]{:S(2)}, u32[]{:S(2)}) %collective-permute-start.1) | collective-permute-done | bytes 20512 | tf_op jit(solution)/shard_map/ppermute | solution.py:278
  15.8 0.0 collective-permute-done.2
  15.8 0.0 collective-permute-done.3
  15.9 1.4 %collective-permute-start.4 = (bf16[8,8,640]{2,1,0:T(8,128)(2,1)S(1)}, bf16[8,8,640]{2,1,0:T(8,128)(2,1)S(1)}, u32[]{:S(2)}, u32[]{:S(2)}) collective-permute-start(bf16[8,8,640]{2,1,0:T(8,128)(2,1)S(1)} %get-tuple-element.23), channel_id=1, source_target_pairs={{0,1},{1,2},{2,3},{3,0},{4,12},{5,13},{6,14},{7,15},{8,9},{9,10},{... | collective-permute-start | bytes 245768 | tf_op jit(solution)/shard_map/ppermute | solution.py:278
  17.2 2.6 %collective-permute-start.6 = (bf16[8,8,640]{2,1,0:T(8,128)(2,1)S(1)}, bf16[8,8,640]{2,1,0:T(8,128)(2,1)S(1)}, u32[]{:S(2)}, u32[]{:S(2)}) collective-permute-start(bf16[8,8,640]{2,1,0:T(8,128)(2,1)S(1)} %get-tuple-element.23), channel_id=1, source_target_pairs={{0,2},{1,3},{2,0},{3,1},{4,20},{5,21},{6,22},{7,23},{8,10},{9,11},... | collective-permute-start | bytes 245768 | tf_op jit(solution)/shard_map/ppermute | solution.py:278
  19.9 1.1 %collective-permute-start.5 = (bf16[8,8,640]{2,1,0:T(8,128)(2,1)S(1)}, bf16[8,8,640]{2,1,0:T(8,128)(2,1)S(1)}, u32[]{:S(2)}, u32[]{:S(2)}) collective-permute-start(bf16[8,8,640]{2,1,0:T(8,128)(2,1)S(1)} %get-tuple-element.23), channel_id=1, source_target_pairs={{0,3},{1,0},{2,1},{3,2},{4,28},{5,29},{6,30},{7,31},{8,11},{9,8},{... | collective-permute-start | bytes 245768 | tf_op jit(solution)/shard_map/ppermute | solution.py:278
  20.9 0.0 collective-permute-done.4
  21.0 2.2 %collective-permute-done.5 = bf16[8,8,640]{2,1,0:T(8,128)(2,1)S(1)} collective-permute-done((bf16[8,8,640]{2,1,0:T(8,128)(2,1)S(1)}, bf16[8,8,640]{2,1,0:T(8,128)(2,1)S(1)}, u32[]{:S(2)}, u32[]{:S(2)}) %collective-permute-start.5) | collective-permute-done | bytes 81952 | tf_op jit(solution)/shard_map/ppermute | solution.py:278
  23.2 0.0 collective-permute-done.6
  23.2 4.8 %collective-permute-start.8 = (bf16[32,8,640]{2,1,0:T(8,128)(2,1)S(1)}, bf16[32,8,640]{2,1,0:T(8,128)(2,1)S(1)}, u32[]{:S(2)}, u32[]{:S(2)}) collective-permute-start(bf16[32,8,640]{2,1,0:T(8,128)(2,1)S(1)} %constant_dynamic-update-slice_fusion.5.refs_0_), channel_id=1, source_target_pairs={{0,4},{1,5},{2,6},{3,7},{4,0},{5,1},{6,2},{7,3},{8,12},{9,13},{10,... | collective-permute-start | bytes 983048 | tf_op jit(solution)/shard_map/ppermute | solution.py:278
  28.0 0.5 collective-permute-start.7
  28.5 2.2 %collective-permute-start.10 = (bf16[32,8,640]{2,1,0:T(8,128)(2,1)S(1)}, bf16[32,8,640]{2,1,0:T(8,128)(2,1)S(1)}, u32[]{:S(2)}, u32[]{:S(2)}) collective-permute-start(bf16[32,8,640]{2,1,0:T(8,128)(2,1)S(1)} %constant_dynamic-update-slice_fusion.5.refs_0_), channel_id=1, source_target_pairs={{0,24},{1,25},{2,26},{3,27},{4,7},{5,4},{6,5},{7,6},{8,0},{9,1},{1... | collective-permute-start | bytes 983048 | tf_op jit(solution)/shard_map/ppermute | solution.py:278
  30.7 0.9 %collective-permute-start.9 = (bf16[32,8,640]{2,1,0:T(8,128)(2,1)S(1)}, bf16[32,8,640]{2,1,0:T(8,128)(2,1)S(1)}, u32[]{:S(2)}, u32[]{:S(2)}) collective-permute-start(bf16[32,8,640]{2,1,0:T(8,128)(2,1)S(1)} %constant_dynamic-update-slice_fusion.5.refs_0_), channel_id=1, source_target_pairs={{0,16},{1,17},{2,18},{3,19},{4,6},{5,7},{6,4},{7,5},{8,24},{9,25},... | collective-permute-start | bytes 983048 | tf_op jit(solution)/shard_map/ppermute | solution.py:278
  31.6 0.0 collective-permute-done.8.refs_4_
  31.6 3.7 %shard_map.73 = (bf16[1024,512]{1,0:T(8,128)(2,1)S(1)}, bf16[1024,512]{1,0:T(8,128)(2,1)S(1)}, f32[10,256,256]{2,1,0:T(8,128)S(1)}) custom-call(s32[4]{0:T(128)} %bitcast.14, f32[12]{0:T(128)} %pos_hbm.1, f32[20]{0:T(128)} %time_hbm.1, bf16[1024,512]{1,0:T(8,128)(2,1)} %tokens_hbm.1, s32[8,128]{1,0:T(8,128)} %bitcast.13), custom_call_target="tpu_custom_call" | custom-call | flops 20000000 | bytes 5000000 | tf_op jit(solution)/shard_map/pallas_call | solution.py:104
  35.3 0.1 collective-permute-done.7.refs_1_
  35.4 2.8 %collective-permute-done.10.refs_3_ = bf16[32,8,640]{2,1,0:T(8,128)(2,1)S(1)} collective-permute-done((bf16[32,8,640]{2,1,0:T(8,128)(2,1)S(1)}, bf16[32,8,640]{2,1,0:T(8,128)(2,1)S(1)}, u32[]{:S(2)}, u32[]{:S(2)}) %collective-permute-start.10) | collective-permute-done | bytes 327712 | tf_op jit(solution)/shard_map/ppermute | solution.py:278
  38.2 0.0 collective-permute-start.13
  38.2 1.6 %collective-permute-done.9.refs_2_ = bf16[32,8,640]{2,1,0:T(8,128)(2,1)S(1)} collective-permute-done((bf16[32,8,640]{2,1,0:T(8,128)(2,1)S(1)}, bf16[32,8,640]{2,1,0:T(8,128)(2,1)S(1)}, u32[]{:S(2)}, u32[]{:S(2)}) %collective-permute-start.9) | collective-permute-done | bytes 327712 | tf_op jit(solution)/shard_map/ppermute | solution.py:278
  39.8 1.3 %collective-permute-start.12 = (bf16[32,8,640]{2,1,0:T(8,128)(2,1)S(1)}, bf16[32,8,640]{2,1,0:T(8,128)(2,1)S(1)}, u32[]{:S(2)}, u32[]{:S(2)}) collective-permute-start(bf16[32,8,640]{2,1,0:T(8,128)(2,1)S(1)} %collective-permute-done.9.refs_2_), channel_id=1, source_target_pairs={{0,4},{1,5},{2,6},{3,7},{4,0},{5,1},{6,2},{7,3},{8,12},{9,13},{10,... | collective-permute-start | bytes 983048 | tf_op jit(solution)/shard_map/ppermute | solution.py:278
  41.1 0.0 collective-permute-start.11
  41.1 0.0 collective-permute-done.13.refs_7_
  41.1 1.2 %collective-permute-done.12.refs_6_ = bf16[32,8,640]{2,1,0:T(8,128)(2,1)S(1)} collective-permute-done((bf16[32,8,640]{2,1,0:T(8,128)(2,1)S(1)}, bf16[32,8,640]{2,1,0:T(8,128)(2,1)S(1)}, u32[]{:S(2)}, u32[]{:S(2)}) %collective-permute-start.12) | collective-permute-done | bytes 327712 | tf_op jit(solution)/shard_map/ppermute | solution.py:278
  42.4 0.5 collective-permute-done.11.refs_5_
  42.9 8.2 %shard_map.74 = bf16[1024,512]{1,0:T(8,128)(2,1)} custom-call(bf16[1024,512]{1,0:T(8,128)(2,1)S(1)} %get-tuple-element.18.tokens, bf16[1024,512]{1,0:T(8,128)(2,1)S(1)} %get-tuple-element.19.normed, f32[10,256,256]{2,1,0:T(8,128)S(1)} %get-tuple-element.20.bias, bf16[32,8,640]{2,1,0:T(8,128)(2,1)S(1)} %constant_dynamic-update-slice_fusion.5.refs_0_, ...), custom_call_target="tpu_custom_call" | custom-call | flops 5000000000 | bytes 9000000 | tf_op jit(solution)/shard_map/pallas_call | solution.py:241
  (9 shorter events, 0.1 us)
Async XLA Ops:
  0.0 0.7 %copy-start = (bf16[512,8]{0,1:T(8,128)(2,1)S(1)}, bf16[512,8]{0,1:T(8,128)(2,1)}, u32[]{:S(2)}) copy-start(bf16[512,8]{0,1:T(8,128)(2,1)} %param.11) | copy-start | bytes 24580
  1.4 3.5 %collective-permute-start = (bf16[1,8,640]{2,1,0:T(8,128)(2,1)S(1)}, bf16[1,8,640]{2,1,0:T(8,128)(2,1)S(1)}, u32[]{:S(2)}, u32[]{:S(2)}) collective-permute-start(bf16[1,8,640]{2,1,0:T(8,128)(2,1)S(1)} %maximum_bitcast_fusion), channel_id=1, source_target_pairs={{0,32},{1,33},{2,34},{3,35},{4,36},{5,37},{6,38},{7,39},{8,40},{9,... | collective-permute-start | bytes 30728 | tf_op jit(solution)/shard_map/ppermute | solution.py:278
  4.9 10.9 %collective-permute-start.3 = (bf16[2,8,640]{2,1,0:T(8,128)(2,1)S(1)}, bf16[2,8,640]{2,1,0:T(8,128)(2,1)S(1)}, u32[]{:S(2)}, u32[]{:S(2)}) collective-permute-start(bf16[2,8,640]{2,1,0:T(8,128)(2,1)S(1)} %pad_maximum_fusion), channel_id=1, source_target_pairs={{0,160},{1,161},{2,162},{3,163},{4,164},{5,165},{6,166},{7,167},{8... | collective-permute-start | bytes 61448 | tf_op jit(solution)/shard_map/ppermute | solution.py:278
  11.3 4.5 %collective-permute-start.2 = (bf16[2,8,640]{2,1,0:T(8,128)(2,1)S(1)}, bf16[2,8,640]{2,1,0:T(8,128)(2,1)S(1)}, u32[]{:S(2)}, u32[]{:S(2)}) collective-permute-start(bf16[2,8,640]{2,1,0:T(8,128)(2,1)S(1)} %pad_maximum_fusion), channel_id=1, source_target_pairs={{0,192},{1,193},{2,194},{3,195},{4,196},{5,197},{6,198},{7,199},{8... | collective-permute-start | bytes 61448 | tf_op jit(solution)/shard_map/ppermute | solution.py:278
  11.6 4.2 %collective-permute-start.1 = (bf16[2,8,640]{2,1,0:T(8,128)(2,1)S(1)}, bf16[2,8,640]{2,1,0:T(8,128)(2,1)S(1)}, u32[]{:S(2)}, u32[]{:S(2)}) collective-permute-start(bf16[2,8,640]{2,1,0:T(8,128)(2,1)S(1)} %pad_maximum_fusion), channel_id=1, source_target_pairs={{0,224},{1,225},{2,226},{3,227},{4,228},{5,229},{6,230},{7,231},{8... | collective-permute-start | bytes 61448 | tf_op jit(solution)/shard_map/ppermute | solution.py:278
  15.9 5.1 %collective-permute-start.4 = (bf16[8,8,640]{2,1,0:T(8,128)(2,1)S(1)}, bf16[8,8,640]{2,1,0:T(8,128)(2,1)S(1)}, u32[]{:S(2)}, u32[]{:S(2)}) collective-permute-start(bf16[8,8,640]{2,1,0:T(8,128)(2,1)S(1)} %get-tuple-element.23), channel_id=1, source_target_pairs={{0,1},{1,2},{2,3},{3,0},{4,12},{5,13},{6,14},{7,15},{8,9},{9,10},{... | collective-permute-start | bytes 245768 | tf_op jit(solution)/shard_map/ppermute | solution.py:278
  17.2 5.9 %collective-permute-start.6 = (bf16[8,8,640]{2,1,0:T(8,128)(2,1)S(1)}, bf16[8,8,640]{2,1,0:T(8,128)(2,1)S(1)}, u32[]{:S(2)}, u32[]{:S(2)}) collective-permute-start(bf16[8,8,640]{2,1,0:T(8,128)(2,1)S(1)} %get-tuple-element.23), channel_id=1, source_target_pairs={{0,2},{1,3},{2,0},{3,1},{4,20},{5,21},{6,22},{7,23},{8,10},{9,11},... | collective-permute-start | bytes 245768 | tf_op jit(solution)/shard_map/ppermute | solution.py:278
  19.9 3.3 %collective-permute-start.5 = (bf16[8,8,640]{2,1,0:T(8,128)(2,1)S(1)}, bf16[8,8,640]{2,1,0:T(8,128)(2,1)S(1)}, u32[]{:S(2)}, u32[]{:S(2)}) collective-permute-start(bf16[8,8,640]{2,1,0:T(8,128)(2,1)S(1)} %get-tuple-element.23), channel_id=1, source_target_pairs={{0,3},{1,0},{2,1},{3,2},{4,28},{5,29},{6,30},{7,31},{8,11},{9,8},{... | collective-permute-start | bytes 245768 | tf_op jit(solution)/shard_map/ppermute | solution.py:278
  23.2 8.3 %collective-permute-start.8 = (bf16[32,8,640]{2,1,0:T(8,128)(2,1)S(1)}, bf16[32,8,640]{2,1,0:T(8,128)(2,1)S(1)}, u32[]{:S(2)}, u32[]{:S(2)}) collective-permute-start(bf16[32,8,640]{2,1,0:T(8,128)(2,1)S(1)} %constant_dynamic-update-slice_fusion.5.refs_0_), channel_id=1, source_target_pairs={{0,4},{1,5},{2,6},{3,7},{4,0},{5,1},{6,2},{7,3},{8,12},{9,13},{10,... | collective-permute-start | bytes 983048 | tf_op jit(solution)/shard_map/ppermute | solution.py:278
  28.0 7.4 %collective-permute-start.7 = (bf16[32,8,640]{2,1,0:T(8,128)(2,1)S(1)}, bf16[32,8,640]{2,1,0:T(8,128)(2,1)S(1)}, u32[]{:S(2)}, u32[]{:S(2)}) collective-permute-start(bf16[32,8,640]{2,1,0:T(8,128)(2,1)S(1)} %constant_dynamic-update-slice_fusion.5.refs_0_), channel_id=1, source_target_pairs={{0,8},{1,9},{2,10},{3,11},{4,5},{5,6},{6,7},{7,4},{8,16},{9,17},{1... | collective-permute-start | bytes 983048 | tf_op jit(solution)/shard_map/ppermute | solution.py:278
  28.5 9.7 %collective-permute-start.10 = (bf16[32,8,640]{2,1,0:T(8,128)(2,1)S(1)}, bf16[32,8,640]{2,1,0:T(8,128)(2,1)S(1)}, u32[]{:S(2)}, u32[]{:S(2)}) collective-permute-start(bf16[32,8,640]{2,1,0:T(8,128)(2,1)S(1)} %constant_dynamic-update-slice_fusion.5.refs_0_), channel_id=1, source_target_pairs={{0,24},{1,25},{2,26},{3,27},{4,7},{5,4},{6,5},{7,6},{8,0},{9,1},{1... | collective-permute-start | bytes 983048 | tf_op jit(solution)/shard_map/ppermute | solution.py:278
  30.7 9.1 %collective-permute-start.9 = (bf16[32,8,640]{2,1,0:T(8,128)(2,1)S(1)}, bf16[32,8,640]{2,1,0:T(8,128)(2,1)S(1)}, u32[]{:S(2)}, u32[]{:S(2)}) collective-permute-start(bf16[32,8,640]{2,1,0:T(8,128)(2,1)S(1)} %constant_dynamic-update-slice_fusion.5.refs_0_), channel_id=1, source_target_pairs={{0,16},{1,17},{2,18},{3,19},{4,6},{5,7},{6,4},{7,5},{8,24},{9,25},... | collective-permute-start | bytes 983048 | tf_op jit(solution)/shard_map/ppermute | solution.py:278
  38.2 2.9 %collective-permute-start.13 = (bf16[32,8,640]{2,1,0:T(8,128)(2,1)S(1)}, bf16[32,8,640]{2,1,0:T(8,128)(2,1)S(1)}, u32[]{:S(2)}, u32[]{:S(2)}) collective-permute-start(bf16[32,8,640]{2,1,0:T(8,128)(2,1)S(1)} %collective-permute-done.10.refs_3_), channel_id=1, source_target_pairs={{0,4},{1,5},{2,6},{3,7},{4,0},{5,1},{6,2},{7,3},{8,12},{9,13},{10,... | collective-permute-start | bytes 983048 | tf_op jit(solution)/shard_map/ppermute | solution.py:278
  39.8 2.6 %collective-permute-start.12 = (bf16[32,8,640]{2,1,0:T(8,128)(2,1)S(1)}, bf16[32,8,640]{2,1,0:T(8,128)(2,1)S(1)}, u32[]{:S(2)}, u32[]{:S(2)}) collective-permute-start(bf16[32,8,640]{2,1,0:T(8,128)(2,1)S(1)} %collective-permute-done.9.refs_2_), channel_id=1, source_target_pairs={{0,4},{1,5},{2,6},{3,7},{4,0},{5,1},{6,2},{7,3},{8,12},{9,13},{10,... | collective-permute-start | bytes 983048 | tf_op jit(solution)/shard_map/ppermute | solution.py:278
  41.1 1.7 %collective-permute-start.11 = (bf16[32,8,640]{2,1,0:T(8,128)(2,1)S(1)}, bf16[32,8,640]{2,1,0:T(8,128)(2,1)S(1)}, u32[]{:S(2)}, u32[]{:S(2)}) collective-permute-start(bf16[32,8,640]{2,1,0:T(8,128)(2,1)S(1)} %collective-permute-done.7.refs_1_), channel_id=1, source_target_pairs={{0,4},{1,5},{2,6},{3,7},{4,0},{5,1},{6,2},{7,3},{8,12},{9,13},{10,... | collective-permute-start | bytes 983048 | tf_op jit(solution)/shard_map/ppermute | solution.py:278

commit v5 on v4

--- a/solution.py
+++ b/solution.py
@@ -141,12 +141,15 @@
 def main_kernel(
     tokens, normed, bias, *refs
 ):
-    planes_hbm, updated_hbm = refs[:8], refs[8]
-    planes, in_weight, out_weight, mixed, totals, updated, sems, out_sems = refs[9:]
+    own_planes, (swapped_own, swapped_near, swapped_far), updated_hbm = refs[:4], refs[4:7], refs[7]
+    planes, in_weight, out_weight, mixed, totals, updated, sems, out_sems = refs[8:]
+    near, last = swapped_near.at[pl.ds(0, 32)], swapped_near.at[pl.ds(32, 32)]
+    sources = [own_planes, (swapped_own, near, swapped_far, last)]
     dp, own_x = lax.axis_index("dp"), lax.axis_index("group")
     own_z = dp // 8
     own_odd = lax.rem(own_z, 2)
     own_y, own_core = lax.rem(dp // 2, 4), lax.rem(dp, 2)
+
     def fetch(k, source, target):
         copy = pltpu.make_async_copy(source, target, sems.at[k])
         copy.start()
@@ -160,7 +163,7 @@
             copies_in.append(
                 fetch(
                     side * 4 + k,
-                    planes_hbm[side * 4 + k],
+                    sources[side][k],
                     planes.at[core * 4 + lax.rem(place + 4 - k, 4)],
                 )
             )
@@ -241,7 +244,7 @@
     return pl.pallas_call(
         main_kernel,
         out_shape=jax.ShapeDtypeStruct((ROWS, D), jnp.bfloat16),
-        in_specs=[vmem] * 3 + [anywhere] * 8,
+        in_specs=[vmem] * 3 + [anywhere] * 7,
         out_specs=anywhere,
         scratch_shapes=[
             pltpu.VMEM((8, 32, 8, D + HEAD_DIM), jnp.bfloat16),
@@ -279,10 +282,17 @@
 
 
 def gather(in_weight, out_weight):
-    group = lax.axis_index("group")
-    own = lax.dynamic_slice_in_dim(out_weight.T, group * HEAD_DIM, HEAD_DIM, axis=1)
-    piece = jnp.concatenate([in_weight.T, own], axis=1)[None]
-    other = send(piece, lambda x, y, z, core: (x, y, z ^ 1, core))
+    part = lax.axis_index("group") * HEAD_DIM
+
+    def piece_of(in_rows, out_rows):
+        side = lax.dynamic_slice_in_dim(out_rows, part, HEAD_DIM, axis=1)
+        return jnp.concatenate([in_rows, side], axis=1)[None]
+
+    piece = piece_of(in_weight.T, out_weight.T)
+    other = piece_of(
+        send(in_weight.T, lambda x, y, z, core: (x, y, z ^ 1, core)),
+        send(out_weight.T, lambda x, y, z, core: (x, y, z ^ 1, core)),
+    )
     unit = jnp.concatenate([piece, other])
     units = [
         unit,
@@ -302,19 +312,19 @@
     ]
 
 
-def swap(planes):
-    return [send(plane, lambda x, y, z, core: (x, y, z, core + 1)) for plane in planes]
+def swap(array):
+    return send(array, lambda x, y, z, core: (x, y, z, core + 1))
 
 
 def shards(tokens, stamps, lengths, in_weight, out_weight, pos_table, time_table):
     own_lengths = lengths.reshape(-1)
     planes = gather(in_weight, out_weight)
-    swapped = swap(planes[:1])
-    swapped, stamps = lax.optimization_barrier((swapped, stamps))
+    swapped_own = swap(planes[0])
+    swapped_own, stamps = lax.optimization_barrier((swapped_own, stamps))
     prepared = prepare(own_lengths, pos_table, time_table, tokens, stamps.reshape(8, TILE))
     planes[1], prepared = lax.optimization_barrier((planes[1], prepared))
-    swapped += swap(planes[1:2])
-    return main(*prepared, planes + swapped + swap(planes[2:]))
+    swapped_near = swap(jnp.concatenate([planes[1], planes[3]]))
+    return main(*prepared, [*planes, swapped_own, swapped_near, swap(planes[2])])
 
 
 def solution(mesh):

time: 51.5 us -> 50.8 us (0.986)
    dynamic_slice x1 -> x2, local copies, waits for them, and re-layouts: 0.01 us -> 0.72 us  [piece_of(): side = lax.dynamic_slice_in_dim(out_rows, part, HEAD_DIM, axis=1)]
    unnamed x7 -> x4, local copies, waits for them, and re-layouts: 0.75 us -> 0.05 us
  transfers between devices with their start and end apart: 14 -> 14, of which waited for: 8 -> 7; matrix products, arithmetic and copies ran while one was open for 1% -> 4% of each run, Pallas kernels for 7% -> 7%
where the time goes in v5:
time: 50.8 us; the launch traced here: 50.6 us
  starting transfers between devices  26.4 us (52%)
  Pallas kernels  11.9 us (23%)
  waiting for transfers between devices  9.75 us (19%)
  other arithmetic  1.49 us (3%)
  local copies, waits for them, and re-layouts  0.79 us (2%)
    ppermute x14, starting transfers between devices, send(): return lax.ppermute(array, ('dp', 'group'), moves(step))  26.4 us
    ppermute x14, waiting for transfers between devices, send(): return lax.ppermute(array, ('dp', 'group'), moves(step))  9.75 us
    pallas_call x1, Pallas kernels, main(): pl.pallas_call(main_kernel, out_shape=jax.ShapeDtypeStruct((ROWS, D), jnp...  8.19 us
    pallas_call x1, Pallas kernels, prepare(): pl.pallas_call(prepare_kernel, out_shape=(jax.ShapeDtypeStruct((ROWS, D),...  3.75 us
  transfers between devices with their start and end apart: 14, of which 7 were waited for; matrix products, arithmetic and copies ran while one was open for 4% of the time, Pallas kernels for 7%

profile of v5, /device:TPU:1, one launch (start us, length us, event | category | flops | bytes accessed | tf_op | source)
XLA Modules:
  0.0 50.6 jit_solution(10722347979645684503)
XLA Ops:
  0.0 2.5 %collective-permute-start = (bf16[8,512]{1,0:T(8,128)(2,1)}, bf16[8,512]{1,0:T(8,128)(2,1)S(1)}, u32[]{:S(2)}, u32[]{:S(2)}) collective-permute-start(bf16[8,512]{1,0:T(8,128)(2,1)} %bitcast.18), channel_id=1, source_target_pairs={{0,32},{1,33},{2,34},{3,35},{4,36},{5,37},{6,38},{7,39},{8,40},{9,... | collective-permute-start | bytes 24584 | tf_op jit(solution)/shard_map/ppermute | solution.py:281
  2.5 0.0 collective-permute-start.1
  2.5 0.7 %dynamic-slice_bitcast_fusion = bf16[8,128]{1,0:T(8,128)(2,1)S(1)} fusion(bf16[512,8]{0,1:T(8,128)(2,1)} %param.11, s32[]{:T(128)S(6)} %select_n.4), kind=kLoop, calls=%fused_computation.17 | loop fusion | bytes 4100 | tf_op jit(solution)/shard_map/dynamic_slice | solution.py:288
  3.2 0.7 %constant_dynamic-update-slice_fusion.4 = (bf16[8,8,640]{2,1,0:T(8,128)(2,1)S(1)}, bf16[32,8,640]{2,1,0:T(8,128)(2,1)S(1)}) fusion(bf16[8,128]{1,0:T(8,128)(2,1)S(1)} %dynamic-slice_bitcast_fusion, bf16[8,512]{1,0:T(8,128)(2,1)} %bitcast.19), kind=kLoop, calls=%fused_computation.5 | loop fusion | flops 20478 | bytes 30720
  3.9 0.7 %maximum_bitcast_fusion = bf16[1,8,640]{2,1,0:T(8,128)(2,1)S(1)} fusion(bf16[8,128]{1,0:T(8,128)(2,1)S(1)} %dynamic-slice_bitcast_fusion, bf16[8,512]{1,0:T(8,128)(2,1)} %bitcast.20), kind=kLoop, calls=%fused_computation.15 | loop fusion | flops 20480 | bytes 20480 | tf_op jit(solution)/shard_map/broadcast_in_dim | solution.py:289
  4.6 0.6 %collective-permute-done.1 = bf16[8,512]{1,0:T(8,128)(2,1)S(1)} collective-permute-done((bf16[8,512]{1,0:T(8,128)(2,1)}, bf16[8,512]{1,0:T(8,128)(2,1)S(1)}, u32[]{:S(2)}, u32[]{:S(2)}) %collective-permute-start.1) | collective-permute-done | bytes 8224 | tf_op jit(solution)/shard_map/ppermute | solution.py:281
  5.2 0.0 collective-permute-done
  5.2 5.8 %collective-permute-start.4 = (bf16[2,8,640]{2,1,0:T(8,128)(2,1)S(1)}, bf16[2,8,640]{2,1,0:T(8,128)(2,1)S(1)}, u32[]{:S(2)}, u32[]{:S(2)}) collective-permute-start(bf16[2,8,640]{2,1,0:T(8,128)(2,1)S(1)} %pad_maximum_fusion.1), channel_id=1, source_target_pairs={{0,160},{1,161},{2,162},{3,163},{4,164},{5,165},{6,166},{7,167},{8... | collective-permute-start | bytes 61448 | tf_op jit(solution)/shard_map/ppermute | solution.py:281
  11.0 0.3 collective-permute-start.3
  11.3 2.8 %collective-permute-start.2 = (bf16[2,8,640]{2,1,0:T(8,128)(2,1)S(1)}, bf16[2,8,640]{2,1,0:T(8,128)(2,1)S(1)}, u32[]{:S(2)}, u32[]{:S(2)}) collective-permute-start(bf16[2,8,640]{2,1,0:T(8,128)(2,1)S(1)} %pad_maximum_fusion.1), channel_id=1, source_target_pairs={{0,224},{1,225},{2,226},{3,227},{4,228},{5,229},{6,230},{7,231},{8... | collective-permute-start | bytes 61448 | tf_op jit(solution)/shard_map/ppermute | solution.py:281
  14.1 1.4 %collective-permute-done.2 = bf16[2,8,640]{2,1,0:T(8,128)(2,1)S(1)} collective-permute-done((bf16[2,8,640]{2,1,0:T(8,128)(2,1)S(1)}, bf16[2,8,640]{2,1,0:T(8,128)(2,1)S(1)}, u32[]{:S(2)}, u32[]{:S(2)}) %collective-permute-start.2) | collective-permute-done | bytes 20512 | tf_op jit(solution)/shard_map/ppermute | solution.py:281
  15.5 0.0 collective-permute-done.3
  15.5 0.0 collective-permute-done.4
  15.6 1.4 %collective-permute-start.5 = (bf16[8,8,640]{2,1,0:T(8,128)(2,1)S(1)}, bf16[8,8,640]{2,1,0:T(8,128)(2,1)S(1)}, u32[]{:S(2)}, u32[]{:S(2)}) collective-permute-start(bf16[8,8,640]{2,1,0:T(8,128)(2,1)S(1)} %get-tuple-element.23), channel_id=1, source_target_pairs={{0,1},{1,2},{2,3},{3,0},{4,12},{5,13},{6,14},{7,15},{8,9},{9,10},{... | collective-permute-start | bytes 245768 | tf_op jit(solution)/shard_map/ppermute | solution.py:281
  16.9 2.6 %collective-permute-start.7 = (bf16[8,8,640]{2,1,0:T(8,128)(2,1)S(1)}, bf16[8,8,640]{2,1,0:T(8,128)(2,1)S(1)}, u32[]{:S(2)}, u32[]{:S(2)}) collective-permute-start(bf16[8,8,640]{2,1,0:T(8,128)(2,1)S(1)} %get-tuple-element.23), channel_id=1, source_target_pairs={{0,2},{1,3},{2,0},{3,1},{4,20},{5,21},{6,22},{7,23},{8,10},{9,11},... | collective-permute-start | bytes 245768 | tf_op jit(solution)/shard_map/ppermute | solution.py:281
  19.6 1.1 %collective-permute-start.6 = (bf16[8,8,640]{2,1,0:T(8,128)(2,1)S(1)}, bf16[8,8,640]{2,1,0:T(8,128)(2,1)S(1)}, u32[]{:S(2)}, u32[]{:S(2)}) collective-permute-start(bf16[8,8,640]{2,1,0:T(8,128)(2,1)S(1)} %get-tuple-element.23), channel_id=1, source_target_pairs={{0,3},{1,0},{2,1},{3,2},{4,28},{5,29},{6,30},{7,31},{8,11},{9,8},{... | collective-permute-start | bytes 245768 | tf_op jit(solution)/shard_map/ppermute | solution.py:281
  20.6 0.0 collective-permute-done.5
  20.6 2.2 %collective-permute-done.6 = bf16[8,8,640]{2,1,0:T(8,128)(2,1)S(1)} collective-permute-done((bf16[8,8,640]{2,1,0:T(8,128)(2,1)S(1)}, bf16[8,8,640]{2,1,0:T(8,128)(2,1)S(1)}, u32[]{:S(2)}, u32[]{:S(2)}) %collective-permute-start.6) | collective-permute-done | bytes 81952 | tf_op jit(solution)/shard_map/ppermute | solution.py:281
  22.9 0.0 collective-permute-done.7
  22.9 4.9 %collective-permute-start.9 = (bf16[32,8,640]{2,1,0:T(8,128)(2,1)S(1)}, bf16[32,8,640]{2,1,0:T(8,128)(2,1)S(1)}, u32[]{:S(2)}, u32[]{:S(2)}) collective-permute-start(bf16[32,8,640]{2,1,0:T(8,128)(2,1)S(1)} %constant_dynamic-update-slice_fusion.5.refs_0_), channel_id=1, source_target_pairs={{0,4},{1,5},{2,6},{3,7},{4,0},{5,1},{6,2},{7,3},{8,12},{9,13},{10,... | collective-permute-start | bytes 983048 | tf_op jit(solution)/shard_map/ppermute | solution.py:281
  27.8 0.5 collective-permute-start.8
  28.3 2.2 %collective-permute-start.11 = (bf16[32,8,640]{2,1,0:T(8,128)(2,1)S(1)}, bf16[32,8,640]{2,1,0:T(8,128)(2,1)S(1)}, u32[]{:S(2)}, u32[]{:S(2)}) collective-permute-start(bf16[32,8,640]{2,1,0:T(8,128)(2,1)S(1)} %constant_dynamic-update-slice_fusion.5.refs_0_), channel_id=1, source_target_pairs={{0,24},{1,25},{2,26},{3,27},{4,7},{5,4},{6,5},{7,6},{8,0},{9,1},{1... | collective-permute-start | bytes 983048 | tf_op jit(solution)/shard_map/ppermute | solution.py:281
  30.5 0.9 %collective-permute-start.10 = (bf16[32,8,640]{2,1,0:T(8,128)(2,1)S(1)}, bf16[32,8,640]{2,1,0:T(8,128)(2,1)S(1)}, u32[]{:S(2)}, u32[]{:S(2)}) collective-permute-start(bf16[32,8,640]{2,1,0:T(8,128)(2,1)S(1)} %constant_dynamic-update-slice_fusion.5.refs_0_), channel_id=1, source_target_pairs={{0,16},{1,17},{2,18},{3,19},{4,6},{5,7},{6,4},{7,5},{8,24},{9,25},... | collective-permute-start | bytes 983048 | tf_op jit(solution)/shard_map/ppermute | solution.py:281
  31.4 0.0 collective-permute-done.9.refs_4_
  31.4 3.7 %shard_map.73 = (bf16[1024,512]{1,0:T(8,128)(2,1)S(1)}, bf16[1024,512]{1,0:T(8,128)(2,1)S(1)}, f32[10,256,256]{2,1,0:T(8,128)S(1)}) custom-call(s32[4]{0:T(128)} %bitcast.22, f32[12]{0:T(128)} %pos_hbm.1, f32[20]{0:T(128)} %time_hbm.1, bf16[1024,512]{1,0:T(8,128)(2,1)} %tokens_hbm.1, s32[8,128]{1,0:T(8,128)} %bitcast.21), custom_call_target="tpu_custom_call" | custom-call | flops 20000000 | bytes 5000000 | tf_op jit(solution)/shard_map/pallas_call | solution.py:104
  35.1 0.1 collective-permute-done.8.refs_1_
  35.3 2.8 %collective-permute-done.11.refs_3_ = bf16[32,8,640]{2,1,0:T(8,128)(2,1)S(1)} collective-permute-done((bf16[32,8,640]{2,1,0:T(8,128)(2,1)S(1)}, bf16[32,8,640]{2,1,0:T(8,128)(2,1)S(1)}, u32[]{:S(2)}, u32[]{:S(2)}) %collective-permute-start.11) | collective-permute-done | bytes 327712 | tf_op jit(solution)/shard_map/ppermute | solution.py:281
  38.0 0.1 pad_maximum_fusion
  38.1 0.1 collective-permute-start.12
  38.2 1.4 %collective-permute-done.10.refs_2_ = bf16[32,8,640]{2,1,0:T(8,128)(2,1)S(1)} collective-permute-done((bf16[32,8,640]{2,1,0:T(8,128)(2,1)S(1)}, bf16[32,8,640]{2,1,0:T(8,128)(2,1)S(1)}, u32[]{:S(2)}, u32[]{:S(2)}) %collective-permute-start.10) | collective-permute-done | bytes 327712 | tf_op jit(solution)/shard_map/ppermute | solution.py:281
  39.6 1.3 %collective-permute-start.13 = (bf16[32,8,640]{2,1,0:T(8,128)(2,1)S(1)}, bf16[32,8,640]{2,1,0:T(8,128)(2,1)S(1)}, u32[]{:S(2)}, u32[]{:S(2)}) collective-permute-start(bf16[32,8,640]{2,1,0:T(8,128)(2,1)S(1)} %collective-permute-done.10.refs_2_), channel_id=1, source_target_pairs={{0,4},{1,5},{2,6},{3,7},{4,0},{5,1},{6,2},{7,3},{8,12},{9,13},{10,... | collective-permute-start | bytes 983048 | tf_op jit(solution)/shard_map/ppermute | solution.py:281
  41.0 1.3 %collective-permute-done.13.refs_6_ = bf16[32,8,640]{2,1,0:T(8,128)(2,1)S(1)} collective-permute-done((bf16[32,8,640]{2,1,0:T(8,128)(2,1)S(1)}, bf16[32,8,640]{2,1,0:T(8,128)(2,1)S(1)}, u32[]{:S(2)}, u32[]{:S(2)}) %collective-permute-start.13) | collective-permute-done | bytes 327712 | tf_op jit(solution)/shard_map/ppermute | solution.py:281
  42.2 0.0 collective-permute-done.12.refs_5_
  42.2 8.2 %shard_map.74 = bf16[1024,512]{1,0:T(8,128)(2,1)} custom-call(bf16[1024,512]{1,0:T(8,128)(2,1)S(1)} %get-tuple-element.18.tokens, bf16[1024,512]{1,0:T(8,128)(2,1)S(1)} %get-tuple-element.19.normed, f32[10,256,256]{2,1,0:T(8,128)S(1)} %get-tuple-element.20.bias, bf16[32,8,640]{2,1,0:T(8,128)(2,1)S(1)} %constant_dynamic-update-slice_fusion.5.refs_0_, ...), custom_call_target="tpu_custom_call" | custom-call | flops 5000000000 | bytes 9000000 | tf_op jit(solution)/shard_map/pallas_call | solution.py:244
  (10 shorter events, 0.1 us)
Async XLA Ops:
  0.0 5.2 %collective-permute-start = (bf16[8,512]{1,0:T(8,128)(2,1)}, bf16[8,512]{1,0:T(8,128)(2,1)S(1)}, u32[]{:S(2)}, u32[]{:S(2)}) collective-permute-start(bf16[8,512]{1,0:T(8,128)(2,1)} %bitcast.18), channel_id=1, source_target_pairs={{0,32},{1,33},{2,34},{3,35},{4,36},{5,37},{6,38},{7,39},{8,40},{9,... | collective-permute-start | bytes 24584 | tf_op jit(solution)/shard_map/ppermute | solution.py:281
  2.5 2.7 %collective-permute-start.1 = (bf16[8,512]{1,0:T(8,128)(2,1)}, bf16[8,512]{1,0:T(8,128)(2,1)S(1)}, u32[]{:S(2)}, u32[]{:S(2)}) collective-permute-start(bf16[8,512]{1,0:T(8,128)(2,1)} %bitcast.23), channel_id=1, source_target_pairs={{0,32},{1,33},{2,34},{3,35},{4,36},{5,37},{6,38},{7,39},{8,40},{9,... | collective-permute-start | bytes 24584 | tf_op jit(solution)/shard_map/ppermute | solution.py:281
  5.2 10.3 %collective-permute-start.4 = (bf16[2,8,640]{2,1,0:T(8,128)(2,1)S(1)}, bf16[2,8,640]{2,1,0:T(8,128)(2,1)S(1)}, u32[]{:S(2)}, u32[]{:S(2)}) collective-permute-start(bf16[2,8,640]{2,1,0:T(8,128)(2,1)S(1)} %pad_maximum_fusion.1), channel_id=1, source_target_pairs={{0,160},{1,161},{2,162},{3,163},{4,164},{5,165},{6,166},{7,167},{8... | collective-permute-start | bytes 61448 | tf_op jit(solution)/shard_map/ppermute | solution.py:281
  11.0 4.5 %collective-permute-start.3 = (bf16[2,8,640]{2,1,0:T(8,128)(2,1)S(1)}, bf16[2,8,640]{2,1,0:T(8,128)(2,1)S(1)}, u32[]{:S(2)}, u32[]{:S(2)}) collective-permute-start(bf16[2,8,640]{2,1,0:T(8,128)(2,1)S(1)} %pad_maximum_fusion.1), channel_id=1, source_target_pairs={{0,192},{1,193},{2,194},{3,195},{4,196},{5,197},{6,198},{7,199},{8... | collective-permute-start | bytes 61448 | tf_op jit(solution)/shard_map/ppermute | solution.py:281
  11.3 4.2 %collective-permute-start.2 = (bf16[2,8,640]{2,1,0:T(8,128)(2,1)S(1)}, bf16[2,8,640]{2,1,0:T(8,128)(2,1)S(1)}, u32[]{:S(2)}, u32[]{:S(2)}) collective-permute-start(bf16[2,8,640]{2,1,0:T(8,128)(2,1)S(1)} %pad_maximum_fusion.1), channel_id=1, source_target_pairs={{0,224},{1,225},{2,226},{3,227},{4,228},{5,229},{6,230},{7,231},{8... | collective-permute-start | bytes 61448 | tf_op jit(solution)/shard_map/ppermute | solution.py:281
  15.6 5.1 %collective-permute-start.5 = (bf16[8,8,640]{2,1,0:T(8,128)(2,1)S(1)}, bf16[8,8,640]{2,1,0:T(8,128)(2,1)S(1)}, u32[]{:S(2)}, u32[]{:S(2)}) collective-permute-start(bf16[8,8,640]{2,1,0:T(8,128)(2,1)S(1)} %get-tuple-element.23), channel_id=1, source_target_pairs={{0,1},{1,2},{2,3},{3,0},{4,12},{5,13},{6,14},{7,15},{8,9},{9,10},{... | collective-permute-start | bytes 245768 | tf_op jit(solution)/shard_map/ppermute | solution.py:281
  16.9 5.9 %collective-permute-start.7 = (bf16[8,8,640]{2,1,0:T(8,128)(2,1)S(1)}, bf16[8,8,640]{2,1,0:T(8,128)(2,1)S(1)}, u32[]{:S(2)}, u32[]{:S(2)}) collective-permute-start(bf16[8,8,640]{2,1,0:T(8,128)(2,1)S(1)} %get-tuple-element.23), channel_id=1, source_target_pairs={{0,2},{1,3},{2,0},{3,1},{4,20},{5,21},{6,22},{7,23},{8,10},{9,11},... | collective-permute-start | bytes 245768 | tf_op jit(solution)/shard_map/ppermute | solution.py:281
  19.6 3.3 %collective-permute-start.6 = (bf16[8,8,640]{2,1,0:T(8,128)(2,1)S(1)}, bf16[8,8,640]{2,1,0:T(8,128)(2,1)S(1)}, u32[]{:S(2)}, u32[]{:S(2)}) collective-permute-start(bf16[8,8,640]{2,1,0:T(8,128)(2,1)S(1)} %get-tuple-element.23), channel_id=1, source_target_pairs={{0,3},{1,0},{2,1},{3,2},{4,28},{5,29},{6,30},{7,31},{8,11},{9,8},{... | collective-permute-start | bytes 245768 | tf_op jit(solution)/shard_map/ppermute | solution.py:281
  22.9 8.5 %collective-permute-start.9 = (bf16[32,8,640]{2,1,0:T(8,128)(2,1)S(1)}, bf16[32,8,640]{2,1,0:T(8,128)(2,1)S(1)}, u32[]{:S(2)}, u32[]{:S(2)}) collective-permute-start(bf16[32,8,640]{2,1,0:T(8,128)(2,1)S(1)} %constant_dynamic-update-slice_fusion.5.refs_0_), channel_id=1, source_target_pairs={{0,4},{1,5},{2,6},{3,7},{4,0},{5,1},{6,2},{7,3},{8,12},{9,13},{10,... | collective-permute-start | bytes 983048 | tf_op jit(solution)/shard_map/ppermute | solution.py:281
  27.8 7.4 %collective-permute-start.8 = (bf16[32,8,640]{2,1,0:T(8,128)(2,1)S(1)}, bf16[32,8,640]{2,1,0:T(8,128)(2,1)S(1)}, u32[]{:S(2)}, u32[]{:S(2)}) collective-permute-start(bf16[32,8,640]{2,1,0:T(8,128)(2,1)S(1)} %constant_dynamic-update-slice_fusion.5.refs_0_), channel_id=1, source_target_pairs={{0,8},{1,9},{2,10},{3,11},{4,5},{5,6},{6,7},{7,4},{8,16},{9,17},{1... | collective-permute-start | bytes 983048 | tf_op jit(solution)/shard_map/ppermute | solution.py:281
  28.3 9.7 %collective-permute-start.11 = (bf16[32,8,640]{2,1,0:T(8,128)(2,1)S(1)}, bf16[32,8,640]{2,1,0:T(8,128)(2,1)S(1)}, u32[]{:S(2)}, u32[]{:S(2)}) collective-permute-start(bf16[32,8,640]{2,1,0:T(8,128)(2,1)S(1)} %constant_dynamic-update-slice_fusion.5.refs_0_), channel_id=1, source_target_pairs={{0,24},{1,25},{2,26},{3,27},{4,7},{5,4},{6,5},{7,6},{8,0},{9,1},{1... | collective-permute-start | bytes 983048 | tf_op jit(solution)/shard_map/ppermute | solution.py:281
  30.5 9.1 %collective-permute-start.10 = (bf16[32,8,640]{2,1,0:T(8,128)(2,1)S(1)}, bf16[32,8,640]{2,1,0:T(8,128)(2,1)S(1)}, u32[]{:S(2)}, u32[]{:S(2)}) collective-permute-start(bf16[32,8,640]{2,1,0:T(8,128)(2,1)S(1)} %constant_dynamic-update-slice_fusion.5.refs_0_), channel_id=1, source_target_pairs={{0,16},{1,17},{2,18},{3,19},{4,6},{5,7},{6,4},{7,5},{8,24},{9,25},... | collective-permute-start | bytes 983048 | tf_op jit(solution)/shard_map/ppermute | solution.py:281
  38.1 4.1 %collective-permute-start.12 = (bf16[64,8,640]{2,1,0:T(8,128)(2,1)S(1)}, bf16[64,8,640]{2,1,0:T(8,128)(2,1)S(1)}, u32[]{:S(2)}, u32[]{:S(2)}) collective-permute-start(bf16[64,8,640]{2,1,0:T(8,128)(2,1)S(1)} %pad_maximum_fusion), channel_id=1, source_target_pairs={{0,4},{1,5},{2,6},{3,7},{4,0},{5,1},{6,2},{7,3},{8,12},{9,13},{10,... | collective-permute-start | bytes 1966088 | tf_op jit(solution)/shard_map/ppermute | solution.py:281
  39.6 2.6 %collective-permute-start.13 = (bf16[32,8,640]{2,1,0:T(8,128)(2,1)S(1)}, bf16[32,8,640]{2,1,0:T(8,128)(2,1)S(1)}, u32[]{:S(2)}, u32[]{:S(2)}) collective-permute-start(bf16[32,8,640]{2,1,0:T(8,128)(2,1)S(1)} %collective-permute-done.10.refs_2_), channel_id=1, source_target_pairs={{0,4},{1,5},{2,6},{3,7},{4,0},{5,1},{6,2},{7,3},{8,12},{9,13},{10,... | collective-permute-start | bytes 983048 | tf_op jit(solution)/shard_map/ppermute | solution.py:281

commit v6 on v5

--- a/solution.py
+++ b/solution.py
@@ -138,70 +138,67 @@
     return jnp.where(apart == 0, 0, slot)
 
 
+def coordinates():
+    dp = lax.axis_index("dp")
+    return lax.axis_index("group"), lax.rem(dp // 2, 4), dp // 8, lax.rem(dp, 2)
+
+
+def place(source, start, own_core, far, in_weight, out_weight):
+    own_x, own_y, own_z, core = coordinates()
+    core = core if own_core else 1 - core
+    step = jnp.where(lax.rem(own_z, 2) == 1, 1, -1)
+    first, second = jnp.where(core == 0, own_x, own_y), jnp.where(core == 0, own_y, own_x)
+    second = lax.rem(second + 4 - far, 4)
+
+    def line(apart, carry):
+        along = lax.rem(first + 4 - apart, 4)
+        x, y = jnp.where(core == 0, along, second), jnp.where(core == 0, second, along)
+        lanes = pl.ds(pl.multiple_of(x * HEAD_DIM, HEAD_DIM), HEAD_DIM)
+        at = start + line_slot(apart) * 8
+        for slot in range(8):
+            z = lax.rem(own_z + 8 + step * STEPS[slot], 8)
+            piece = source[at + slot]
+            in_weight[z * 32 + y * 8 + core * 4 + x] = piece[:, :D]
+            out_weight[z * 8 + y * 2 + core, :, lanes] = piece[:, D:]
+        return carry
+
+    lax.fori_loop(0, 4, line, 0)
+
+
+def arrange_kernel(own, near, far, last, swapped_own, swapped_near, in_weight, out_weight):
+    for k, source in enumerate((own, near, far, last)):
+        place(source, 0, True, k, in_weight, out_weight)
+    place(swapped_own, 0, False, 0, in_weight, out_weight)
+    place(swapped_near, 0, False, 1, in_weight, out_weight)
+    place(swapped_near, 32, False, 3, in_weight, out_weight)
+
+
+def arrange(planes, swapped_own, swapped_near):
+    vmem = pl.BlockSpec(memory_space=pltpu.VMEM)
+    return pl.pallas_call(
+        arrange_kernel,
+        out_shape=(
+            jax.ShapeDtypeStruct((4 * D // 8, 8, D), jnp.bfloat16),
+            jax.ShapeDtypeStruct((D // 8, 8, D), jnp.bfloat16),
+        ),
+        in_specs=[vmem] * 6,
+        out_specs=(vmem,) * 2,
+        compiler_params=pltpu.CompilerParams(vmem_limit_bytes=VMEM_PREPARE * 2**20),
+        cost_estimate=pl.CostEstimate(flops=10**6, bytes_accessed=10**6, transcendentals=0),
+    )(*planes, swapped_own, swapped_near)
+
+
 def main_kernel(
-    tokens, normed, bias, *refs
+    tokens, normed, bias, swapped_far, in_weight_given, out_weight_given,
+    updated_hbm, in_weight, out_weight, mixed, totals, updated, out_sems,
 ):
-    own_planes, (swapped_own, swapped_near, swapped_far), updated_hbm = refs[:4], refs[4:7], refs[7]
-    planes, in_weight, out_weight, mixed, totals, updated, sems, out_sems = refs[8:]
-    near, last = swapped_near.at[pl.ds(0, 32)], swapped_near.at[pl.ds(32, 32)]
-    sources = [own_planes, (swapped_own, near, swapped_far, last)]
-    dp, own_x = lax.axis_index("dp"), lax.axis_index("group")
-    own_z = dp // 8
-    own_odd = lax.rem(own_z, 2)
-    own_y, own_core = lax.rem(dp // 2, 4), lax.rem(dp, 2)
-
-    def fetch(k, source, target):
-        copy = pltpu.make_async_copy(source, target, sems.at[k])
-        copy.start()
-        return copy
-
-    copies_in = []
-    for side in range(2):
-        core = own_core if side == 0 else 1 - own_core
-        place = jnp.where(core == 0, own_y, own_x)
-        for k in range(4):
-            copies_in.append(
-                fetch(
-                    side * 4 + k,
-                    sources[side][k],
-                    planes.at[core * 4 + lax.rem(place + 4 - k, 4)],
-                )
-            )
-
-    for copy in copies_in:
-        copy.wait()
-
-    def arrange(y, carry):
-        for slot in range(8):
-            z = lax.rem(own_z + 8 + jnp.where(own_odd == 1, STEPS[slot], -STEPS[slot]), 8)
-            pieces = []
-            for core in range(2):
-                for x in range(4):
-                    if core == 0:
-                        plane, line = y, line_slot(own_x + 4 - x)
-                    else:
-                        plane, line = 4 + x, line_slot(own_y + 4 - y)
-                    pieces.append(planes[plane, line * 8 + slot].astype(jnp.float32))
-            start = pl.multiple_of(z * 256 + y * 64, 64)
-            in_weight[pl.ds(start, 64), :] = jnp.concatenate(
-                [piece[:, :D] for piece in pieces]
-            ).astype(jnp.bfloat16)
-            start = pl.multiple_of(z * 64 + y * 16, 16)
-            out_weight[pl.ds(start, 16), :] = jnp.concatenate(
-                [
-                    jnp.concatenate([piece[:, D:] for piece in pieces[c * 4 : c * 4 + 4]], axis=1)
-                    for c in range(2)
-                ]
-            ).astype(jnp.bfloat16)
-        return carry
-
-    lax.fori_loop(0, 4, arrange, 0)
+    place(swapped_far, 0, False, 2, in_weight, out_weight)
     for i in range(ROWS // 256):
         rows = pl.ds(i * 256, 256)
         for part in range(4):
             cols = pl.ds(part * 512, 512)
             product = lax.dot_general(
-                normed[rows, :], in_weight[cols, :], TRANS_B, preferred_element_type=jnp.float32
+                normed[rows, :], in_weight[pl.ds(part * (D // 8), D // 8)].reshape(D, D), TRANS_B, preferred_element_type=jnp.float32
             )
             mixed[rows, cols] = half_silu(product * 0.5).astype(jnp.bfloat16)
     def finish(i):
@@ -210,7 +207,7 @@
         gate = mixed[rows, pl.ds(0, D)].astype(jnp.float32)
         gated = (normalize(attended) * gate).astype(jnp.bfloat16)
         projected = lax.dot_general(
-            gated, out_weight[...], TRANS_B, preferred_element_type=jnp.float32
+            gated, out_weight[...].reshape(D, D), TRANS_B, preferred_element_type=jnp.float32
         )
         updated[rows, :] = (tokens[rows, :].astype(jnp.float32) + projected).astype(jnp.bfloat16)
         copy = pltpu.make_async_copy(updated.at[rows, :], updated_hbm.at[rows, :], out_sems.at[i])
@@ -238,29 +235,30 @@
         copy.wait()
 
 
-def main(tokens, normed, bias, planes):
-    anywhere = pl.BlockSpec(memory_space=pl.ANY)
+def main(tokens, normed, bias, swapped_far, in_weight, out_weight):
     vmem = pl.BlockSpec(memory_space=pltpu.VMEM)
-    return pl.pallas_call(
+    updated, _, _ = pl.pallas_call(
         main_kernel,
-        out_shape=jax.ShapeDtypeStruct((ROWS, D), jnp.bfloat16),
-        in_specs=[vmem] * 3 + [anywhere] * 7,
-        out_specs=anywhere,
+        out_shape=(
+            jax.ShapeDtypeStruct((ROWS, D), jnp.bfloat16),
+            jax.ShapeDtypeStruct(in_weight.shape, jnp.bfloat16),
+            jax.ShapeDtypeStruct(out_weight.shape, jnp.bfloat16),
+        ),
+        in_specs=[vmem] * 6,
+        out_specs=(pl.BlockSpec(memory_space=pl.ANY), vmem, vmem),
+        input_output_aliases={4: 1, 5: 2},
         scratch_shapes=[
-            pltpu.VMEM((8, 32, 8, D + HEAD_DIM), jnp.bfloat16),
-            pltpu.VMEM((4 * D, D), jnp.bfloat16),
-            pltpu.VMEM((D, D), jnp.bfloat16),
             pltpu.VMEM((ROWS, 4 * D), jnp.bfloat16),
             pltpu.VMEM((ROWS, D), jnp.float32),
             pltpu.VMEM((ROWS, D), jnp.bfloat16),
-            pltpu.SemaphoreType.DMA((8,)),
             pltpu.SemaphoreType.DMA((ROWS // BLOCK,)),
         ],
         compiler_params=pltpu.CompilerParams(vmem_limit_bytes=VMEM_MAIN * 2**20),
         cost_estimate=pl.CostEstimate(
             flops=5 * 10**9, bytes_accessed=9 * 10**6, transcendentals=4 * 10**6
         ),
-    )(tokens, normed, bias, *planes)
+    )(tokens, normed, bias, swapped_far, in_weight, out_weight)
+    return updated
 
 
 def device_of(x, y, z, core):
@@ -323,8 +321,9 @@
     swapped_own, stamps = lax.optimization_barrier((swapped_own, stamps))
     prepared = prepare(own_lengths, pos_table, time_table, tokens, stamps.reshape(8, TILE))
     planes[1], prepared = lax.optimization_barrier((planes[1], prepared))
+    planes[2], prepared = lax.optimization_barrier((planes[2], prepared))
     swapped_near = swap(jnp.concatenate([planes[1], planes[3]]))
-    return main(*prepared, [*planes, swapped_own, swapped_near, swap(planes[2])])
+    return main(*prepared, swap(planes[2]), *arrange(planes, swapped_own, swapped_near))
 
 
 def solution(mesh):

time: 50.8 us -> 49.9 us (0.982)
  waiting for transfers between devices: 9.75 us -> 8.5 us
    ppermute x14, waiting for transfers between devices: 9.75 us -> 8.5 us  [send(): return lax.ppermute(array, ('dp', 'group'), moves(step))]
    pallas_call x1 -> x2, Pallas kernels: 8.19 us -> 8.48 us  [the longest x1 7.15 us: main(): pl.pallas_call(main_kernel, out_shape=(jax.ShapeDtypeStruct((ROWS, D), jn...]
  transfers between devices with their start and end apart: 14 -> 14, of which waited for: 7 -> 6; matrix products, arithmetic and copies ran while one was open for 4% -> 5% of each run, Pallas kernels for 7% -> 10%
where the time goes in v6:
time: 49.9 us; the launch traced here: 49.6 us
  starting transfers between devices  26.4 us (53%)
  Pallas kernels  12.2 us (24%)
  waiting for transfers between devices  8.5 us (17%)
  other arithmetic  1.49 us (3%)
  local copies, waits for them, and re-layouts  0.79 us (2%)
    ppermute x14, starting transfers between devices, send(): return lax.ppermute(array, ('dp', 'group'), moves(step))  26.4 us
    ppermute x14, waiting for transfers between devices, send(): return lax.ppermute(array, ('dp', 'group'), moves(step))  8.5 us
    pallas_call x1, Pallas kernels, main(): pl.pallas_call(main_kernel, out_shape=(jax.ShapeDtypeStruct((ROWS, D), jn...  7.15 us
    pallas_call x1, Pallas kernels, prepare(): pl.pallas_call(prepare_kernel, out_shape=(jax.ShapeDtypeStruct((ROWS, D),...  3.75 us
    pallas_call x1, Pallas kernels, arrange(): pl.pallas_call(arrange_kernel, out_shape=(jax.ShapeDtypeStruct((4 * D //...  1.33 us
  transfers between devices with their start and end apart: 14, of which 6 were waited for; matrix products, arithmetic and copies ran while one was open for 5% of the time, Pallas kernels for 10%

profile of v6, /device:TPU:1, one launch (start us, length us, event | category | flops | bytes accessed | tf_op | source)
XLA Modules:
  0.0 49.6 jit_solution(4884819002762884240)
XLA Ops:
  0.0 2.5 %collective-permute-start = (bf16[8,512]{1,0:T(8,128)(2,1)}, bf16[8,512]{1,0:T(8,128)(2,1)S(1)}, u32[]{:S(2)}, u32[]{:S(2)}) collective-permute-start(bf16[8,512]{1,0:T(8,128)(2,1)} %bitcast.18), channel_id=1, source_target_pairs={{0,32},{1,33},{2,34},{3,35},{4,36},{5,37},{6,38},{7,39},{8,40},{9,... | collective-permute-start | bytes 24584 | tf_op jit(solution)/shard_map/ppermute | solution.py:279
  2.5 0.0 collective-permute-start.1
  2.5 0.7 %dynamic-slice_bitcast_fusion = bf16[8,128]{1,0:T(8,128)(2,1)S(1)} fusion(bf16[512,8]{0,1:T(8,128)(2,1)} %param.11, s32[]{:T(128)S(6)} %select_n.4), kind=kLoop, calls=%fused_computation.17 | loop fusion | bytes 4100 | tf_op jit(solution)/shard_map/dynamic_slice | solution.py:286
  3.2 0.7 %constant_dynamic-update-slice_fusion.4 = (bf16[8,8,640]{2,1,0:T(8,128)(2,1)S(1)}, bf16[32,8,640]{2,1,0:T(8,128)(2,1)S(1)}) fusion(bf16[8,128]{1,0:T(8,128)(2,1)S(1)} %dynamic-slice_bitcast_fusion, bf16[8,512]{1,0:T(8,128)(2,1)} %bitcast.19), kind=kLoop, calls=%fused_computation.5 | loop fusion | flops 20478 | bytes 30720
  3.9 0.7 %maximum_bitcast_fusion = bf16[1,8,640]{2,1,0:T(8,128)(2,1)S(1)} fusion(bf16[8,128]{1,0:T(8,128)(2,1)S(1)} %dynamic-slice_bitcast_fusion, bf16[8,512]{1,0:T(8,128)(2,1)} %bitcast.20), kind=kLoop, calls=%fused_computation.15 | loop fusion | flops 20480 | bytes 20480 | tf_op jit(solution)/shard_map/broadcast_in_dim | solution.py:287
  4.6 0.6 %collective-permute-done.1 = bf16[8,512]{1,0:T(8,128)(2,1)S(1)} collective-permute-done((bf16[8,512]{1,0:T(8,128)(2,1)}, bf16[8,512]{1,0:T(8,128)(2,1)S(1)}, u32[]{:S(2)}, u32[]{:S(2)}) %collective-permute-start.1) | collective-permute-done | bytes 8224 | tf_op jit(solution)/shard_map/ppermute | solution.py:279
  5.2 0.0 collective-permute-done
  5.2 5.8 %collective-permute-start.4 = (bf16[2,8,640]{2,1,0:T(8,128)(2,1)S(1)}, bf16[2,8,640]{2,1,0:T(8,128)(2,1)S(1)}, u32[]{:S(2)}, u32[]{:S(2)}) collective-permute-start(bf16[2,8,640]{2,1,0:T(8,128)(2,1)S(1)} %pad_maximum_fusion.1), channel_id=1, source_target_pairs={{0,160},{1,161},{2,162},{3,163},{4,164},{5,165},{6,166},{7,167},{8... | collective-permute-start | bytes 61448 | tf_op jit(solution)/shard_map/ppermute | solution.py:279
  11.0 0.3 collective-permute-start.3
  11.3 2.8 %collective-permute-start.2 = (bf16[2,8,640]{2,1,0:T(8,128)(2,1)S(1)}, bf16[2,8,640]{2,1,0:T(8,128)(2,1)S(1)}, u32[]{:S(2)}, u32[]{:S(2)}) collective-permute-start(bf16[2,8,640]{2,1,0:T(8,128)(2,1)S(1)} %pad_maximum_fusion.1), channel_id=1, source_target_pairs={{0,224},{1,225},{2,226},{3,227},{4,228},{5,229},{6,230},{7,231},{8... | collective-permute-start | bytes 61448 | tf_op jit(solution)/shard_map/ppermute | solution.py:279
  14.1 1.4 %collective-permute-done.2 = bf16[2,8,640]{2,1,0:T(8,128)(2,1)S(1)} collective-permute-done((bf16[2,8,640]{2,1,0:T(8,128)(2,1)S(1)}, bf16[2,8,640]{2,1,0:T(8,128)(2,1)S(1)}, u32[]{:S(2)}, u32[]{:S(2)}) %collective-permute-start.2) | collective-permute-done | bytes 20512 | tf_op jit(solution)/shard_map/ppermute | solution.py:279
  15.5 0.0 collective-permute-done.3
  15.5 0.0 collective-permute-done.4
  15.6 1.4 %collective-permute-start.5 = (bf16[8,8,640]{2,1,0:T(8,128)(2,1)S(1)}, bf16[8,8,640]{2,1,0:T(8,128)(2,1)S(1)}, u32[]{:S(2)}, u32[]{:S(2)}) collective-permute-start(bf16[8,8,640]{2,1,0:T(8,128)(2,1)S(1)} %get-tuple-element.37), channel_id=1, source_target_pairs={{0,1},{1,2},{2,3},{3,0},{4,12},{5,13},{6,14},{7,15},{8,9},{9,10},{... | collective-permute-start | bytes 245768 | tf_op jit(solution)/shard_map/ppermute | solution.py:279
  16.9 2.6 %collective-permute-start.7 = (bf16[8,8,640]{2,1,0:T(8,128)(2,1)S(1)}, bf16[8,8,640]{2,1,0:T(8,128)(2,1)S(1)}, u32[]{:S(2)}, u32[]{:S(2)}) collective-permute-start(bf16[8,8,640]{2,1,0:T(8,128)(2,1)S(1)} %get-tuple-element.37), channel_id=1, source_target_pairs={{0,2},{1,3},{2,0},{3,1},{4,20},{5,21},{6,22},{7,23},{8,10},{9,11},... | collective-permute-start | bytes 245768 | tf_op jit(solution)/shard_map/ppermute | solution.py:279
  19.6 1.1 %collective-permute-start.6 = (bf16[8,8,640]{2,1,0:T(8,128)(2,1)S(1)}, bf16[8,8,640]{2,1,0:T(8,128)(2,1)S(1)}, u32[]{:S(2)}, u32[]{:S(2)}) collective-permute-start(bf16[8,8,640]{2,1,0:T(8,128)(2,1)S(1)} %get-tuple-element.37), channel_id=1, source_target_pairs={{0,3},{1,0},{2,1},{3,2},{4,28},{5,29},{6,30},{7,31},{8,11},{9,8},{... | collective-permute-start | bytes 245768 | tf_op jit(solution)/shard_map/ppermute | solution.py:279
  20.6 0.0 collective-permute-done.5
  20.6 2.2 %collective-permute-done.6 = bf16[8,8,640]{2,1,0:T(8,128)(2,1)S(1)} collective-permute-done((bf16[8,8,640]{2,1,0:T(8,128)(2,1)S(1)}, bf16[8,8,640]{2,1,0:T(8,128)(2,1)S(1)}, u32[]{:S(2)}, u32[]{:S(2)}) %collective-permute-start.6) | collective-permute-done | bytes 81952 | tf_op jit(solution)/shard_map/ppermute | solution.py:279
  22.9 0.0 collective-permute-done.7
  22.9 4.9 %collective-permute-start.10 = (bf16[32,8,640]{2,1,0:T(8,128)(2,1)S(1)}, bf16[32,8,640]{2,1,0:T(8,128)(2,1)S(1)}, u32[]{:S(2)}, u32[]{:S(2)}) collective-permute-start(bf16[32,8,640]{2,1,0:T(8,128)(2,1)S(1)} %constant_dynamic-update-slice_fusion.5.own), channel_id=1, source_target_pairs={{0,4},{1,5},{2,6},{3,7},{4,0},{5,1},{6,2},{7,3},{8,12},{9,13},{10,... | collective-permute-start | bytes 983048 | tf_op jit(solution)/shard_map/ppermute | solution.py:279
  27.8 0.5 collective-permute-start.9
  28.3 2.2 %collective-permute-start.12 = (bf16[32,8,640]{2,1,0:T(8,128)(2,1)S(1)}, bf16[32,8,640]{2,1,0:T(8,128)(2,1)S(1)}, u32[]{:S(2)}, u32[]{:S(2)}) collective-permute-start(bf16[32,8,640]{2,1,0:T(8,128)(2,1)S(1)} %constant_dynamic-update-slice_fusion.5.own), channel_id=1, source_target_pairs={{0,24},{1,25},{2,26},{3,27},{4,7},{5,4},{6,5},{7,6},{8,0},{9,1},{1... | collective-permute-start | bytes 983048 | tf_op jit(solution)/shard_map/ppermute | solution.py:279
  30.5 0.9 %collective-permute-start.8 = (bf16[32,8,640]{2,1,0:T(8,128)(2,1)S(1)}, bf16[32,8,640]{2,1,0:T(8,128)(2,1)S(1)}, u32[]{:S(2)}, u32[]{:S(2)}) collective-permute-start(bf16[32,8,640]{2,1,0:T(8,128)(2,1)S(1)} %constant_dynamic-update-slice_fusion.5.own), channel_id=1, source_target_pairs={{0,16},{1,17},{2,18},{3,19},{4,6},{5,7},{6,4},{7,5},{8,24},{9,25},... | collective-permute-start | bytes 983048 | tf_op jit(solution)/shard_map/ppermute | solution.py:279
  31.4 0.0 collective-permute-done.10.swapped_own
  31.4 3.7 %shard_map.73 = (bf16[1024,512]{1,0:T(8,128)(2,1)S(1)}, bf16[1024,512]{1,0:T(8,128)(2,1)S(1)}, f32[10,256,256]{2,1,0:T(8,128)S(1)}) custom-call(s32[4]{0:T(128)} %bitcast.22, f32[12]{0:T(128)} %pos_hbm.1, f32[20]{0:T(128)} %time_hbm.1, bf16[1024,512]{1,0:T(8,128)(2,1)} %tokens_hbm.1, s32[8,128]{1,0:T(8,128)} %bitcast.21), custom_call_target="tpu_custom_call" | custom-call | flops 20000000 | bytes 5000000 | tf_op jit(solution)/shard_map/pallas_call | solution.py:104
  35.1 0.1 collective-permute-done.9.near
  35.3 2.8 %collective-permute-done.12.last = bf16[32,8,640]{2,1,0:T(8,128)(2,1)S(1)} collective-permute-done((bf16[32,8,640]{2,1,0:T(8,128)(2,1)S(1)}, bf16[32,8,640]{2,1,0:T(8,128)(2,1)S(1)}, u32[]{:S(2)}, u32[]{:S(2)}) %collective-permute-start.12) | collective-permute-done | bytes 327712 | tf_op jit(solution)/shard_map/ppermute | solution.py:279
  38.0 0.1 pad_maximum_fusion
  38.1 0.1 collective-permute-start.13
  38.2 1.4 %collective-permute-done.8.far = bf16[32,8,640]{2,1,0:T(8,128)(2,1)S(1)} collective-permute-done((bf16[32,8,640]{2,1,0:T(8,128)(2,1)S(1)}, bf16[32,8,640]{2,1,0:T(8,128)(2,1)S(1)}, u32[]{:S(2)}, u32[]{:S(2)}) %collective-permute-start.8) | collective-permute-done | bytes 327712 | tf_op jit(solution)/shard_map/ppermute | solution.py:279
  39.6 1.3 %collective-permute-start.11 = (bf16[32,8,640]{2,1,0:T(8,128)(2,1)S(1)}, bf16[32,8,640]{2,1,0:T(8,128)(2,1)S(1)}, u32[]{:S(2)}, u32[]{:S(2)}) collective-permute-start(bf16[32,8,640]{2,1,0:T(8,128)(2,1)S(1)} %collective-permute-done.8.far), channel_id=1, source_target_pairs={{0,4},{1,5},{2,6},{3,7},{4,0},{5,1},{6,2},{7,3},{8,12},{9,13},{10,... | collective-permute-start | bytes 983048 | tf_op jit(solution)/shard_map/ppermute | solution.py:279
  41.0 0.0 collective-permute-done.13.swapped_near
  41.0 1.3 %shard_map.74 = (bf16[256,8,512]{2,1,0:T(8,128)(2,1)S(1)}, bf16[64,8,512]{2,1,0:T(8,128)(2,1)S(1)}) custom-call(bf16[32,8,640]{2,1,0:T(8,128)(2,1)S(1)} %constant_dynamic-update-slice_fusion.5.own, bf16[32,8,640]{2,1,0:T(8,128)(2,1)S(1)} %collective-permute-done.9.near, bf16[32,8,640]{2,1,0:T(8,128)(2,1)S(1)} %collective-permute-done.8.far, ...), custom_call_target="tpu_custom_call" | custom-call | flops 1000000 | bytes 1000000 | tf_op jit(solution)/shard_map/pallas_call | solution.py:178
  42.3 0.0 collective-permute-done.11.swapped_far
  42.3 7.2 %shard_map.75 = (bf16[1024,512]{1,0:T(8,128)(2,1)}, bf16[256,8,512]{2,1,0:T(8,128)(2,1)S(1)}, bf16[64,8,512]{2,1,0:T(8,128)(2,1)S(1)}) custom-call(bf16[1024,512]{1,0:T(8,128)(2,1)S(1)} %get-tuple-element.28.tokens, bf16[1024,512]{1,0:T(8,128)(2,1)S(1)} %get-tuple-element.29.normed, ...), custom_call_target="tpu_custom_call", output_to_operand_aliasing={{1}: (4, {}), {2}: (5, {})} | custom-call | flops 5000000000 | bytes 9000000 | tf_op jit(solution)/shard_map/pallas_call | solution.py:240
  (10 shorter events, 0.1 us)
Async XLA Ops:
  0.0 5.2 %collective-permute-start = (bf16[8,512]{1,0:T(8,128)(2,1)}, bf16[8,512]{1,0:T(8,128)(2,1)S(1)}, u32[]{:S(2)}, u32[]{:S(2)}) collective-permute-start(bf16[8,512]{1,0:T(8,128)(2,1)} %bitcast.18), channel_id=1, source_target_pairs={{0,32},{1,33},{2,34},{3,35},{4,36},{5,37},{6,38},{7,39},{8,40},{9,... | collective-permute-start | bytes 24584 | tf_op jit(solution)/shard_map/ppermute | solution.py:279
  2.5 2.7 %collective-permute-start.1 = (bf16[8,512]{1,0:T(8,128)(2,1)}, bf16[8,512]{1,0:T(8,128)(2,1)S(1)}, u32[]{:S(2)}, u32[]{:S(2)}) collective-permute-start(bf16[8,512]{1,0:T(8,128)(2,1)} %bitcast.23), channel_id=1, source_target_pairs={{0,32},{1,33},{2,34},{3,35},{4,36},{5,37},{6,38},{7,39},{8,40},{9,... | collective-permute-start | bytes 24584 | tf_op jit(solution)/shard_map/ppermute | solution.py:279
  5.2 10.3 %collective-permute-start.4 = (bf16[2,8,640]{2,1,0:T(8,128)(2,1)S(1)}, bf16[2,8,640]{2,1,0:T(8,128)(2,1)S(1)}, u32[]{:S(2)}, u32[]{:S(2)}) collective-permute-start(bf16[2,8,640]{2,1,0:T(8,128)(2,1)S(1)} %pad_maximum_fusion.1), channel_id=1, source_target_pairs={{0,160},{1,161},{2,162},{3,163},{4,164},{5,165},{6,166},{7,167},{8... | collective-permute-start | bytes 61448 | tf_op jit(solution)/shard_map/ppermute | solution.py:279
  11.0 4.5 %collective-permute-start.3 = (bf16[2,8,640]{2,1,0:T(8,128)(2,1)S(1)}, bf16[2,8,640]{2,1,0:T(8,128)(2,1)S(1)}, u32[]{:S(2)}, u32[]{:S(2)}) collective-permute-start(bf16[2,8,640]{2,1,0:T(8,128)(2,1)S(1)} %pad_maximum_fusion.1), channel_id=1, source_target_pairs={{0,192},{1,193},{2,194},{3,195},{4,196},{5,197},{6,198},{7,199},{8... | collective-permute-start | bytes 61448 | tf_op jit(solution)/shard_map/ppermute | solution.py:279
  11.3 4.2 %collective-permute-start.2 = (bf16[2,8,640]{2,1,0:T(8,128)(2,1)S(1)}, bf16[2,8,640]{2,1,0:T(8,128)(2,1)S(1)}, u32[]{:S(2)}, u32[]{:S(2)}) collective-permute-start(bf16[2,8,640]{2,1,0:T(8,128)(2,1)S(1)} %pad_maximum_fusion.1), channel_id=1, source_target_pairs={{0,224},{1,225},{2,226},{3,227},{4,228},{5,229},{6,230},{7,231},{8... | collective-permute-start | bytes 61448 | tf_op jit(solution)/shard_map/ppermute | solution.py:279
  15.6 5.1 %collective-permute-start.5 = (bf16[8,8,640]{2,1,0:T(8,128)(2,1)S(1)}, bf16[8,8,640]{2,1,0:T(8,128)(2,1)S(1)}, u32[]{:S(2)}, u32[]{:S(2)}) collective-permute-start(bf16[8,8,640]{2,1,0:T(8,128)(2,1)S(1)} %get-tuple-element.37), channel_id=1, source_target_pairs={{0,1},{1,2},{2,3},{3,0},{4,12},{5,13},{6,14},{7,15},{8,9},{9,10},{... | collective-permute-start | bytes 245768 | tf_op jit(solution)/shard_map/ppermute | solution.py:279
  16.9 5.9 %collective-permute-start.7 = (bf16[8,8,640]{2,1,0:T(8,128)(2,1)S(1)}, bf16[8,8,640]{2,1,0:T(8,128)(2,1)S(1)}, u32[]{:S(2)}, u32[]{:S(2)}) collective-permute-start(bf16[8,8,640]{2,1,0:T(8,128)(2,1)S(1)} %get-tuple-element.37), channel_id=1, source_target_pairs={{0,2},{1,3},{2,0},{3,1},{4,20},{5,21},{6,22},{7,23},{8,10},{9,11},... | collective-permute-start | bytes 245768 | tf_op jit(solution)/shard_map/ppermute | solution.py:279
  19.6 3.3 %collective-permute-start.6 = (bf16[8,8,640]{2,1,0:T(8,128)(2,1)S(1)}, bf16[8,8,640]{2,1,0:T(8,128)(2,1)S(1)}, u32[]{:S(2)}, u32[]{:S(2)}) collective-permute-start(bf16[8,8,640]{2,1,0:T(8,128)(2,1)S(1)} %get-tuple-element.37), channel_id=1, source_target_pairs={{0,3},{1,0},{2,1},{3,2},{4,28},{5,29},{6,30},{7,31},{8,11},{9,8},{... | collective-permute-start | bytes 245768 | tf_op jit(solution)/shard_map/ppermute | solution.py:279
  22.9 8.5 %collective-permute-start.10 = (bf16[32,8,640]{2,1,0:T(8,128)(2,1)S(1)}, bf16[32,8,640]{2,1,0:T(8,128)(2,1)S(1)}, u32[]{:S(2)}, u32[]{:S(2)}) collective-permute-start(bf16[32,8,640]{2,1,0:T(8,128)(2,1)S(1)} %constant_dynamic-update-slice_fusion.5.own), channel_id=1, source_target_pairs={{0,4},{1,5},{2,6},{3,7},{4,0},{5,1},{6,2},{7,3},{8,12},{9,13},{10,... | collective-permute-start | bytes 983048 | tf_op jit(solution)/shard_map/ppermute | solution.py:279
  27.8 7.4 %collective-permute-start.9 = (bf16[32,8,640]{2,1,0:T(8,128)(2,1)S(1)}, bf16[32,8,640]{2,1,0:T(8,128)(2,1)S(1)}, u32[]{:S(2)}, u32[]{:S(2)}) collective-permute-start(bf16[32,8,640]{2,1,0:T(8,128)(2,1)S(1)} %constant_dynamic-update-slice_fusion.5.own), channel_id=1, source_target_pairs={{0,8},{1,9},{2,10},{3,11},{4,5},{5,6},{6,7},{7,4},{8,16},{9,17},{1... | collective-permute-start | bytes 983048 | tf_op jit(solution)/shard_map/ppermute | solution.py:279
  28.3 9.7 %collective-permute-start.12 = (bf16[32,8,640]{2,1,0:T(8,128)(2,1)S(1)}, bf16[32,8,640]{2,1,0:T(8,128)(2,1)S(1)}, u32[]{:S(2)}, u32[]{:S(2)}) collective-permute-start(bf16[32,8,640]{2,1,0:T(8,128)(2,1)S(1)} %constant_dynamic-update-slice_fusion.5.own), channel_id=1, source_target_pairs={{0,24},{1,25},{2,26},{3,27},{4,7},{5,4},{6,5},{7,6},{8,0},{9,1},{1... | collective-permute-start | bytes 983048 | tf_op jit(solution)/shard_map/ppermute | solution.py:279
  30.5 9.1 %collective-permute-start.8 = (bf16[32,8,640]{2,1,0:T(8,128)(2,1)S(1)}, bf16[32,8,640]{2,1,0:T(8,128)(2,1)S(1)}, u32[]{:S(2)}, u32[]{:S(2)}) collective-permute-start(bf16[32,8,640]{2,1,0:T(8,128)(2,1)S(1)} %constant_dynamic-update-slice_fusion.5.own), channel_id=1, source_target_pairs={{0,16},{1,17},{2,18},{3,19},{4,6},{5,7},{6,4},{7,5},{8,24},{9,25},... | collective-permute-start | bytes 983048 | tf_op jit(solution)/shard_map/ppermute | solution.py:279
  38.1 2.8 %collective-permute-start.13 = (bf16[64,8,640]{2,1,0:T(8,128)(2,1)S(1)}, bf16[64,8,640]{2,1,0:T(8,128)(2,1)S(1)}, u32[]{:S(2)}, u32[]{:S(2)}) collective-permute-start(bf16[64,8,640]{2,1,0:T(8,128)(2,1)S(1)} %pad_maximum_fusion), channel_id=1, source_target_pairs={{0,4},{1,5},{2,6},{3,7},{4,0},{5,1},{6,2},{7,3},{8,12},{9,13},{10,... | collective-permute-start | bytes 1966088 | tf_op jit(solution)/shard_map/ppermute | solution.py:279
  39.6 2.7 %collective-permute-start.11 = (bf16[32,8,640]{2,1,0:T(8,128)(2,1)S(1)}, bf16[32,8,640]{2,1,0:T(8,128)(2,1)S(1)}, u32[]{:S(2)}, u32[]{:S(2)}) collective-permute-start(bf16[32,8,640]{2,1,0:T(8,128)(2,1)S(1)} %collective-permute-done.8.far), channel_id=1, source_target_pairs={{0,4},{1,5},{2,6},{3,7},{4,0},{5,1},{6,2},{7,3},{8,12},{9,13},{10,... | collective-permute-start | bytes 983048 | tf_op jit(solution)/shard_map/ppermute | solution.py:279

commit v7 on v6

--- a/solution.py
+++ b/solution.py
@@ -201,8 +201,8 @@
                 normed[rows, :], in_weight[pl.ds(part * (D // 8), D // 8)].reshape(D, D), TRANS_B, preferred_element_type=jnp.float32
             )
             mixed[rows, cols] = half_silu(product * 0.5).astype(jnp.bfloat16)
-    def finish(i):
-        rows = pl.ds(i * BLOCK, BLOCK)
+    def finish(at, first, count):
+        rows = pl.ds(first, count)
         attended = totals[rows, :].astype(jnp.bfloat16).astype(jnp.float32)
         gate = mixed[rows, pl.ds(0, D)].astype(jnp.float32)
         gated = (normalize(attended) * gate).astype(jnp.bfloat16)
@@ -210,7 +210,7 @@
             gated, out_weight[...].reshape(D, D), TRANS_B, preferred_element_type=jnp.float32
         )
         updated[rows, :] = (tokens[rows, :].astype(jnp.float32) + projected).astype(jnp.bfloat16)
-        copy = pltpu.make_async_copy(updated.at[rows, :], updated_hbm.at[rows, :], out_sems.at[i])
+        copy = pltpu.make_async_copy(updated.at[rows, :], updated_hbm.at[rows, :], out_sems.at[at])
         copy.start()
         sends.append(copy)
 
@@ -229,8 +229,8 @@
             product = jnp.dot(weights, mixed[keys, cols[1]], preferred_element_type=jnp.float32)
             own = pl.ds(head * HEAD_DIM, HEAD_DIM)
             totals[rows, own] = product if j == 0 else totals[rows, own] + product
-    for i in range(ROWS // BLOCK):
-        finish(i)
+    for at, (first, count) in enumerate(((0, 512), (512, 256), (768, 256))):
+        finish(at, first, count)
     for copy in sends:
         copy.wait()
 
@@ -251,7 +251,7 @@
             pltpu.VMEM((ROWS, 4 * D), jnp.bfloat16),
             pltpu.VMEM((ROWS, D), jnp.float32),
             pltpu.VMEM((ROWS, D), jnp.bfloat16),
-            pltpu.SemaphoreType.DMA((ROWS // BLOCK,)),
+            pltpu.SemaphoreType.DMA((3,)),
         ],
         compiler_params=pltpu.CompilerParams(vmem_limit_bytes=VMEM_MAIN * 2**20),
         cost_estimate=pl.CostEstimate(

time: 49.9 us -> 49.9 us (level)
  no operation moved by 1% of the time
where the time goes in v7:
time: 49.9 us; the launch traced here: 49.6 us
  starting transfers between devices  26.4 us (53%)
  Pallas kernels  12.2 us (24%)
  waiting for transfers between devices  8.5 us (17%)
  other arithmetic  1.49 us (3%)
  local copies, waits for them, and re-layouts  0.79 us (2%)
    ppermute x14, starting transfers between devices, send(): return lax.ppermute(array, ('dp', 'group'), moves(step))  26.4 us
    ppermute x14, waiting for transfers between devices, send(): return lax.ppermute(array, ('dp', 'group'), moves(step))  8.5 us
    pallas_call x1, Pallas kernels, main(): pl.pallas_call(main_kernel, out_shape=(jax.ShapeDtypeStruct((ROWS, D), jn...  7.17 us
    pallas_call x1, Pallas kernels, prepare(): pl.pallas_call(prepare_kernel, out_shape=(jax.ShapeDtypeStruct((ROWS, D),...  3.75 us
    pallas_call x1, Pallas kernels, arrange(): pl.pallas_call(arrange_kernel, out_shape=(jax.ShapeDtypeStruct((4 * D //...  1.33 us
  transfers between devices with their start and end apart: 14, of which 6 were waited for; matrix products, arithmetic and copies ran while one was open for 5% of the time, Pallas kernels for 10%

profile of v7, /device:TPU:1, one launch (start us, length us, event | category | flops | bytes accessed | tf_op | source)
XLA Modules:
  0.0 49.6 jit_solution(1465010464951606872)
XLA Ops:
  0.0 2.5 %collective-permute-start = (bf16[8,512]{1,0:T(8,128)(2,1)}, bf16[8,512]{1,0:T(8,128)(2,1)S(1)}, u32[]{:S(2)}, u32[]{:S(2)}) collective-permute-start(bf16[8,512]{1,0:T(8,128)(2,1)} %bitcast.18), channel_id=1, source_target_pairs={{0,32},{1,33},{2,34},{3,35},{4,36},{5,37},{6,38},{7,39},{8,40},{9,... | collective-permute-start | bytes 24584 | tf_op jit(solution)/shard_map/ppermute | solution.py:279
  2.5 0.0 collective-permute-start.1
  2.5 0.7 %dynamic-slice_bitcast_fusion = bf16[8,128]{1,0:T(8,128)(2,1)S(1)} fusion(bf16[512,8]{0,1:T(8,128)(2,1)} %param.11, s32[]{:T(128)S(6)} %select_n.4), kind=kLoop, calls=%fused_computation.17 | loop fusion | bytes 4100 | tf_op jit(solution)/shard_map/dynamic_slice | solution.py:286
  3.2 0.7 %constant_dynamic-update-slice_fusion.4 = (bf16[8,8,640]{2,1,0:T(8,128)(2,1)S(1)}, bf16[32,8,640]{2,1,0:T(8,128)(2,1)S(1)}) fusion(bf16[8,128]{1,0:T(8,128)(2,1)S(1)} %dynamic-slice_bitcast_fusion, bf16[8,512]{1,0:T(8,128)(2,1)} %bitcast.19), kind=kLoop, calls=%fused_computation.5 | loop fusion | flops 20478 | bytes 30720
  3.9 0.7 %maximum_bitcast_fusion = bf16[1,8,640]{2,1,0:T(8,128)(2,1)S(1)} fusion(bf16[8,128]{1,0:T(8,128)(2,1)S(1)} %dynamic-slice_bitcast_fusion, bf16[8,512]{1,0:T(8,128)(2,1)} %bitcast.20), kind=kLoop, calls=%fused_computation.15 | loop fusion | flops 20480 | bytes 20480 | tf_op jit(solution)/shard_map/broadcast_in_dim | solution.py:287
  4.6 0.6 %collective-permute-done.1 = bf16[8,512]{1,0:T(8,128)(2,1)S(1)} collective-permute-done((bf16[8,512]{1,0:T(8,128)(2,1)}, bf16[8,512]{1,0:T(8,128)(2,1)S(1)}, u32[]{:S(2)}, u32[]{:S(2)}) %collective-permute-start.1) | collective-permute-done | bytes 8224 | tf_op jit(solution)/shard_map/ppermute | solution.py:279
  5.2 0.0 collective-permute-done
  5.2 5.8 %collective-permute-start.4 = (bf16[2,8,640]{2,1,0:T(8,128)(2,1)S(1)}, bf16[2,8,640]{2,1,0:T(8,128)(2,1)S(1)}, u32[]{:S(2)}, u32[]{:S(2)}) collective-permute-start(bf16[2,8,640]{2,1,0:T(8,128)(2,1)S(1)} %pad_maximum_fusion.1), channel_id=1, source_target_pairs={{0,160},{1,161},{2,162},{3,163},{4,164},{5,165},{6,166},{7,167},{8... | collective-permute-start | bytes 61448 | tf_op jit(solution)/shard_map/ppermute | solution.py:279
  11.0 0.3 collective-permute-start.3
  11.3 2.8 %collective-permute-start.2 = (bf16[2,8,640]{2,1,0:T(8,128)(2,1)S(1)}, bf16[2,8,640]{2,1,0:T(8,128)(2,1)S(1)}, u32[]{:S(2)}, u32[]{:S(2)}) collective-permute-start(bf16[2,8,640]{2,1,0:T(8,128)(2,1)S(1)} %pad_maximum_fusion.1), channel_id=1, source_target_pairs={{0,224},{1,225},{2,226},{3,227},{4,228},{5,229},{6,230},{7,231},{8... | collective-permute-start | bytes 61448 | tf_op jit(solution)/shard_map/ppermute | solution.py:279
  14.1 1.4 %collective-permute-done.2 = bf16[2,8,640]{2,1,0:T(8,128)(2,1)S(1)} collective-permute-done((bf16[2,8,640]{2,1,0:T(8,128)(2,1)S(1)}, bf16[2,8,640]{2,1,0:T(8,128)(2,1)S(1)}, u32[]{:S(2)}, u32[]{:S(2)}) %collective-permute-start.2) | collective-permute-done | bytes 20512 | tf_op jit(solution)/shard_map/ppermute | solution.py:279
  15.5 0.0 collective-permute-done.3
  15.5 0.0 collective-permute-done.4
  15.6 1.4 %collective-permute-start.5 = (bf16[8,8,640]{2,1,0:T(8,128)(2,1)S(1)}, bf16[8,8,640]{2,1,0:T(8,128)(2,1)S(1)}, u32[]{:S(2)}, u32[]{:S(2)}) collective-permute-start(bf16[8,8,640]{2,1,0:T(8,128)(2,1)S(1)} %get-tuple-element.37), channel_id=1, source_target_pairs={{0,1},{1,2},{2,3},{3,0},{4,12},{5,13},{6,14},{7,15},{8,9},{9,10},{... | collective-permute-start | bytes 245768 | tf_op jit(solution)/shard_map/ppermute | solution.py:279
  16.9 2.6 %collective-permute-start.7 = (bf16[8,8,640]{2,1,0:T(8,128)(2,1)S(1)}, bf16[8,8,640]{2,1,0:T(8,128)(2,1)S(1)}, u32[]{:S(2)}, u32[]{:S(2)}) collective-permute-start(bf16[8,8,640]{2,1,0:T(8,128)(2,1)S(1)} %get-tuple-element.37), channel_id=1, source_target_pairs={{0,2},{1,3},{2,0},{3,1},{4,20},{5,21},{6,22},{7,23},{8,10},{9,11},... | collective-permute-start | bytes 245768 | tf_op jit(solution)/shard_map/ppermute | solution.py:279
  19.6 1.1 %collective-permute-start.6 = (bf16[8,8,640]{2,1,0:T(8,128)(2,1)S(1)}, bf16[8,8,640]{2,1,0:T(8,128)(2,1)S(1)}, u32[]{:S(2)}, u32[]{:S(2)}) collective-permute-start(bf16[8,8,640]{2,1,0:T(8,128)(2,1)S(1)} %get-tuple-element.37), channel_id=1, source_target_pairs={{0,3},{1,0},{2,1},{3,2},{4,28},{5,29},{6,30},{7,31},{8,11},{9,8},{... | collective-permute-start | bytes 245768 | tf_op jit(solution)/shard_map/ppermute | solution.py:279
  20.6 0.0 collective-permute-done.5
  20.6 2.2 %collective-permute-done.6 = bf16[8,8,640]{2,1,0:T(8,128)(2,1)S(1)} collective-permute-done((bf16[8,8,640]{2,1,0:T(8,128)(2,1)S(1)}, bf16[8,8,640]{2,1,0:T(8,128)(2,1)S(1)}, u32[]{:S(2)}, u32[]{:S(2)}) %collective-permute-start.6) | collective-permute-done | bytes 81952 | tf_op jit(solution)/shard_map/ppermute | solution.py:279
  22.9 0.0 collective-permute-done.7
  22.9 4.9 %collective-permute-start.10 = (bf16[32,8,640]{2,1,0:T(8,128)(2,1)S(1)}, bf16[32,8,640]{2,1,0:T(8,128)(2,1)S(1)}, u32[]{:S(2)}, u32[]{:S(2)}) collective-permute-start(bf16[32,8,640]{2,1,0:T(8,128)(2,1)S(1)} %constant_dynamic-update-slice_fusion.5.own), channel_id=1, source_target_pairs={{0,4},{1,5},{2,6},{3,7},{4,0},{5,1},{6,2},{7,3},{8,12},{9,13},{10,... | collective-permute-start | bytes 983048 | tf_op jit(solution)/shard_map/ppermute | solution.py:279
  27.8 0.5 collective-permute-start.9
  28.3 2.2 %collective-permute-start.12 = (bf16[32,8,640]{2,1,0:T(8,128)(2,1)S(1)}, bf16[32,8,640]{2,1,0:T(8,128)(2,1)S(1)}, u32[]{:S(2)}, u32[]{:S(2)}) collective-permute-start(bf16[32,8,640]{2,1,0:T(8,128)(2,1)S(1)} %constant_dynamic-update-slice_fusion.5.own), channel_id=1, source_target_pairs={{0,24},{1,25},{2,26},{3,27},{4,7},{5,4},{6,5},{7,6},{8,0},{9,1},{1... | collective-permute-start | bytes 983048 | tf_op jit(solution)/shard_map/ppermute | solution.py:279
  30.5 0.9 %collective-permute-start.8 = (bf16[32,8,640]{2,1,0:T(8,128)(2,1)S(1)}, bf16[32,8,640]{2,1,0:T(8,128)(2,1)S(1)}, u32[]{:S(2)}, u32[]{:S(2)}) collective-permute-start(bf16[32,8,640]{2,1,0:T(8,128)(2,1)S(1)} %constant_dynamic-update-slice_fusion.5.own), channel_id=1, source_target_pairs={{0,16},{1,17},{2,18},{3,19},{4,6},{5,7},{6,4},{7,5},{8,24},{9,25},... | collective-permute-start | bytes 983048 | tf_op jit(solution)/shard_map/ppermute | solution.py:279
  31.4 0.0 collective-permute-done.10.swapped_own
  31.4 3.7 %shard_map.73 = (bf16[1024,512]{1,0:T(8,128)(2,1)S(1)}, bf16[1024,512]{1,0:T(8,128)(2,1)S(1)}, f32[10,256,256]{2,1,0:T(8,128)S(1)}) custom-call(s32[4]{0:T(128)} %bitcast.22, f32[12]{0:T(128)} %pos_hbm.1, f32[20]{0:T(128)} %time_hbm.1, bf16[1024,512]{1,0:T(8,128)(2,1)} %tokens_hbm.1, s32[8,128]{1,0:T(8,128)} %bitcast.21), custom_call_target="tpu_custom_call" | custom-call | flops 20000000 | bytes 5000000 | tf_op jit(solution)/shard_map/pallas_call | solution.py:104
  35.1 0.1 collective-permute-done.9.near
  35.3 2.8 %collective-permute-done.12.last = bf16[32,8,640]{2,1,0:T(8,128)(2,1)S(1)} collective-permute-done((bf16[32,8,640]{2,1,0:T(8,128)(2,1)S(1)}, bf16[32,8,640]{2,1,0:T(8,128)(2,1)S(1)}, u32[]{:S(2)}, u32[]{:S(2)}) %collective-permute-start.12) | collective-permute-done | bytes 327712 | tf_op jit(solution)/shard_map/ppermute | solution.py:279
  38.0 0.1 pad_maximum_fusion
  38.1 0.1 collective-permute-start.13
  38.2 1.4 %collective-permute-done.8.far = bf16[32,8,640]{2,1,0:T(8,128)(2,1)S(1)} collective-permute-done((bf16[32,8,640]{2,1,0:T(8,128)(2,1)S(1)}, bf16[32,8,640]{2,1,0:T(8,128)(2,1)S(1)}, u32[]{:S(2)}, u32[]{:S(2)}) %collective-permute-start.8) | collective-permute-done | bytes 327712 | tf_op jit(solution)/shard_map/ppermute | solution.py:279
  39.6 1.3 %collective-permute-start.11 = (bf16[32,8,640]{2,1,0:T(8,128)(2,1)S(1)}, bf16[32,8,640]{2,1,0:T(8,128)(2,1)S(1)}, u32[]{:S(2)}, u32[]{:S(2)}) collective-permute-start(bf16[32,8,640]{2,1,0:T(8,128)(2,1)S(1)} %collective-permute-done.8.far), channel_id=1, source_target_pairs={{0,4},{1,5},{2,6},{3,7},{4,0},{5,1},{6,2},{7,3},{8,12},{9,13},{10,... | collective-permute-start | bytes 983048 | tf_op jit(solution)/shard_map/ppermute | solution.py:279
  41.0 0.0 collective-permute-done.13.swapped_near
  41.0 1.3 %shard_map.74 = (bf16[256,8,512]{2,1,0:T(8,128)(2,1)S(1)}, bf16[64,8,512]{2,1,0:T(8,128)(2,1)S(1)}) custom-call(bf16[32,8,640]{2,1,0:T(8,128)(2,1)S(1)} %constant_dynamic-update-slice_fusion.5.own, bf16[32,8,640]{2,1,0:T(8,128)(2,1)S(1)} %collective-permute-done.9.near, bf16[32,8,640]{2,1,0:T(8,128)(2,1)S(1)} %collective-permute-done.8.far, ...), custom_call_target="tpu_custom_call" | custom-call | flops 1000000 | bytes 1000000 | tf_op jit(solution)/shard_map/pallas_call | solution.py:178
  42.3 0.0 collective-permute-done.11.swapped_far
  42.3 7.2 %shard_map.75 = (bf16[1024,512]{1,0:T(8,128)(2,1)}, bf16[256,8,512]{2,1,0:T(8,128)(2,1)S(1)}, bf16[64,8,512]{2,1,0:T(8,128)(2,1)S(1)}) custom-call(bf16[1024,512]{1,0:T(8,128)(2,1)S(1)} %get-tuple-element.28.tokens, bf16[1024,512]{1,0:T(8,128)(2,1)S(1)} %get-tuple-element.29.normed, ...), custom_call_target="tpu_custom_call", output_to_operand_aliasing={{1}: (4, {}), {2}: (5, {})} | custom-call | flops 5000000000 | bytes 9000000 | tf_op jit(solution)/shard_map/pallas_call | solution.py:240
  (10 shorter events, 0.1 us)
Async XLA Ops:
  0.0 5.2 %collective-permute-start = (bf16[8,512]{1,0:T(8,128)(2,1)}, bf16[8,512]{1,0:T(8,128)(2,1)S(1)}, u32[]{:S(2)}, u32[]{:S(2)}) collective-permute-start(bf16[8,512]{1,0:T(8,128)(2,1)} %bitcast.18), channel_id=1, source_target_pairs={{0,32},{1,33},{2,34},{3,35},{4,36},{5,37},{6,38},{7,39},{8,40},{9,... | collective-permute-start | bytes 24584 | tf_op jit(solution)/shard_map/ppermute | solution.py:279
  2.5 2.7 %collective-permute-start.1 = (bf16[8,512]{1,0:T(8,128)(2,1)}, bf16[8,512]{1,0:T(8,128)(2,1)S(1)}, u32[]{:S(2)}, u32[]{:S(2)}) collective-permute-start(bf16[8,512]{1,0:T(8,128)(2,1)} %bitcast.23), channel_id=1, source_target_pairs={{0,32},{1,33},{2,34},{3,35},{4,36},{5,37},{6,38},{7,39},{8,40},{9,... | collective-permute-start | bytes 24584 | tf_op jit(solution)/shard_map/ppermute | solution.py:279
  5.2 10.3 %collective-permute-start.4 = (bf16[2,8,640]{2,1,0:T(8,128)(2,1)S(1)}, bf16[2,8,640]{2,1,0:T(8,128)(2,1)S(1)}, u32[]{:S(2)}, u32[]{:S(2)}) collective-permute-start(bf16[2,8,640]{2,1,0:T(8,128)(2,1)S(1)} %pad_maximum_fusion.1), channel_id=1, source_target_pairs={{0,160},{1,161},{2,162},{3,163},{4,164},{5,165},{6,166},{7,167},{8... | collective-permute-start | bytes 61448 | tf_op jit(solution)/shard_map/ppermute | solution.py:279
  11.0 4.5 %collective-permute-start.3 = (bf16[2,8,640]{2,1,0:T(8,128)(2,1)S(1)}, bf16[2,8,640]{2,1,0:T(8,128)(2,1)S(1)}, u32[]{:S(2)}, u32[]{:S(2)}) collective-permute-start(bf16[2,8,640]{2,1,0:T(8,128)(2,1)S(1)} %pad_maximum_fusion.1), channel_id=1, source_target_pairs={{0,192},{1,193},{2,194},{3,195},{4,196},{5,197},{6,198},{7,199},{8... | collective-permute-start | bytes 61448 | tf_op jit(solution)/shard_map/ppermute | solution.py:279
  11.3 4.2 %collective-permute-start.2 = (bf16[2,8,640]{2,1,0:T(8,128)(2,1)S(1)}, bf16[2,8,640]{2,1,0:T(8,128)(2,1)S(1)}, u32[]{:S(2)}, u32[]{:S(2)}) collective-permute-start(bf16[2,8,640]{2,1,0:T(8,128)(2,1)S(1)} %pad_maximum_fusion.1), channel_id=1, source_target_pairs={{0,224},{1,225},{2,226},{3,227},{4,228},{5,229},{6,230},{7,231},{8... | collective-permute-start | bytes 61448 | tf_op jit(solution)/shard_map/ppermute | solution.py:279
  15.6 5.1 %collective-permute-start.5 = (bf16[8,8,640]{2,1,0:T(8,128)(2,1)S(1)}, bf16[8,8,640]{2,1,0:T(8,128)(2,1)S(1)}, u32[]{:S(2)}, u32[]{:S(2)}) collective-permute-start(bf16[8,8,640]{2,1,0:T(8,128)(2,1)S(1)} %get-tuple-element.37), channel_id=1, source_target_pairs={{0,1},{1,2},{2,3},{3,0},{4,12},{5,13},{6,14},{7,15},{8,9},{9,10},{... | collective-permute-start | bytes 245768 | tf_op jit(solution)/shard_map/ppermute | solution.py:279
  16.9 5.9 %collective-permute-start.7 = (bf16[8,8,640]{2,1,0:T(8,128)(2,1)S(1)}, bf16[8,8,640]{2,1,0:T(8,128)(2,1)S(1)}, u32[]{:S(2)}, u32[]{:S(2)}) collective-permute-start(bf16[8,8,640]{2,1,0:T(8,128)(2,1)S(1)} %get-tuple-element.37), channel_id=1, source_target_pairs={{0,2},{1,3},{2,0},{3,1},{4,20},{5,21},{6,22},{7,23},{8,10},{9,11},... | collective-permute-start | bytes 245768 | tf_op jit(solution)/shard_map/ppermute | solution.py:279
  19.6 3.3 %collective-permute-start.6 = (bf16[8,8,640]{2,1,0:T(8,128)(2,1)S(1)}, bf16[8,8,640]{2,1,0:T(8,128)(2,1)S(1)}, u32[]{:S(2)}, u32[]{:S(2)}) collective-permute-start(bf16[8,8,640]{2,1,0:T(8,128)(2,1)S(1)} %get-tuple-element.37), channel_id=1, source_target_pairs={{0,3},{1,0},{2,1},{3,2},{4,28},{5,29},{6,30},{7,31},{8,11},{9,8},{... | collective-permute-start | bytes 245768 | tf_op jit(solution)/shard_map/ppermute | solution.py:279
  22.9 8.5 %collective-permute-start.10 = (bf16[32,8,640]{2,1,0:T(8,128)(2,1)S(1)}, bf16[32,8,640]{2,1,0:T(8,128)(2,1)S(1)}, u32[]{:S(2)}, u32[]{:S(2)}) collective-permute-start(bf16[32,8,640]{2,1,0:T(8,128)(2,1)S(1)} %constant_dynamic-update-slice_fusion.5.own), channel_id=1, source_target_pairs={{0,4},{1,5},{2,6},{3,7},{4,0},{5,1},{6,2},{7,3},{8,12},{9,13},{10,... | collective-permute-start | bytes 983048 | tf_op jit(solution)/shard_map/ppermute | solution.py:279
  27.8 7.4 %collective-permute-start.9 = (bf16[32,8,640]{2,1,0:T(8,128)(2,1)S(1)}, bf16[32,8,640]{2,1,0:T(8,128)(2,1)S(1)}, u32[]{:S(2)}, u32[]{:S(2)}) collective-permute-start(bf16[32,8,640]{2,1,0:T(8,128)(2,1)S(1)} %constant_dynamic-update-slice_fusion.5.own), channel_id=1, source_target_pairs={{0,8},{1,9},{2,10},{3,11},{4,5},{5,6},{6,7},{7,4},{8,16},{9,17},{1... | collective-permute-start | bytes 983048 | tf_op jit(solution)/shard_map/ppermute | solution.py:279
  28.3 9.7 %collective-permute-start.12 = (bf16[32,8,640]{2,1,0:T(8,128)(2,1)S(1)}, bf16[32,8,640]{2,1,0:T(8,128)(2,1)S(1)}, u32[]{:S(2)}, u32[]{:S(2)}) collective-permute-start(bf16[32,8,640]{2,1,0:T(8,128)(2,1)S(1)} %constant_dynamic-update-slice_fusion.5.own), channel_id=1, source_target_pairs={{0,24},{1,25},{2,26},{3,27},{4,7},{5,4},{6,5},{7,6},{8,0},{9,1},{1... | collective-permute-start | bytes 983048 | tf_op jit(solution)/shard_map/ppermute | solution.py:279
  30.5 9.1 %collective-permute-start.8 = (bf16[32,8,640]{2,1,0:T(8,128)(2,1)S(1)}, bf16[32,8,640]{2,1,0:T(8,128)(2,1)S(1)}, u32[]{:S(2)}, u32[]{:S(2)}) collective-permute-start(bf16[32,8,640]{2,1,0:T(8,128)(2,1)S(1)} %constant_dynamic-update-slice_fusion.5.own), channel_id=1, source_target_pairs={{0,16},{1,17},{2,18},{3,19},{4,6},{5,7},{6,4},{7,5},{8,24},{9,25},... | collective-permute-start | bytes 983048 | tf_op jit(solution)/shard_map/ppermute | solution.py:279
  38.1 2.8 %collective-permute-start.13 = (bf16[64,8,640]{2,1,0:T(8,128)(2,1)S(1)}, bf16[64,8,640]{2,1,0:T(8,128)(2,1)S(1)}, u32[]{:S(2)}, u32[]{:S(2)}) collective-permute-start(bf16[64,8,640]{2,1,0:T(8,128)(2,1)S(1)} %pad_maximum_fusion), channel_id=1, source_target_pairs={{0,4},{1,5},{2,6},{3,7},{4,0},{5,1},{6,2},{7,3},{8,12},{9,13},{10,... | collective-permute-start | bytes 1966088 | tf_op jit(solution)/shard_map/ppermute | solution.py:279
  39.6 2.7 %collective-permute-start.11 = (bf16[32,8,640]{2,1,0:T(8,128)(2,1)S(1)}, bf16[32,8,640]{2,1,0:T(8,128)(2,1)S(1)}, u32[]{:S(2)}, u32[]{:S(2)}) collective-permute-start(bf16[32,8,640]{2,1,0:T(8,128)(2,1)S(1)} %collective-permute-done.8.far), channel_id=1, source_target_pairs={{0,4},{1,5},{2,6},{3,7},{4,0},{5,1},{6,2},{7,3},{8,12},{9,13},{10,... | collective-permute-start | bytes 983048 | tf_op jit(solution)/shard_map/ppermute | solution.py:279
